TPU v7x, 32 devices: a whole 2x2x4 slice. The times are simulated.
32 devices in a mesh: dp: 4 (over x, core), expert: 8 (over z, y).
Axes of the slice: x: 2, y: 2, z: 4, core: 2. Of those that a mesh axis runs over, the one named last changes fastest.
Arguments:
- tokens: bfloat16 [4096, 768], P(('dp', 'expert')), may hold values from -6 to 6
- attn_weights: bfloat16 [3072, 768], P(('dp', 'expert')), may hold values from -0.3125 to 0.3125
- gain_attn: float32 [768], replicated, may hold values from 0.5 to 1.5
- gain_ffn: float32 [768], replicated, may hold values from 0.5 to 1.5
- rel_table: float32 [32, 12], replicated, may hold values from -4 to 4
- expert_in: bfloat16 [8, 768, 3072], P('expert', None, 'dp'), may hold values from -0.21875 to 0.21875
- expert_out: bfloat16 [8, 3072, 768], P('expert', 'dp'), may hold values from -0.21875 to 0.21875
- gate_weights: float32 [4096, 2], P(('dp', 'expert')), may hold values from 0.25 to 0.75
- expert_ids: int32 [4096, 2], P(('dp', 'expert')), may hold values from 0 to 7, all different within a row; in each aligned block of 64 rows (0 to 63, 64 to 127, ...) at most 24 rows name the same one
- doc_ids: int32 [64, 64], P(('dp', 'expert')), may hold values from 0 to 3, never falling along the last dimension, each value on 1 to 32 neighbouring positions
- cotangent: bfloat16 [4096, 768], P(('dp', 'expert')), may hold values from -6 to 6
Outputs:
- output: bfloat16 [4096, 768], P(('dp', 'expert'))
- grad_tokens: float32 [4096, 768], P(('dp', 'expert'))
- grad_attn_weights: float32 [3072, 768], P(('dp', 'expert'))
- grad_gain_attn: float32 [768], replicated
- grad_gain_ffn: float32 [768], replicated
- grad_rel_table: float32 [32, 12], replicated
- grad_expert_in: float32 [8, 768, 3072], P('expert', None, 'dp')
- grad_expert_out: float32 [8, 3072, 768], P('expert', 'dp')
Inputs may be any that keep to these rules, and one draw needn't show every extreme that they name: `expert_ids`: the two experts of a token differ. Within each aligned block of 64 tokens (one micro-batch of one device) no expert is named more than 24 times; in some blocks some expert exactly 24 times. `doc_ids`: within each sequence the numbers never fall; each of the four documents holds 1 to half of 64 tokens, and one exactly half.
All inputs are finite; a program needn't handle non-finite values.
Results may differ from a plain program's by a relative error of at most 0.012.
The roundings to bfloat16 on the way count: a program that leaves them out, or rounds other values in their place, can miss the bound.
Values may be sent and summed in bfloat16 or wider, within the bound.
No kernel may reach another device: no remote copies, remote signals or barrier semaphores. Data moves between devices by JAX's collectives and lax.ppermute only.
A program may use at most 128 MiB of HBM per device.

v0:
```python
import jax
import jax.numpy as jnp
import numpy as np
from jax import lax
from jax.experimental import pallas as pl
from jax.experimental.pallas import tpu as pltpu
from jax.sharding import PartitionSpec as P

epsilon = 1e-06
top_precision = lax.Precision.HIGHEST
f32 = jnp.float32
bf16 = jnp.bfloat16


def bucket_table(length, top_bucket):
    offset = np.arange(length)[:, None] - np.arange(length)[None, :]
    offset = np.maximum(offset, 0)
    octave = offset * 0
    for exponent in range(1, 24):
        octave = octave + (offset >= 2**exponent)
    shifted = offset >> np.maximum(octave - 2, 0)
    logbucket = 16 + 4 * (octave - 4) + (shifted & 3)
    return np.where(offset < 16, offset, np.minimum(logbucket, top_bucket))


def swap(value, axis, bits):
    size = lax.axis_size(axis)
    return lax.ppermute(value, axis, [(i, i ^ bits) for i in range(size)])


def swap_core(value):
    return swap(value, "dp", 1)


def swap_x(value):
    return swap(value, "dp", 2)


def gather_projections(block):
    experts = lax.axis_size("expert")
    if experts != 8:
        full = lax.all_gather(block, ("dp", "expert"), axis=0, tiled=True)
        return [full[None]], [None]
    near_y = swap(block, "expert", 1)
    far = jnp.stack([swap(block, "expert", bits) for bits in (2, 4, 6)])
    near = jnp.stack([block, near_y])
    near_x = swap_x(near)
    far, near_x = lax.optimization_barrier((far, near_x))
    far_y = swap(far, "expert", 1)
    far_x = swap_x(far)
    far_yx = swap_x(far_y)
    arrays = [near, near_x, far, far_y, far_x, far_yx]
    offsets = [
        [(0, 0), (0, 1)],
        [(2, 0), (2, 1)],
        [(0, 2), (0, 4), (0, 6)],
        [(0, 3), (0, 5), (0, 7)],
        [(2, 2), (2, 4), (2, 6)],
        [(2, 3), (2, 5), (2, 7)],
    ]
    arrays = arrays + [swap_core(a) for a in arrays]
    offsets = offsets + [[(d + 1, e) for d, e in group] for group in offsets]
    return arrays, offsets


def place_projections(pieces, offsets, dense, sems):
    copies = []
    d_here, e_here = lax.axis_index("dp"), lax.axis_index("expert")
    experts = lax.axis_size("expert")
    for piece, group in zip(pieces, offsets):
        rows = piece.shape[1]
        for i in range(piece.shape[0]):
            target = dense
            if group is not None:
                block = (d_here ^ group[i][0]) * experts + (e_here ^ group[i][1])
                target = dense.at[pl.ds(pl.multiple_of(block * rows, rows), rows)]
            copies.append(pltpu.make_async_copy(piece.at[i], target, sems.at[len(copies)]))
    for copy in copies:
        copy.start()
    return copies


VMEM = pl.BlockSpec(memory_space=pltpu.VMEM)
ANY = pl.BlockSpec(memory_space=pl.ANY)
LIMIT = pltpu.CompilerParams(vmem_limit_bytes=58 * 1024 * 1024)


def dot(a, b):
    return jnp.dot(a, b, preferred_element_type=f32)


def dot_t(a, b):
    return lax.dot_general(a, b, (((1,), (1,)), ((), ())), preferred_element_type=f32)


def t_dot(a, b):
    return lax.dot_general(a, b, (((0,), (0,)), ((), ())), preferred_element_type=f32)


def inverse_rms(values):
    return lax.rsqrt(jnp.mean(values * values, axis=-1, keepdims=True) + epsilon)


def attention_forward(pieces, offsets, tokens, gains, bias_rows, docs_col, docs_row, select, heads):
    count, width = tokens.shape
    slots = select.shape[0]
    blocks = sum(p.shape[0] for p in pieces)
    n = len(pieces)

    def kernel(*refs):
        piece_refs, refs = refs[:n], refs[n:]
        tok, gain, bias, dcol, drow, sel = refs[:6]
        normed_o, qkv_o, mixed_o, probs_o, residual_o, buffer_o, dense, sems = refs[6:]
        copies = place_projections(piece_refs, offsets, dense, sems)
        x = tok[...].astype(f32)
        normed = (x * inverse_rms(x) * gain[0:1, :]).astype(bf16)
        normed_o[...] = normed
        row = lax.broadcasted_iota(jnp.int32, (count, count), 0)
        col = lax.broadcasted_iota(jnp.int32, (count, count), 1)
        allowed = (dcol[...] == drow[...]) & (col <= row)
        low_lanes = lax.broadcasted_iota(jnp.int32, (count, 128), 1) < 64
        for copy in copies:
            copy.wait()
        for i in range(3):
            qkv_o[i] = dot(normed, dense[i * width : (i + 1) * width, :]).astype(bf16)
        for pair in range(heads // 2):
            lanes = slice(128 * pair, 128 * pair + 128)
            q, k, v = qkv_o[0, :, lanes], qkv_o[1, :, lanes], qkv_o[2, :, lanes]
            out = []
            for half in range(2):
                mask = low_lanes if half == 0 else ~low_lanes
                head = 2 * pair + half
                shift = jnp.broadcast_to(bias[head : head + 1, :], (count, 128))
                shift = pltpu.roll(shift, 0, 1, stride=1, stride_axis=0)
                scores = dot_t(jnp.where(mask, q, jnp.zeros_like(q)), k) * 0.125 + shift
                scores = jnp.where(allowed, scores, -1000000000.0)
                scores = jnp.exp(scores - jnp.max(scores, axis=-1, keepdims=True))
                probs = scores / jnp.sum(scores, axis=-1, keepdims=True)
                probs_o[head] = probs
                out.append(dot(probs.astype(bf16), v))
            mixed_o[:, lanes] = jnp.where(low_lanes, out[0], out[1]).astype(bf16)
        residual = x + dot(mixed_o[...], dense[3 * width : 4 * width, :])
        residual_o[...] = residual
        moe_in = (residual * inverse_rms(residual) * gain[1:2, :]).astype(bf16)
        buffer_o[...] = dot(sel[...], moe_in).astype(bf16)

    return pl.pallas_call(
        kernel,
        out_shape=(
            jax.ShapeDtypeStruct((count, width), bf16),
            jax.ShapeDtypeStruct((3, count, width), bf16),
            jax.ShapeDtypeStruct((count, width), bf16),
            jax.ShapeDtypeStruct((heads, count, count), f32),
            jax.ShapeDtypeStruct((count, width), f32),
            jax.ShapeDtypeStruct((slots, width), bf16),
        ),
        in_specs=[ANY] * n + [VMEM] * 6,
        out_specs=(VMEM,) * 6,
        scratch_shapes=[
            pltpu.VMEM((4 * width, width), bf16),
            pltpu.SemaphoreType.DMA((blocks,)),
        ],
        compiler_params=LIMIT,
        name="attention_forward",
    )(*pieces, tokens, gains, bias_rows, docs_col, docs_row, select)


def attention_backward(
    pieces, offsets, tokens, gains, cotangent, residual, d_returned, select_t, qkv, probs, heads
):
    count, width = tokens.shape
    blocks = sum(p.shape[0] for p in pieces)
    n = len(pieces)

    def kernel(*refs):
        piece_refs, refs = refs[:n], refs[n:]
        tok, gain, cot, res, d_ret, sel_t, qkv_r, probs_r = refs[:8]
        grads_o, d_tok_o, diag_o, d_gain_o, dense, d_mixed_s, sems = refs[8:]
        copies = place_projections(piece_refs, offsets, dense, sems)
        d_moe = dot(sel_t[...], d_ret[...])
        residual = res[...]
        r = inverse_rms(residual)
        d_gain_o[1:2, :] = jnp.sum(d_moe * residual * r, axis=0, keepdims=True)
        m = d_moe * gain[1:2, :]
        mean = jnp.mean(m * residual, axis=-1, keepdims=True)
        d_residual = cot[...].astype(f32) + r * m - r * r * r * residual * mean
        d_tok_o[...] = d_residual
        d_attn = d_residual.astype(bf16)
        grads_o[3] = d_attn
        for copy in copies:
            copy.wait()
        d_mixed_s[...] = dot_t(d_attn, dense[3 * width : 4 * width, :]).astype(bf16)
        low_lanes = lax.broadcasted_iota(jnp.int32, (count, 128), 1) < 64
        row = lax.broadcasted_iota(jnp.int32, (count, count), 0)
        for pair in range(heads // 2):
            lanes = slice(128 * pair, 128 * pair + 128)
            q, k, v = qkv_r[0, :, lanes], qkv_r[1, :, lanes], qkv_r[2, :, lanes]
            d_mix = d_mixed_s[:, lanes]
            d_q, d_k, d_v = [], [], []
            for half in range(2):
                mask = low_lanes if half == 0 else ~low_lanes
                head = 2 * pair + half
                probs = probs_r[head]
                d_probs = dot_t(jnp.where(mask, d_mix, jnp.zeros_like(d_mix)), v)
                d_v.append(t_dot(probs.astype(bf16), d_mix))
                inner = jnp.sum(probs * d_probs, axis=-1, keepdims=True)
                d_scores = (probs * (d_probs - inner)).astype(bf16)
                d_q.append(dot(d_scores, k))
                d_k.append(t_dot(d_scores, q))
                turned = d_scores.astype(f32)
                for bit in (1, 2, 4, 8, 16, 32, 64):
                    turned = jnp.where(
                        (row & bit) != 0, pltpu.roll(turned, count - bit, 1), turned
                    )
                diag_o[head : head + 1, :] = jnp.sum(turned, axis=0, keepdims=True)
            grads_o[0, :, lanes] = (jnp.where(low_lanes, d_q[0], d_q[1]) * 0.125).astype(bf16)
            grads_o[1, :, lanes] = (jnp.where(low_lanes, d_k[0], d_k[1]) * 0.125).astype(bf16)
            grads_o[2, :, lanes] = jnp.where(low_lanes, d_v[0], d_v[1]).astype(bf16)
        d_normed = dot_t(grads_o[0], dense[0:width, :])
        d_normed = d_normed + dot_t(grads_o[1], dense[width : 2 * width, :])
        d_normed = d_normed + dot_t(grads_o[2], dense[2 * width : 3 * width, :])
        x = tok[...].astype(f32)
        s = inverse_rms(x)
        d_gain_o[0:1, :] = jnp.sum(d_normed * x * s, axis=0, keepdims=True)
        m = d_normed * gain[0:1, :]
        mean = jnp.mean(m * x, axis=-1, keepdims=True)
        d_tok_o[...] += s * m - s * s * s * x * mean

    return pl.pallas_call(
        kernel,
        out_shape=(
            jax.ShapeDtypeStruct((4, count, width), bf16),
            jax.ShapeDtypeStruct((count, width), f32),
            jax.ShapeDtypeStruct((heads, count), f32),
            jax.ShapeDtypeStruct((2, width), f32),
        ),
        in_specs=[ANY] * n + [VMEM] * 8,
        out_specs=(VMEM,) * 4,
        scratch_shapes=[
            pltpu.VMEM((4 * width, width), bf16),
            pltpu.VMEM((count, width), bf16),
            pltpu.SemaphoreType.DMA((blocks,)),
        ],
        compiler_params=LIMIT,
        name="attention_backward",
    )(*pieces, tokens, gains, cotangent, residual, d_returned, select_t, qkv, probs)


def gelu_parts(v):
    c = 0.7978845608028654
    square = v * v
    t = jnp.tanh(c * v * (1.0 + 0.044715 * square))
    half = 0.5 * (1.0 + t)
    slope = half + 0.5 * v * (1.0 - t * t) * (c + (3.0 * 0.044715 * c) * square)
    return v * half, slope


def experts_first(rows, d_rows, win, wout):
    count, width = rows[0].shape
    units = win.shape[1]

    def kernel(*refs):
        row_refs, d_refs, (win_r, wout_r) = refs[0:4], refs[4:8], refs[8:10]
        hidden_o, d_pre_o, keep_o, send_o, row_s, d_s, win_s, wout_s, sems = refs[10:]
        copies = [
            pltpu.make_async_copy(win_r, win_s, sems.at[8]),
            pltpu.make_async_copy(wout_r, wout_s, sems.at[9]),
        ]
        order = (1, 3, 0, 2)
        for i in order:
            copies.append(pltpu.make_async_copy(row_refs[i], row_s.at[i], sems.at[i]))
            copies.append(pltpu.make_async_copy(d_refs[i], d_s.at[i], sems.at[4 + i]))
        for copy in copies:
            copy.start()
        copies[0].wait()
        copies[1].wait()
        for n, i in enumerate(order):
            copies[2 + 2 * n].wait()
            copies[3 + 2 * n].wait()
            pre = dot(row_s[i], win_s[...])
            d_hidden = dot_t(d_s[i], wout_s[...])
            hidden, slope = gelu_parts(pre)
            hidden_o[i] = hidden.astype(bf16)
            d_pre = (d_hidden * slope).astype(bf16)
            d_pre_o[i] = d_pre
            d_slot = dot_t(d_pre, win_s[...])
            if i % 2 == 1:
                send_o[i // 2] = d_slot.astype(bf16)
            else:
                keep_o[i // 2] = d_slot

    return pl.pallas_call(
        kernel,
        out_shape=(
            jax.ShapeDtypeStruct((4, count, units), bf16),
            jax.ShapeDtypeStruct((4, count, units), bf16),
            jax.ShapeDtypeStruct((2, count, width), f32),
            jax.ShapeDtypeStruct((2, count, width), bf16),
        ),
        in_specs=[ANY] * 10,
        out_specs=(VMEM,) * 4,
        scratch_shapes=[
            pltpu.VMEM((4, count, width), bf16),
            pltpu.VMEM((4, count, width), bf16),
            pltpu.VMEM(win.shape, bf16),
            pltpu.VMEM(wout.shape, bf16),
            pltpu.SemaphoreType.DMA((10,)),
        ],
        compiler_params=LIMIT,
        name="experts_first",
    )(*rows, *d_rows, win, wout)


def experts_second(rows, d_rows, hidden, d_pre, wout):
    count, width = rows[0].shape
    units = wout.shape[0]

    def kernel(*refs):
        row_refs, d_refs, (hidden_r, d_pre_r, wout_r) = refs[0:4], refs[4:8], refs[8:11]
        keep_o, send_o, in_o, out_o = refs[11:]
        for i in (1, 3, 0, 2):
            result = dot(hidden_r[i], wout_r[...])
            if i % 2 == 1:
                send_o[i // 2] = result.astype(bf16)
            else:
                keep_o[i // 2] = result
        for i in range(4):
            g_in = t_dot(row_refs[i][...], d_pre_r[i])
            g_out = t_dot(hidden_r[i], d_refs[i][...])
            if i == 0:
                in_o[...] = g_in
                out_o[...] = g_out
            else:
                in_o[...] += g_in
                out_o[...] += g_out

    return pl.pallas_call(
        kernel,
        out_shape=(
            jax.ShapeDtypeStruct((2, count, width), f32),
            jax.ShapeDtypeStruct((2, count, width), bf16),
            jax.ShapeDtypeStruct((width, units), f32),
            jax.ShapeDtypeStruct((units, width), f32),
        ),
        in_specs=[VMEM] * 11,
        out_specs=(VMEM,) * 4,
        compiler_params=LIMIT,
        name="experts_second",
    )(*rows, *d_rows, hidden, d_pre, wout)


def exchange_plain(chunks):
    return lax.all_to_all(chunks, "expert", split_axis=0, concat_axis=0, tiled=True)


def exchange_apart(chunks):
    experts = lax.axis_size("expert")
    if experts != 8:
        return exchange_plain(chunks)
    me = lax.axis_index("expert")
    out = jnp.zeros_like(chunks)
    own = lax.dynamic_index_in_dim(chunks, me, 0, keepdims=True)
    out = lax.dynamic_update_slice_in_dim(out, own, me, 0)
    for bits in (6, 4, 7, 5, 2, 3, 1):
        part = lax.dynamic_index_in_dim(chunks, me ^ bits, 0, keepdims=True)
        out = lax.dynamic_update_slice_in_dim(out, swap(part, "expert", bits), me ^ bits, 0)
    return out


def spread(rows):
    x_rows = swap_x(rows)
    return [rows, swap_core(rows), x_rows, swap_core(x_rows)]


def collect(keep, send):
    from_core = swap_core(send)
    chip_x = (keep[1] + from_core[1].astype(f32)).astype(bf16)
    from_x = swap_x(chip_x)
    return (keep[0] + from_core[0].astype(f32) + from_x.astype(f32)).astype(bf16)


def reduce_experts(grad):
    experts = lax.axis_size("expert")
    rows = grad.shape[0] // experts
    if experts != 8:
        return lax.psum_scatter(grad, "expert", scatter_dimension=0, tiled=True)
    me = lax.axis_index("expert")
    parts = grad.reshape(4, 2, rows, grad.shape[1])
    y_mine = me & 1
    keep = lax.dynamic_index_in_dim(parts, y_mine, 1, keepdims=False)
    send = lax.dynamic_index_in_dim(parts, 1 - y_mine, 1, keepdims=False).astype(bf16)
    pair = keep + swap(send, "expert", 1).astype(f32)
    z_mine = me >> 1
    total = lax.dynamic_index_in_dim(pair, z_mine, 0, keepdims=False)
    for bits in (1, 2, 3):
        part = lax.dynamic_index_in_dim(pair, z_mine ^ bits, 0, keepdims=False).astype(bf16)
        total = total + swap(part, "expert", 2 * bits).astype(f32)
    return total


def sum_all(value):
    for axis in ("dp", "expert"):
        bits = 1
        while bits < lax.axis_size(axis):
            value = value + swap(value, axis, bits)
            bits *= 2
    return value


def shards(
    tokens,
    attn_weights,
    gain_attn,
    gain_ffn,
    rel_table,
    expert_in,
    expert_out,
    gate_weights,
    expert_ids,
    doc_ids,
    cotangent,
):
    seqs, seq_len = doc_ids.shape
    width = tokens.shape[1]
    head_count = rel_table.shape[1]
    head_size = width // head_count
    bucket_count = rel_table.shape[0]
    experts = lax.axis_size("expert")
    token_count = tokens.shape[0]
    block_cap = 3 * seq_len // experts
    capacity = block_cap * seqs
    slots = experts * capacity
    pieces, offsets = gather_projections(attn_weights)
    win, wout = expert_in[0], expert_out[0]

    flat_ids = expert_ids.reshape(-1)
    pairs = flat_ids.shape[0]
    earlier = np.tril(np.ones((pairs, pairs), dtype=np.bool_), -1)
    rank = jnp.sum(
        ((flat_ids[:, None] == flat_ids[None, :]) & earlier).astype(jnp.int32), axis=1
    )
    positions = (flat_ids * capacity + rank).reshape(token_count, 2)
    slot_iota = jnp.arange(slots, dtype=jnp.int32)
    first_hit = slot_iota[:, None] == positions[None, :, 0]
    second_hit = slot_iota[:, None] == positions[None, :, 1]
    select = (first_hit | second_hit).astype(bf16)
    first_t = (slot_iota[None, :] == positions[:, 0:1]).astype(bf16)
    second_t = (slot_iota[None, :] == positions[:, 1:2]).astype(bf16)
    select_t = first_t + second_t
    gate_slot = jnp.sum(
        jnp.where(first_hit, gate_weights[None, :, 0], 0.0)
        + jnp.where(second_hit, gate_weights[None, :, 1], 0.0),
        axis=1,
    )

    def to_experts(buffer):
        got = exchange_plain(buffer.reshape(experts, capacity, width))
        return spread(got.reshape(slots, width))

    def to_tokens(rows, move):
        return move(rows.reshape(experts, capacity, width)).reshape(slots, width)

    d_buffer = gate_slot[:, None] * jnp.dot(select, cotangent, preferred_element_type=f32)
    d_buffer = d_buffer.astype(bf16)
    d_buffer, pieces = lax.optimization_barrier((d_buffer, pieces))
    d_all = to_experts(d_buffer)

    distance = (token_count - np.arange(token_count)) % token_count
    lookup = np.eye(bucket_count, dtype=np.float32)[
        bucket_table(seq_len, bucket_count - 1)[np.minimum(distance, seq_len - 1), 0]
    ]
    lookup = jnp.asarray(lookup * (distance < seq_len)[:, None])
    bias_rows = lax.dot_general(
        rel_table,
        lookup,
        (((0,), (1,)), ((), ())),
        precision=top_precision,
        preferred_element_type=f32,
    )
    gains = jnp.stack([gain_attn, gain_ffn])
    docs = doc_ids + 4 * jnp.arange(seqs, dtype=jnp.int32)[:, None]
    docs_col, docs_row = docs.reshape(-1, 1), docs.reshape(1, -1)
    normed, qkv, mixed, probs, residual, buffer = attention_forward(
        pieces, offsets, tokens, gains, bias_rows, docs_col, docs_row, select, head_count
    )

    rows = to_experts(buffer)
    hidden, d_pre, keep, send = experts_first(rows, d_all, win, wout)
    d_returned = to_tokens(collect(keep, send), exchange_plain)
    keep, send, grad_in, grad_out = experts_second(rows, d_all, hidden, d_pre, wout)
    result = collect(keep, send)
    result, d_returned = lax.optimization_barrier((result, d_returned))
    returned = to_tokens(result, exchange_apart)
    moe_out = gate_weights[:, 0:1] * jnp.dot(first_t, returned, preferred_element_type=f32)
    moe_out = moe_out + gate_weights[:, 1:2] * jnp.dot(
        second_t, returned, preferred_element_type=f32
    )
    output = (residual + moe_out).astype(bf16)

    grads, grad_tokens, diagonals, d_gains = attention_backward(
        pieces,
        offsets,
        tokens,
        gains,
        cotangent,
        residual,
        d_returned,
        select_t,
        qkv,
        probs,
        head_count,
    )

    mine = lax.axis_index("dp")
    left = jnp.stack([normed, mixed])
    left_x = swap_x(left)
    left = jnp.stack([left, left_x], axis=1)
    left_core = swap_core(left)
    left = jnp.where(mine == 3, jnp.stack([left[1], left_core[1]]), jnp.stack([left[0], left_core[0]]))
    to_x = jnp.where(mine >= 2, grads[0:2], grads[2:4])
    here = jnp.where(mine >= 2, grads[2:4], grads[0:2])
    from_x = swap_x(to_x)
    odd = (mine & 1) == 1
    keep = jnp.stack([jnp.where(odd, here[1], here[0]), jnp.where(odd, from_x[1], from_x[0])])
    give = jnp.stack([jnp.where(odd, here[0], here[1]), jnp.where(odd, from_x[0], from_x[1])])
    got = swap_core(give)
    right = jnp.stack([keep, got]).reshape(-1, width)
    left = left.reshape(-1, width)
    grad_own = jnp.einsum("td,te->de", left, right, preferred_element_type=f32)
    grad_attn = reduce_experts(grad_own)

    small = jnp.concatenate([diagonals.reshape(-1), d_gains.reshape(-1)])
    small = sum_all(small)
    diagonals = small[0 : head_count * token_count].reshape(head_count, token_count)
    d_gains = small[head_count * token_count :].reshape(2, width)
    d_table = lax.dot_general(
        lookup,
        diagonals,
        (((0,), (1,)), ((), ())),
        precision=top_precision,
        preferred_element_type=f32,
    )
    return (
        output,
        grad_tokens,
        grad_attn,
        d_gains[0],
        d_gains[1],
        d_table,
        grad_in[None],
        grad_out[None],
    )


def solution(mesh):
    placed = (
        P(("dp", "expert"), None),
        P(("dp", "expert"), None),
        P(),
        P(),
        P(),
        P("expert", None, "dp"),
        P("expert", "dp", None),
        P(("dp", "expert"), None),
        P(("dp", "expert"), None),
        P(("dp", "expert"), None),
        P(("dp", "expert"), None),
    )
    return jax.shard_map(
        shards,
        mesh=mesh,
        in_specs=placed,
        out_specs=(
            P(("dp", "expert"), None),
            P(("dp", "expert"), None),
            P(("dp", "expert"), None),
            P(),
            P(),
            P(),
            P("expert", None, "dp"),
            P("expert", "dp", None),
        ),
        check_vma=False,
    )
```

profile of v0, /device:TPU:0, one launch (start us, length us, event | category | flops | bytes accessed | tf_op | source)
XLA Modules:
  0.0 258.6 jit_solution(14052795580292946964)
XLA Ops:
  0.7 3.0 %collective-permute-start = (bf16[96,768]{1,0:T(8,128)(2,1)}, bf16[96,768]{1,0:T(8,128)(2,1)S(1)}, u32[]{:S(2)}, u32[]{:S(2)}) collective-permute-start(bf16[96,768]{1,0:T(8,128)(2,1)} %param.14), channel_id=1, source_target_pairs={{0,1},{1,0},{2,3},{3,2},{4,5},{5,4},{6,7},{7,6},{8,9},{9,8},{10,11... | collective-permute-start | bytes 442376 | tf_op jit(solution)/shard_map/ppermute | solution.py:28
  5.3 2.6 %collective-permute-start.2 = (bf16[96,768]{1,0:T(8,128)(2,1)}, bf16[96,768]{1,0:T(8,128)(2,1)S(1)}, u32[]{:S(2)}, u32[]{:S(2)}) collective-permute-start(bf16[96,768]{1,0:T(8,128)(2,1)} %param.14), channel_id=1, source_target_pairs={{0,4},{1,5},{2,6},{3,7},{4,0},{5,1},{6,2},{7,3},{8,12},{9,13},{10,... | collective-permute-start | bytes 442376 | tf_op jit(solution)/shard_map/ppermute | solution.py:28
  16.5 2.9 %collective-permute-done.2 = bf16[96,768]{1,0:T(8,128)(2,1)S(1)} collective-permute-done((bf16[96,768]{1,0:T(8,128)(2,1)}, bf16[96,768]{1,0:T(8,128)(2,1)S(1)}, u32[]{:S(2)}, u32[]{:S(2)}) %collective-permute-start.2) | collective-permute-done | bytes 147488 | tf_op jit(solution)/shard_map/ppermute | solution.py:28
  23.3 7.3 %collective-permute-done.5.refs_3_ = bf16[3,96,768]{2,1,0:T(8,128)(2,1)S(1)} collective-permute-done((bf16[3,96,768]{2,1,0:T(8,128)(2,1)S(1)}, bf16[3,96,768]{2,1,0:T(8,128)(2,1)S(1)}, u32[]{:S(2)}, u32[]{:S(2)}) %collective-permute-start.5) | collective-permute-done | bytes 442400 | tf_op jit(solution)/shard_map/ppermute | solution.py:28
  33.8 7.3 %collective-permute-done.7.refs_5_ = bf16[3,96,768]{2,1,0:T(8,128)(2,1)S(1)} collective-permute-done((bf16[3,96,768]{2,1,0:T(8,128)(2,1)S(1)}, bf16[3,96,768]{2,1,0:T(8,128)(2,1)S(1)}, u32[]{:S(2)}, u32[]{:S(2)}) %collective-permute-start.7) | collective-permute-done | bytes 442400 | tf_op jit(solution)/shard_map/ppermute | solution.py:28
  45.8 2.1 fusion
  48.8 9.5 %attention_forward.1 = (bf16[128,768]{1,0:T(8,128)(2,1)}, bf16[3,128,768]{2,1,0:T(8,128)(2,1)}, bf16[128,768]{1,0:T(8,128)(2,1)}, f32[12,128,128]{2,1,0:T(8,128)...) custom-call(bf16[2,96,768]{2,1,0:T(8,128)(2,1)} %copy-done.4, bf16[2,96,768]{2,1,0:T(8,128)(2,1)} %copy-done.21, ...), custom_call_target="tpu_custom_call" | custom-call | tf_op jit(solution)/shard_map/attention_forward/pallas_call | solution.py:147
  58.3 22.3 %all_to_all.15 = bf16[8,48,768]{2,1,0:T(8,128)(2,1)S(1)} all-to-all(bf16[8,48,768]{2,1,0:T(8,128)(2,1)} %bitcast.103), channel_id=1, replica_groups=mesh['dp'=4,'expert'=8] {'expert'}, dimensions={0} | all-to-all | bytes 1179648 | tf_op jit(solution)/shard_map/all_to_all | solution.py:353
  80.5 3.7 %all-to-all-start.1 = ((bf16[8,48,768]{2,1,0:T(8,128)(2,1)}), bf16[8,48,768]{2,1,0:T(8,128)(2,1)S(1)}, u32[]{:S(2)}, u32[]{:S(2)}) async-start(bf16[8,48,768]{2,1,0:T(8,128)(2,1)} %bitcast.12), calls=%async_computation.1 | async-start | bytes 1179648 | tf_op jit(solution)/shard_map/all_to_all | solution.py:353
  85.8 13.5 %all-to-all-done.1 = bf16[8,48,768]{2,1,0:T(8,128)(2,1)S(1)} async-done(((bf16[8,48,768]{2,1,0:T(8,128)(2,1)}), bf16[8,48,768]{2,1,0:T(8,128)(2,1)S(1)}, u32[]{:S(2)}, u32[]{:S(2)}) %all-to-all-start.1) | async-done | bytes 589856 | tf_op jit(solution)/shard_map/all_to_all | solution.py:353
  101.5 11.2 %collective-permute-done.18.refs_6_ = bf16[384,768]{1,0:T(8,128)(2,1)S(1)} collective-permute-done((bf16[384,768]{1,0:T(8,128)(2,1)S(1)}, bf16[384,768]{1,0:T(8,128)(2,1)S(1)}, u32[]{:S(2)}, u32[]{:S(2)}) %collective-permute-start.18) | collective-permute-done | bytes 589856 | tf_op jit(solution)/shard_map/ppermute | solution.py:28
  115.4 11.6 %experts_first.1 = (bf16[4,384,768]{2,1,0:T(8,128)(2,1)}, bf16[4,384,768]{2,1,0:T(8,128)(2,1)}, f32[2,384,768]{2,1,0:T(8,128)}, bf16[2,384,768]{2,1,0:T(8,128)(2,1)}) custom-call(bf16[384,768]{1,0:T(8,128)(2,1)} %bitcast.88, bf16[384,768]{1,0:T(8,128)(2,1)} %copy-done.9, bf16[384,768]{1,0:T(8,128)(2,1)} %copy-done.7, bf16[384,768]{1,0:T(8,128)(2,1)} %copy-done.11, ...), custom_call_target="tpu_custom_call" | custom-call | tf_op jit(solution)/shard_map/experts_first/pallas_call | solution.py:292
  127.2 12.9 %experts_second.1 = (f32[2,384,768]{2,1,0:T(8,128)}, bf16[2,384,768]{2,1,0:T(8,128)(2,1)}, f32[768,768]{1,0:T(8,128)}, f32[768,768]{1,0:T(8,128)}) custom-call(bf16[384,768]{1,0:T(8,128)(2,1)} %bitcast.89, bf16[384,768]{1,0:T(8,128)(2,1)} %copy-done.9, bf16[384,768]{1,0:T(8,128)(2,1)} %copy-done.7, bf16[384,768]{1,0:T(8,128)(2,1)} %copy-done.11, ...), custom_call_target="tpu_custom_call" | custom-call | tf_op jit(solution)/shard_map/experts_second/pallas_call | solution.py:337
  143.9 13.8 %collective-permute-done.23 = bf16[384,768]{1,0:T(8,128)(2,1)S(1)} collective-permute-done((bf16[384,768]{1,0:T(8,128)(2,1)S(1)}, bf16[384,768]{1,0:T(8,128)(2,1)S(1)}, u32[]{:S(2)}, u32[]{:S(2)}) %collective-permute-start.23) | collective-permute-done | bytes 589856 | tf_op jit(solution)/shard_map/ppermute | solution.py:28
  158.8 5.3 %all-to-all-start.2 = ((bf16[8,48,768]{2,1,0:T(8,128)(2,1)}), bf16[8,48,768]{2,1,0:T(8,128)(2,1)}, u32[]{:S(2)}, u32[]{:S(2)}) async-start(bf16[8,48,768]{2,1,0:T(8,128)(2,1)} %bitcast.20), calls=%async_computation.2 | async-start | bytes 1179648 | tf_op jit(solution)/shard_map/all_to_all | solution.py:353
  164.1 2.0 fusion.6
  170.2 9.6 %collective-permute-done.21 = bf16[384,768]{1,0:T(8,128)(2,1)} collective-permute-done((bf16[384,768]{1,0:T(8,128)(2,1)}, bf16[384,768]{1,0:T(8,128)(2,1)}, u32[]{:S(2)}, u32[]{:S(2)}) %collective-permute-start.21) | collective-permute-done | bytes 589856 | tf_op jit(solution)/shard_map/ppermute | solution.py:28
  181.3 13.7 %attention_backward.1 = (bf16[4,128,768]{2,1,0:T(8,128)(2,1)}, f32[128,768]{1,0:T(8,128)}, f32[12,128]{1,0:T(8,128)}, f32[2,768]{1,0:T(2,128)}) custom-call(bf16[2,96,768]{2,1,0:T(8,128)(2,1)} %copy-done.4, bf16[2,96,768]{2,1,0:T(8,128)(2,1)} %copy-done.21, bf16[3,96,768]{2,1,0:T(8,128)(2,1)} %copy-done.3, bf16[3,96,768]{2,1,0:T(8,128)(2,1)} %copy-done.13, ...), custom_call_target="tpu_custom_call" | custom-call | tf_op jit(solution)/shard_map/attention_backward/pallas_call | solution.py:229
  207.0 2.4 collective-permute-start.24
  209.5 3.8 %collective-permute-start.26 = (bf16[1,48,768]{2,1,0:T(8,128)(2,1)S(1)}, bf16[1,48,768]{2,1,0:T(8,128)(2,1)S(1)}, u32[]{:S(2)}, u32[]{:S(2)}) collective-permute-start(bf16[1,48,768]{2,1,0:T(8,128)(2,1)S(1)} %get-tuple-element.91), channel_id=1, source_target_pairs={{0,7},{1,6},{2,5},{3,4},{4,3},{5,2},{6,1},{7,0},{8,15},{9,14},{10,... | collective-permute-start | bytes 221192 | tf_op jit(solution)/shard_map/ppermute | solution.py:28
  213.9 5.1 %collective-permute-done.43 = f32[3072]{0:T(1024)S(1)} collective-permute-done((f32[3072]{0:T(1024)S(1)}, f32[3072]{0:T(1024)S(1)}, u32[]{:S(2)}, u32[]{:S(2)}) %collective-permute-start.43) | collective-permute-done | bytes 12320 | tf_op jit(solution)/shard_map/ppermute | solution.py:28
  220.8 3.0 %collective-permute-start.28 = (bf16[1,48,768]{2,1,0:T(8,128)(2,1)S(1)}, bf16[1,48,768]{2,1,0:T(8,128)(2,1)S(1)}, u32[]{:S(2)}, u32[]{:S(2)}) collective-permute-start(bf16[1,48,768]{2,1,0:T(8,128)(2,1)S(1)} %get-tuple-element.89), channel_id=1, source_target_pairs={{0,2},{1,3},{2,0},{3,1},{4,6},{5,7},{6,4},{7,5},{8,10},{9,11},{10,... | collective-permute-start | bytes 221192 | tf_op jit(solution)/shard_map/ppermute | solution.py:28
  230.0 12.3 %collective-permute-done.35 = bf16[4,96,768]{2,1,0:T(8,128)(2,1)S(1)} collective-permute-done((bf16[4,96,768]{2,1,0:T(8,128)(2,1)S(1)}, bf16[4,96,768]{2,1,0:T(8,128)(2,1)S(1)}, u32[]{:S(2)}, u32[]{:S(2)}) %collective-permute-start.35) | collective-permute-done | bytes 589856 | tf_op jit(solution)/shard_map/ppermute | solution.py:28
  249.3 8.6 %collective-permute-done.37 = bf16[96,768]{1,0:T(8,128)(2,1)S(1)} collective-permute-done((bf16[96,768]{1,0:T(8,128)(2,1)S(1)}, bf16[96,768]{1,0:T(8,128)(2,1)S(1)}, u32[]{:S(2)}, u32[]{:S(2)}) %collective-permute-start.37) | collective-permute-done | bytes 147488 | tf_op jit(solution)/shard_map/ppermute | solution.py:28
  (209 shorter events, 68.1 us)
Async XLA Ops:
  3.7 12.8 %collective-permute-start.1 = (bf16[96,768]{1,0:T(8,128)(2,1)}, bf16[96,768]{1,0:T(8,128)(2,1)S(1)}, u32[]{:S(2)}, u32[]{:S(2)}) collective-permute-start(bf16[96,768]{1,0:T(8,128)(2,1)} %param.14), channel_id=1, source_target_pairs={{0,2},{1,3},{2,0},{3,1},{4,6},{5,7},{6,4},{7,5},{8,10},{9,11},{10,... | collective-permute-start | bytes 442376 | tf_op jit(solution)/shard_map/ppermute | solution.py:28
  5.3 14.1 %collective-permute-start.2 = (bf16[96,768]{1,0:T(8,128)(2,1)}, bf16[96,768]{1,0:T(8,128)(2,1)S(1)}, u32[]{:S(2)}, u32[]{:S(2)}) collective-permute-start(bf16[96,768]{1,0:T(8,128)(2,1)} %param.14), channel_id=1, source_target_pairs={{0,4},{1,5},{2,6},{3,7},{4,0},{5,1},{6,2},{7,3},{8,12},{9,13},{10,... | collective-permute-start | bytes 442376 | tf_op jit(solution)/shard_map/ppermute | solution.py:28
  32.7 15.1 %collective-permute-start.10 = (bf16[3,96,768]{2,1,0:T(8,128)(2,1)S(1)}, bf16[3,96,768]{2,1,0:T(8,128)(2,1)S(1)}, u32[]{:S(2)}, u32[]{:S(2)}) collective-permute-start(bf16[3,96,768]{2,1,0:T(8,128)(2,1)S(1)} %pad_maximum_fusion.2.refs_2_), channel_id=1, source_target_pairs={{0,8},{8,0},{16,24},{24,16},{1,9},{9,1},{17,25},{25,17},{2,10},{10... | collective-permute-start | bytes 1327112 | tf_op jit(solution)/shard_map/ppermute | solution.py:28
  33.3 14.6 %collective-permute-start.11 = (bf16[3,96,768]{2,1,0:T(8,128)(2,1)S(1)}, bf16[3,96,768]{2,1,0:T(8,128)(2,1)S(1)}, u32[]{:S(2)}, u32[]{:S(2)}) collective-permute-start(bf16[3,96,768]{2,1,0:T(8,128)(2,1)S(1)} %collective-permute-done.5.refs_3_), channel_id=1, source_target_pairs={{0,8},{8,0},{16,24},{24,16},{1,9},{9,1},{17,25},{25,17},{2,10},{10... | collective-permute-start | bytes 1327112 | tf_op jit(solution)/shard_map/ppermute | solution.py:28
  33.4 14.5 %collective-permute-start.12 = (bf16[3,96,768]{2,1,0:T(8,128)(2,1)S(1)}, bf16[3,96,768]{2,1,0:T(8,128)(2,1)}, u32[]{:S(2)}, u32[]{:S(2)}) collective-permute-start(bf16[3,96,768]{2,1,0:T(8,128)(2,1)S(1)} %collective-permute-done.6.refs_4_), channel_id=1, source_target_pairs={{0,8},{8,0},{16,24},{24,16},{1,9},{9,1},{17,25},{25,17},{2,10},{10... | collective-permute-start | bytes 1327112 | tf_op jit(solution)/shard_map/ppermute | solution.py:28
  80.5 18.8 %all-to-all-start.1 = ((bf16[8,48,768]{2,1,0:T(8,128)(2,1)}), bf16[8,48,768]{2,1,0:T(8,128)(2,1)S(1)}, u32[]{:S(2)}, u32[]{:S(2)}) async-start(bf16[8,48,768]{2,1,0:T(8,128)(2,1)} %bitcast.12), calls=%async_computation.1 | async-start | bytes 1179648 | tf_op jit(solution)/shard_map/all_to_all | solution.py:353
  84.3 17.1 %collective-permute-start.15 = (bf16[384,768]{1,0:T(8,128)(2,1)S(1)}, bf16[384,768]{1,0:T(8,128)(2,1)S(1)}, u32[]{:S(2)}, u32[]{:S(2)}) collective-permute-start(bf16[384,768]{1,0:T(8,128)(2,1)S(1)} %bitcast.86), channel_id=1, source_target_pairs={{0,16},{8,24},{16,0},{24,8},{1,17},{9,25},{17,1},{25,9},{2,18},{10... | collective-permute-start | bytes 1769480 | tf_op jit(solution)/shard_map/ppermute | solution.py:28
  99.4 13.2 %collective-permute-start.18 = (bf16[384,768]{1,0:T(8,128)(2,1)S(1)}, bf16[384,768]{1,0:T(8,128)(2,1)S(1)}, u32[]{:S(2)}, u32[]{:S(2)}) collective-permute-start(bf16[384,768]{1,0:T(8,128)(2,1)S(1)} %bitcast.90), channel_id=1, source_target_pairs={{0,16},{8,24},{16,0},{24,8},{1,17},{9,25},{17,1},{25,9},{2,18},{10... | collective-permute-start | bytes 1769480 | tf_op jit(solution)/shard_map/ppermute | solution.py:28
  100.9 11.8 %collective-permute-start.14 = (bf16[384,768]{1,0:T(8,128)(2,1)S(1)}, bf16[384,768]{1,0:T(8,128)(2,1)S(1)}, u32[]{:S(2)}, u32[]{:S(2)}) collective-permute-start(bf16[384,768]{1,0:T(8,128)(2,1)S(1)} %bitcast.87), channel_id=1, source_target_pairs={{0,8},{8,0},{16,24},{24,16},{1,9},{9,1},{17,25},{25,17},{2,10},{10... | collective-permute-start | bytes 1769480 | tf_op jit(solution)/shard_map/ppermute | solution.py:28
  100.9 11.8 %collective-permute-start.17 = (bf16[384,768]{1,0:T(8,128)(2,1)S(1)}, bf16[384,768]{1,0:T(8,128)(2,1)S(1)}, u32[]{:S(2)}, u32[]{:S(2)}) collective-permute-start(bf16[384,768]{1,0:T(8,128)(2,1)S(1)} %bitcast.91), channel_id=1, source_target_pairs={{0,8},{8,0},{16,24},{24,16},{1,9},{9,1},{17,25},{25,17},{2,10},{10... | collective-permute-start | bytes 1769480 | tf_op jit(solution)/shard_map/ppermute | solution.py:28
  127.0 13.4 %collective-permute-start.22 = (bf16[2,384,768]{2,1,0:T(8,128)(2,1)}, bf16[2,384,768]{2,1,0:T(8,128)(2,1)S(1)}, u32[]{:S(2)}, u32[]{:S(2)}) collective-permute-start(bf16[2,384,768]{2,1,0:T(8,128)(2,1)} %get-tuple-element.65), channel_id=1, source_target_pairs={{0,8},{8,0},{16,24},{24,16},{1,9},{9,1},{17,25},{25,17},{2,10},{10... | collective-permute-start | bytes 3538952 | tf_op jit(solution)/shard_map/ppermute | solution.py:28
  140.1 24.0 %collective-permute-start.20 = (bf16[2,384,768]{2,1,0:T(8,128)(2,1)}, bf16[2,384,768]{2,1,0:T(8,128)(2,1)}, u32[]{:S(2)}, u32[]{:S(2)}) collective-permute-start(bf16[2,384,768]{2,1,0:T(8,128)(2,1)} %get-tuple-element.63), channel_id=1, source_target_pairs={{0,8},{8,0},{16,24},{24,16},{1,9},{9,1},{17,25},{25,17},{2,10},{10... | collective-permute-start | bytes 3538952 | tf_op jit(solution)/shard_map/ppermute | solution.py:28
  141.5 16.2 %collective-permute-start.23 = (bf16[384,768]{1,0:T(8,128)(2,1)S(1)}, bf16[384,768]{1,0:T(8,128)(2,1)S(1)}, u32[]{:S(2)}, u32[]{:S(2)}) collective-permute-start(bf16[384,768]{1,0:T(8,128)(2,1)S(1)} %fusion.7), channel_id=1, source_target_pairs={{0,16},{8,24},{16,0},{24,8},{1,17},{9,25},{17,1},{25,9},{2,18},{10... | collective-permute-start | bytes 1769480 | tf_op jit(solution)/shard_map/ppermute | solution.py:28
  143.1 24.5 %collective-permute-start.31 = (bf16[2,128,768]{2,1,0:T(8,128)(2,1)S(1)}, bf16[2,128,768]{2,1,0:T(8,128)(2,1)S(1)}, u32[]{:S(2)}, u32[]{:S(2)}) collective-permute-start(bf16[2,128,768]{2,1,0:T(8,128)(2,1)S(1)} %get-tuple-element.100), channel_id=1, source_target_pairs={{0,16},{8,24},{16,0},{24,8},{1,17},{9,25},{17,1},{25,9},{2,18},{10... | collective-permute-start | bytes 1179656 | tf_op jit(solution)/shard_map/ppermute | solution.py:28
  158.8 22.5 %all-to-all-start.2 = ((bf16[8,48,768]{2,1,0:T(8,128)(2,1)}), bf16[8,48,768]{2,1,0:T(8,128)(2,1)}, u32[]{:S(2)}, u32[]{:S(2)}) async-start(bf16[8,48,768]{2,1,0:T(8,128)(2,1)} %bitcast.20), calls=%async_computation.2 | async-start | bytes 1179648 | tf_op jit(solution)/shard_map/all_to_all | solution.py:353
  166.1 13.8 %collective-permute-start.21 = (bf16[384,768]{1,0:T(8,128)(2,1)}, bf16[384,768]{1,0:T(8,128)(2,1)}, u32[]{:S(2)}, u32[]{:S(2)}) collective-permute-start(bf16[384,768]{1,0:T(8,128)(2,1)} %fusion.6), channel_id=1, source_target_pairs={{0,16},{8,24},{16,0},{24,8},{1,17},{9,25},{17,1},{25,9},{2,18},{10... | collective-permute-start | bytes 1769480 | tf_op jit(solution)/shard_map/ppermute | solution.py:28
  168.5 27.9 %collective-permute-start.32 = (bf16[2,2,128,768]{3,2,0,1:T(8,128)(2,1)}, bf16[2,2,128,768]{3,2,0,1:T(8,128)(2,1)}, u32[]{:S(2)}, u32[]{:S(2)}) collective-permute-start(bf16[2,2,128,768]{3,2,0,1:T(8,128)(2,1)} %pad_maximum_fusion), channel_id=1, source_target_pairs={{0,8},{8,0},{16,24},{24,16},{1,9},{9,1},{17,25},{25,17},{2,10},{10... | collective-permute-start | bytes 2359304 | tf_op jit(solution)/shard_map/ppermute | solution.py:28
  203.3 20.6 %collective-permute-start.33 = (bf16[2,128,768]{2,1,0:T(8,128)(2,1)S(1)}, bf16[2,128,768]{2,1,0:T(8,128)(2,1)S(1)}, u32[]{:S(2)}, u32[]{:S(2)}) collective-permute-start(bf16[2,128,768]{2,1,0:T(8,128)(2,1)S(1)} %get-tuple-element.82), channel_id=1, source_target_pairs={{0,16},{8,24},{16,0},{24,8},{1,17},{9,25},{17,1},{25,9},{2,18},{10... | collective-permute-start | bytes 1179656 | tf_op jit(solution)/shard_map/ppermute | solution.py:28
  207.0 13.8 %collective-permute-start.24 = (bf16[1,48,768]{2,1,0:T(8,128)(2,1)S(1)}, bf16[1,48,768]{2,1,0:T(8,128)(2,1)S(1)}, u32[]{:S(2)}, u32[]{:S(2)}) collective-permute-start(bf16[1,48,768]{2,1,0:T(8,128)(2,1)S(1)} %get-tuple-element.93), channel_id=1, source_target_pairs={{0,6},{1,7},{2,4},{3,5},{4,2},{5,3},{6,0},{7,1},{8,14},{9,15},{10,... | collective-permute-start | bytes 221192 | tf_op jit(solution)/shard_map/ppermute | solution.py:28
  209.4 14.6 %collective-permute-start.25 = (bf16[1,48,768]{2,1,0:T(8,128)(2,1)S(1)}, bf16[1,48,768]{2,1,0:T(8,128)(2,1)S(1)}, u32[]{:S(2)}, u32[]{:S(2)}) collective-permute-start(bf16[1,48,768]{2,1,0:T(8,128)(2,1)S(1)} %get-tuple-element.92), channel_id=1, source_target_pairs={{0,4},{1,5},{2,6},{3,7},{4,0},{5,1},{6,2},{7,3},{8,12},{9,13},{10,... | collective-permute-start | bytes 221192 | tf_op jit(solution)/shard_map/ppermute | solution.py:28
  209.5 14.6 %collective-permute-start.26 = (bf16[1,48,768]{2,1,0:T(8,128)(2,1)S(1)}, bf16[1,48,768]{2,1,0:T(8,128)(2,1)S(1)}, u32[]{:S(2)}, u32[]{:S(2)}) collective-permute-start(bf16[1,48,768]{2,1,0:T(8,128)(2,1)S(1)} %get-tuple-element.91), channel_id=1, source_target_pairs={{0,7},{1,6},{2,5},{3,4},{4,3},{5,2},{6,1},{7,0},{8,15},{9,14},{10,... | collective-permute-start | bytes 221192 | tf_op jit(solution)/shard_map/ppermute | solution.py:28
  226.7 15.5 %collective-permute-start.35 = (bf16[4,96,768]{2,1,0:T(8,128)(2,1)S(1)}, bf16[4,96,768]{2,1,0:T(8,128)(2,1)S(1)}, u32[]{:S(2)}, u32[]{:S(2)}) collective-permute-start(bf16[4,96,768]{2,1,0:T(8,128)(2,1)S(1)} %fusion.8), channel_id=1, source_target_pairs={{0,1},{1,0},{2,3},{3,2},{4,5},{5,4},{6,7},{7,6},{8,9},{9,8},{10,11... | collective-permute-start | bytes 1769480 | tf_op jit(solution)/shard_map/ppermute | solution.py:28
  244.4 13.4 %collective-permute-start.37 = (bf16[96,768]{1,0:T(8,128)(2,1)S(1)}, bf16[96,768]{1,0:T(8,128)(2,1)S(1)}, u32[]{:S(2)}, u32[]{:S(2)}) collective-permute-start(bf16[96,768]{1,0:T(8,128)(2,1)S(1)} %get-tuple-element.80), channel_id=1, source_target_pairs={{0,4},{1,5},{2,6},{3,7},{4,0},{5,1},{6,2},{7,3},{8,12},{9,13},{10,... | collective-permute-start | bytes 442376 | tf_op jit(solution)/shard_map/ppermute | solution.py:28
  244.9 12.9 %collective-permute-start.38 = (bf16[96,768]{1,0:T(8,128)(2,1)S(1)}, bf16[96,768]{1,0:T(8,128)(2,1)S(1)}, u32[]{:S(2)}, u32[]{:S(2)}) collective-permute-start(bf16[96,768]{1,0:T(8,128)(2,1)S(1)} %get-tuple-element.79), channel_id=1, source_target_pairs={{0,6},{1,7},{2,4},{3,5},{4,2},{5,3},{6,0},{7,1},{8,14},{9,15},{10,... | collective-permute-start | bytes 442376 | tf_op jit(solution)/shard_map/ppermute | solution.py:28
  (58 other events, 559.4 us)
where the time goes:
time: 259 us
  waiting for transfers between devices  99.6 us (38%)
  starting transfers between devices  55.6 us (21%)
  Pallas kernels  47.6 us (18%)
  blocking collectives  22.3 us (9%)
  other arithmetic  14.6 us (6%)
  local copies, waits for them, and re-layouts  11.1 us (4%)
  matrix products  6.59 us (3%)
    ppermute x44, waiting for transfers between devices, swap(): return lax.ppermute(value, axis, [(i, i ^ bits) for i in range(size)])  86 us
    ppermute x44, starting transfers between devices, swap(): return lax.ppermute(value, axis, [(i, i ^ bits) for i in range(size)])  46.5 us
    all_to_all x1, blocking collectives, exchange_plain(): lax.all_to_all(chunks, 'expert', split_axis=0, concat_axis=0, tiled=True)  22.3 us
    pallas_call x1, Pallas kernels, attention_backward(): pl.pallas_call(kernel, out_shape=(jax.ShapeDtypeStruct((4, count, width),...  13.7 us
    all_to_all x2, waiting for transfers between devices, exchange_plain(): lax.all_to_all(chunks, 'expert', split_axis=0, concat_axis=0, tiled=True)  13.5 us
    pallas_call x1, Pallas kernels, experts_second(): pl.pallas_call(kernel, out_shape=(jax.ShapeDtypeStruct((2, count, width),...  12.9 us
    pallas_call x1, Pallas kernels, experts_first(): pl.pallas_call(kernel, out_shape=(jax.ShapeDtypeStruct((4, count, units),...  11.6 us
    pallas_call x1, Pallas kernels, attention_forward(): pl.pallas_call(kernel, out_shape=(jax.ShapeDtypeStruct((count, width), bf...  9.46 us
  transfers between devices with their start and end apart: 46, of which 18 were waited for; matrix products, arithmetic and copies ran while one was open for 11% of the time, Pallas kernels for 10%

commit v1 on v0

v1 whole, which is shorter than its diff:
```python
import jax
import jax.numpy as jnp
import numpy as np
from jax import lax
from jax.experimental import pallas as pl
from jax.experimental.pallas import tpu as pltpu
from jax.sharding import PartitionSpec as P

epsilon = 1e-06
top_precision = lax.Precision.HIGHEST
f32 = jnp.float32
bf16 = jnp.bfloat16


def bucket_table(length, top_bucket):
    offset = np.arange(length)[:, None] - np.arange(length)[None, :]
    offset = np.maximum(offset, 0)
    octave = offset * 0
    for exponent in range(1, 24):
        octave = octave + (offset >= 2**exponent)
    shifted = offset >> np.maximum(octave - 2, 0)
    logbucket = 16 + 4 * (octave - 4) + (shifted & 3)
    return np.where(offset < 16, offset, np.minimum(logbucket, top_bucket))


def swap(value, axis, bits):
    size = lax.axis_size(axis)
    return lax.ppermute(value, axis, [(i, i ^ bits) for i in range(size)])


def swap_core(value):
    return swap(value, "dp", 1)


def swap_x(value):
    return swap(value, "dp", 2)


def gather_projections(block, d_buffer, prepared):
    experts = lax.axis_size("expert")
    if experts != 8:
        full = lax.all_gather(block, ("dp", "expert"), axis=0, tiled=True)
        return [full[None]], [None], exchange_plain(d_buffer), prepared
    first = [swap(block, "expert", bits) for bits in (4, 6, 2, 1)] + [swap_x(block)]
    first, prepared = lax.optimization_barrier((first, prepared))
    z_far, z_last, z_near, near_y, near_x = first
    two = jnp.stack([z_far, z_near])
    two_y = swap(two, "expert", 1)
    two_x = swap_x(two)
    last_x = swap_x(z_last)
    last_y = swap(z_last, "expert", 1)
    near_xy = swap(near_x, "expert", 1)
    two_y, last_x = lax.optimization_barrier((two_y, last_x))
    two_yx = swap_x(two_y)
    last_xy = swap(last_x, "expert", 1)
    two_x, d_buffer = lax.optimization_barrier((two_x, d_buffer))
    d_got = exchange_plain(d_buffer)
    one = jnp.stack([block, near_y, near_x])
    arrays = [one, two, two_y, two_x, two_yx]
    offsets = [
        [(0, 0), (0, 1), (2, 0)],
        [(0, 4), (0, 2)],
        [(0, 5), (0, 3)],
        [(2, 4), (2, 2)],
        [(2, 5), (2, 3)],
    ]
    rest = jnp.stack([z_last, last_x, last_y, near_xy])
    arrays = arrays + [rest, last_xy[None]]
    offsets = offsets + [[(0, 6), (2, 6), (0, 7), (2, 1)], [(2, 7)]]
    arrays = arrays + [swap_core(a) for a in arrays]
    offsets = offsets + [[(d + 1, e) for d, e in group] for group in offsets]
    return arrays, offsets, d_got, prepared


def place_projections(pieces, offsets, dense, sems):
    copies = []
    d_here, e_here = lax.axis_index("dp"), lax.axis_index("expert")
    experts = lax.axis_size("expert")
    for piece, group in zip(pieces, offsets):
        rows = piece.shape[1]
        for i in range(piece.shape[0]):
            target = dense
            if group is not None:
                block = (d_here ^ group[i][0]) * experts + (e_here ^ group[i][1])
                target = dense.at[pl.ds(pl.multiple_of(block * rows, rows), rows)]
            copies.append(pltpu.make_async_copy(piece.at[i], target, sems.at[len(copies)]))
    for copy in copies:
        copy.start()
    return copies


VMEM = pl.BlockSpec(memory_space=pltpu.VMEM)
ANY = pl.BlockSpec(memory_space=pl.ANY)
LIMIT = pltpu.CompilerParams(vmem_limit_bytes=58 * 1024 * 1024)


def cost(microseconds):
    return pl.CostEstimate(
        flops=int(microseconds * 1.0e9), bytes_accessed=int(microseconds * 3.0e6), transcendentals=0
    )


def dot(a, b):
    return jnp.dot(a, b, preferred_element_type=f32)


def dot_t(a, b):
    return lax.dot_general(a, b, (((1,), (1,)), ((), ())), preferred_element_type=f32)


def t_dot(a, b):
    return lax.dot_general(a, b, (((0,), (0,)), ((), ())), preferred_element_type=f32)


def inverse_rms(values):
    return lax.rsqrt(jnp.mean(values * values, axis=-1, keepdims=True) + epsilon)


def attention_forward(
    pieces, offsets, tokens, gains, bias_rows, docs_row, select, heads
):
    count, width = tokens.shape
    slots = select.shape[0]
    blocks = sum(p.shape[0] for p in pieces)
    n = len(pieces)

    def kernel(*refs):
        piece_refs, refs = refs[:n], refs[n:]
        tok, gain, bias, drow, sel = refs[:5]
        normed_o, mixed_o, qkv_o, probs_o, residual_o, buffer_o, dense, sems = refs[5:]
        copies = place_projections(piece_refs, offsets, dense, sems)
        x = tok[...].astype(f32)
        normed = (x * inverse_rms(x) * gain[0:1, :]).astype(bf16)
        normed_o[...] = normed
        row = lax.broadcasted_iota(jnp.int32, (count, count), 0)
        col = lax.broadcasted_iota(jnp.int32, (count, count), 1)
        docs = jnp.broadcast_to(drow[...], (count, count))
        allowed = (docs == docs.T) & (col <= row)
        low_lanes = lax.broadcasted_iota(jnp.int32, (count, 128), 1) < 64
        for copy in copies:
            copy.wait()
        for i in range(3):
            qkv_o[i] = dot(normed, dense[i * width : (i + 1) * width, :]).astype(bf16)
        for pair in range(heads // 2):
            lanes = slice(128 * pair, 128 * pair + 128)
            q, k, v = qkv_o[0, :, lanes], qkv_o[1, :, lanes], qkv_o[2, :, lanes]
            out = []
            for half in range(2):
                mask = low_lanes if half == 0 else ~low_lanes
                head = 2 * pair + half
                shift = jnp.broadcast_to(bias[head : head + 1, :], (count, 128))
                shift = pltpu.roll(shift, 0, 1, stride=1, stride_axis=0)
                scores = dot_t(jnp.where(mask, q, jnp.zeros_like(q)), k) * 0.125 + shift
                scores = jnp.where(allowed, scores, -1000000000.0)
                scores = jnp.exp(scores - jnp.max(scores, axis=-1, keepdims=True))
                probs = scores / jnp.sum(scores, axis=-1, keepdims=True)
                probs_o[head] = probs
                out.append(dot(probs.astype(bf16), v))
            mixed_o[:, lanes] = jnp.where(low_lanes, out[0], out[1]).astype(bf16)
        residual = x + dot(mixed_o[...], dense[3 * width : 4 * width, :])
        residual_o[...] = residual
        moe_in = (residual * inverse_rms(residual) * gain[1:2, :]).astype(bf16)
        buffer_o[...] = dot(sel[...], moe_in).astype(bf16)

    return pl.pallas_call(
        kernel,
        out_shape=(
            jax.ShapeDtypeStruct((count, width), bf16),
            jax.ShapeDtypeStruct((count, width), bf16),
            jax.ShapeDtypeStruct((3, count, width), bf16),
            jax.ShapeDtypeStruct((heads, count, count), f32),
            jax.ShapeDtypeStruct((count, width), f32),
            jax.ShapeDtypeStruct((slots, width), bf16),
        ),
        in_specs=[ANY] * n + [VMEM] * 5,
        out_specs=(VMEM,) * 6,
        scratch_shapes=[
            pltpu.VMEM((4 * width, width), bf16),
            pltpu.SemaphoreType.DMA((blocks,)),
        ],
        compiler_params=LIMIT,
        cost_estimate=cost(3),
        name="attention_forward",
    )(*pieces, tokens, gains, bias_rows, docs_row, select)


def attention_backward(
    pieces, offsets, tokens, gains, cotangent, residual, d_returned, select_t, qkv, probs, heads
):
    count, width = tokens.shape
    blocks = sum(p.shape[0] for p in pieces)
    n = len(pieces)

    def kernel(*refs):
        piece_refs, refs = refs[:n], refs[n:]
        tok, gain, cot, res, d_ret, sel_t, qkv_r, probs_r = refs[:8]
        outs, (d_tok_o, small_o) = refs[8:12], refs[12:14]
        dense, d_mixed_s, grads_o, packed_s, sems = refs[14:]
        d_here = lax.axis_index("dp")
        copies = place_projections(piece_refs, offsets, dense, sems)
        d_moe = dot(sel_t[...], d_ret[...])
        residual = res[...]
        r = inverse_rms(residual)
        small_o[3:4, :] = jnp.sum(d_moe * residual * r, axis=0, keepdims=True)
        m = d_moe * gain[1:2, :]
        mean = jnp.mean(m * residual, axis=-1, keepdims=True)
        d_residual = cot[...].astype(f32) + r * m - r * r * r * residual * mean
        d_tok_o[...] = d_residual
        d_attn = d_residual.astype(bf16)
        grads_o[d_here ^ 3] = d_attn
        for copy in copies:
            copy.wait()
        d_mixed_s[...] = dot_t(d_attn, dense[3 * width : 4 * width, :]).astype(bf16)
        low_lanes = lax.broadcasted_iota(jnp.int32, (count, 128), 1) < 64
        row = lax.broadcasted_iota(jnp.int32, (count, count), 0)
        for pair in range(heads // 2):
            lanes = slice(128 * pair, 128 * pair + 128)
            q, k, v = qkv_r[0, :, lanes], qkv_r[1, :, lanes], qkv_r[2, :, lanes]
            d_mix = d_mixed_s[:, lanes]
            d_q, d_k, d_v = [], [], []
            for half in range(2):
                mask = low_lanes if half == 0 else ~low_lanes
                head = 2 * pair + half
                probs = probs_r[head]
                d_probs = dot_t(jnp.where(mask, d_mix, jnp.zeros_like(d_mix)), v)
                d_v.append(t_dot(probs.astype(bf16), d_mix))
                inner = jnp.sum(probs * d_probs, axis=-1, keepdims=True)
                d_scores = (probs * (d_probs - inner)).astype(bf16)
                d_q.append(dot(d_scores, k))
                d_k.append(t_dot(d_scores, q))
                turned = d_scores.astype(f32)
                for bit in (1, 2, 4, 8, 16, 32, 64):
                    turned = jnp.where(
                        (row & bit) != 0, pltpu.roll(turned, count - bit, 1), turned
                    )
                at, slot = head // 6, 128 * (head % 6)
                small_o[at : at + 1, slot : slot + 128] = jnp.sum(turned, axis=0, keepdims=True)
            grads_o[d_here ^ 0, :, lanes] = (jnp.where(low_lanes, d_q[0], d_q[1]) * 0.125).astype(bf16)
            grads_o[d_here ^ 1, :, lanes] = (jnp.where(low_lanes, d_k[0], d_k[1]) * 0.125).astype(bf16)
            grads_o[d_here ^ 2, :, lanes] = jnp.where(low_lanes, d_v[0], d_v[1]).astype(bf16)
        outs[0][...] = grads_o[0]
        d_normed = dot_t(grads_o[d_here ^ 0], dense[0:width, :])
        d_normed = d_normed + dot_t(grads_o[d_here ^ 1], dense[width : 2 * width, :])
        d_normed = d_normed + dot_t(grads_o[d_here ^ 2], dense[2 * width : 3 * width, :])
        x = tok[...].astype(f32)
        s = inverse_rms(x)
        small_o[2:3, :] = jnp.sum(d_normed * x * s, axis=0, keepdims=True)
        m = d_normed * gain[0:1, :]
        mean = jnp.mean(m * x, axis=-1, keepdims=True)
        d_tok_o[...] += s * m - s * s * s * x * mean
        small = small_o[0:4, :]
        high = small.astype(bf16).astype(f32)
        packed_s[...] = jnp.zeros_like(packed_s)
        packed_s[0:4, :] = high
        packed_s[4:8, :] = small - high
        for i in range(1, 4):
            outs[i][0:count, :] = grads_o[i]
            outs[i][count:, :] = packed_s[...].astype(bf16)

    return pl.pallas_call(
        kernel,
        out_shape=(jax.ShapeDtypeStruct((count, width), bf16),)
        + (jax.ShapeDtypeStruct((count + 16, width), bf16),) * 3
        + (
            jax.ShapeDtypeStruct((count, width), f32),
            jax.ShapeDtypeStruct((8, width), f32),
        ),
        in_specs=[ANY] * n + [VMEM] * 8,
        out_specs=(VMEM,) * 6,
        scratch_shapes=[
            pltpu.VMEM((4 * width, width), bf16),
            pltpu.VMEM((count, width), bf16),
            pltpu.VMEM((4, count, width), bf16),
            pltpu.VMEM((16, width), f32),
            pltpu.SemaphoreType.DMA((blocks,)),
        ],
        compiler_params=LIMIT,
        cost_estimate=cost(13),
        name="attention_backward",
    )(*pieces, tokens, gains, cotangent, residual, d_returned, select_t, qkv, probs)


def gelu_parts(v):
    c = 0.7978845608028654
    square = v * v
    t = jnp.tanh(c * v * (1.0 + 0.044715 * square))
    half = 0.5 * (1.0 + t)
    slope = half + 0.5 * v * (1.0 - t * t) * (c + (3.0 * 0.044715 * c) * square)
    return v * half, slope


def experts_first(rows, d_rows, win, wout):
    count, width = rows[0].shape
    units = win.shape[1]

    def kernel(*refs):
        row_refs, d_refs, (win_r, wout_r) = refs[0:2], refs[2:4], refs[4:6]
        hidden_o, d_pre_o, keep_o, send_o, row_s, d_s, win_s, wout_s, sems = refs[6:]
        sources = (d_refs[1], wout_r, row_refs[1], win_r, d_refs[0], row_refs[0])
        targets = (d_s.at[1], wout_s, row_s.at[1], win_s, d_s.at[0], row_s.at[0])
        copies = [
            pltpu.make_async_copy(source, target, sems.at[n])
            for n, (source, target) in enumerate(zip(sources, targets))
        ]
        for copy in copies:
            copy.start()
        for i in (1, 0):
            for copy in copies[0:4] if i else copies[4:6]:
                copy.wait()
            d_hidden = dot_t(d_s[i], wout_s[...])
            pre = dot(row_s[i], win_s[...])
            hidden, slope = gelu_parts(pre)
            hidden_o[i] = hidden.astype(bf16)
            d_pre = (d_hidden * slope).astype(bf16)
            d_pre_o[i] = d_pre
            d_slot = dot_t(d_pre, win_s[...])
            if i == 1:
                send_o[...] = d_slot.astype(bf16)
            else:
                keep_o[...] = d_slot

    return pl.pallas_call(
        kernel,
        out_shape=(
            jax.ShapeDtypeStruct((2, count, units), bf16),
            jax.ShapeDtypeStruct((2, count, units), bf16),
            jax.ShapeDtypeStruct((count, width), f32),
            jax.ShapeDtypeStruct((count, width), bf16),
        ),
        in_specs=[ANY] * 6,
        out_specs=(VMEM,) * 4,
        scratch_shapes=[
            pltpu.VMEM((2, count, width), bf16),
            pltpu.VMEM((2, count, width), bf16),
            pltpu.VMEM(win.shape, bf16),
            pltpu.VMEM(wout.shape, bf16),
            pltpu.SemaphoreType.DMA((6,)),
        ],
        compiler_params=LIMIT,
        cost_estimate=cost(6),
        name="experts_first",
    )(*rows, *d_rows, win, wout)


def experts_result(hidden, wout):
    _, count, units = hidden.shape
    width = wout.shape[1]

    def kernel(hidden_r, wout_r, keep_o, send_o):
        send_o[...] = dot(hidden_r[1], wout_r[...]).astype(bf16)
        keep_o[...] = dot(hidden_r[0], wout_r[...])

    return pl.pallas_call(
        kernel,
        out_shape=(
            jax.ShapeDtypeStruct((count, width), f32),
            jax.ShapeDtypeStruct((count, width), bf16),
        ),
        in_specs=[VMEM] * 2,
        out_specs=(VMEM,) * 2,
        compiler_params=LIMIT,
        cost_estimate=cost(2),
        name="experts_result",
    )(hidden, wout)


def experts_gradients(rows, d_rows, hidden, d_pre):
    width = rows[0].shape[1]
    units = hidden[0].shape[2]

    def kernel(*refs):
        row_refs, d_refs, hidden_r, d_pre_r = refs[0:4], refs[4:8], refs[8:10], refs[10:12]
        in_o, out_o = refs[12:]
        for i in range(4):
            g_in = t_dot(row_refs[i][...], d_pre_r[i // 2][i % 2])
            g_out = t_dot(hidden_r[i // 2][i % 2], d_refs[i][...])
            if i == 0:
                in_o[...] = g_in
                out_o[...] = g_out
            else:
                in_o[...] += g_in
                out_o[...] += g_out

    return pl.pallas_call(
        kernel,
        out_shape=(
            jax.ShapeDtypeStruct((width, units), f32),
            jax.ShapeDtypeStruct((units, width), f32),
        ),
        in_specs=[VMEM] * 12,
        out_specs=(VMEM,) * 2,
        compiler_params=LIMIT,
        cost_estimate=cost(10),
        name="experts_gradients",
    )(*rows, *d_rows, *hidden, *d_pre)


def block_output(returned, residual, first_t, second_t, gates):
    def kernel(held, res, first, second, gate, out):
        moe_out = gate[:, 0:1] * dot(first[...], held[...])
        moe_out = moe_out + gate[:, 1:2] * dot(second[...], held[...])
        out[...] = (res[...] + moe_out).astype(bf16)

    return pl.pallas_call(
        kernel,
        out_shape=jax.ShapeDtypeStruct(residual.shape, bf16),
        in_specs=[VMEM] * 5,
        out_specs=VMEM,
        compiler_params=LIMIT,
        cost_estimate=cost(3),
        name="block_output",
    )(returned, residual, first_t, second_t, gates)


def pack_small(packed, small):
    high = small.astype(bf16).astype(f32)
    packed[...] = jnp.zeros_like(packed)
    packed[0:12, :] = high
    packed[12:24, :] = small - high


def unpack_small(rows):
    rows = rows.astype(f32)
    return rows[0:12, :] + rows[12:24, :]


def shape_of(rows, width, dtype):
    return jax.ShapeDtypeStruct((rows, width), dtype)


def projection_gradient(normed, mixed, right, small):
    count, width = normed[0].shape
    block, first = width // 8, 2 * width // 3

    def kernel(*refs):
        normed_r, mixed_r, right_r, small_r = refs[0:4], refs[4:8], refs[8:12], refs[12]
        keep_y, send_y, keep_z = refs[13:16]
        send_z, small_o, total, packed = refs[16:19], refs[19], refs[20], refs[21]
        e_here = lax.axis_index("expert")
        last = lax.axis_index("dp") == 3
        y_here, z_here = lax.rem(e_here, 2), lax.div(e_here, 2)
        acc = None
        for i in range(4):
            left = jnp.where(last, mixed_r[i][...], normed_r[i][...])
            term = t_dot(left, right_r[i][0:count, :])
            acc = term if acc is None else acc + term
        for i in range(8):
            total[i] = acc[i * block : (i + 1) * block]
        for k in range(4):
            z_block = (z_here ^ k) * 2
            rows = slice(k * block, (k + 1) * block)
            keep_y[rows, :] = total[z_block + y_here, :, 0:first]
            send_y[rows, :] = total[z_block + 1 - y_here, :, 0:first].astype(bf16)
            for i, y in enumerate((y_here, 1 - y_here)):
                rows = slice(i * block, (i + 1) * block)
                if k == 0:
                    keep_z[rows, :] = total[z_block + y, :, first:]
                else:
                    send_z[k - 1][rows, :] = total[z_block + y, :, first:].astype(bf16)
        four = small_r[0:4, :]
        for i in range(1, 4):
            part = right_r[i][count:, :].astype(f32)
            four = four + part[0:4, :] + part[4:8, :]
        small_o[...] = jnp.zeros_like(small_o)
        for c in range(3):
            small_o[4 * c : 4 * c + 4, :] = four[:, 256 * c : 256 * c + 256]
        pack_small(packed, small_o[0:12, :])
        for k in range(3):
            send_z[k][2 * block :, :] = packed[...].astype(bf16)

    return pl.pallas_call(
        kernel,
        out_shape=(
            shape_of(4 * block, first, f32),
            shape_of(4 * block, first, bf16),
            shape_of(2 * block, width - first, f32),
        )
        + (shape_of(2 * block + 32, width - first, bf16),) * 3
        + (shape_of(16, 256, f32),),
        in_specs=[VMEM] * 13,
        out_specs=(VMEM,) * 7,
        scratch_shapes=[pltpu.VMEM((8, block, width), f32), pltpu.VMEM((32, 256), f32)],
        compiler_params=LIMIT,
        cost_estimate=cost(3),
        name="projection_gradient",
    )(*normed, *mixed, *right, small)


def middle_sums(keep_y, got_y, keep_z, got_z, small):
    block, first, rest = keep_z.shape[0] // 2, keep_y.shape[1], keep_z.shape[1]

    def kernel(keep_y, got_y, keep_z, z_1, z_2, z_3, small_r, *outs):
        own_y, send_y, own_z, send_z, small_o, packed = outs[0], outs[1:4], *outs[4:]
        for k in range(4):
            rows = slice(k * block, (k + 1) * block)
            sums = keep_y[rows, :] + got_y[rows, :].astype(f32)
            if k == 0:
                own_y[...] = sums
            else:
                send_y[k - 1][...] = sums.astype(bf16)
        sums = keep_z[...]
        small = small_r[0:12, :]
        for ref in (z_1, z_2, z_3):
            sums = sums + ref[0 : 2 * block, :].astype(f32)
            small = small + unpack_small(ref[2 * block :, :])
        own_z[...] = sums[0:block]
        send_z[0:block, :] = sums[block:].astype(bf16)
        small_o[...] = jnp.zeros_like(small_o)
        small_o[0:12, :] = small
        pack_small(packed, small)
        send_z[block:, :] = packed[...].astype(bf16)

    return pl.pallas_call(
        kernel,
        out_shape=(shape_of(block, first, f32),)
        + (shape_of(block, first, bf16),) * 3
        + (
            shape_of(block, rest, f32),
            shape_of(block + 32, rest, bf16),
            shape_of(16, 256, f32),
        ),
        in_specs=[VMEM] * 7,
        out_specs=(VMEM,) * 7,
        scratch_shapes=[pltpu.VMEM((32, 256), f32)],
        compiler_params=LIMIT,
        cost_estimate=cost(1),
        name="middle_sums",
    )(keep_y, got_y, keep_z, *got_z, small)


def last_sums(own_y, got_y, own_z, got_z, small, lookup, heads):
    block, first = own_y.shape
    rest = own_z.shape[1]
    buckets, count = lookup.shape

    def kernel(own_y, z_1, z_2, z_3, own_z, got_z, small_r, look, out, table, gain_a, gain_f, diag):
        sums = own_y[...]
        for ref in (z_1, z_2, z_3):
            sums = sums + ref[...].astype(f32)
        out[:, 0:first] = sums
        out[:, first:] = own_z[...] + got_z[0:block, :].astype(f32)
        small = small_r[0:12, :] + unpack_small(got_z[block:, :])
        for c in range(3):
            lanes = slice(256 * c, 256 * c + 256)
            gain_a[lanes] = small[4 * c + 2, :]
            gain_f[lanes] = small[4 * c + 3, :]
            for half in range(2):
                for row in range(2):
                    head = 6 * row + 2 * c + half
                    part = small[4 * c + row : 4 * c + row + 1, 128 * half : 128 * half + 128]
                    diag[head : head + 1, :] = part
        table[...] = lax.dot_general(
            diag[...],
            look[...],
            (((1,), (1,)), ((), ())),
            precision=top_precision,
            preferred_element_type=f32,
        )

    return pl.pallas_call(
        kernel,
        out_shape=(
            shape_of(block, first + rest, f32),
            shape_of(heads, buckets, f32),
            jax.ShapeDtypeStruct((first + rest,), f32),
            jax.ShapeDtypeStruct((first + rest,), f32),
        ),
        in_specs=[VMEM] * 8,
        out_specs=(VMEM,) * 4,
        scratch_shapes=[pltpu.VMEM((heads, count), f32)],
        compiler_params=LIMIT,
        cost_estimate=cost(1),
        name="last_sums",
    )(own_y, *got_y, own_z, got_z, small, lookup)


def exchange_plain(chunks):
    return lax.all_to_all(chunks, "expert", split_axis=0, concat_axis=0, tiled=True)


def spread(rows):
    x_rows = swap_x(rows)
    return [rows, swap_core(rows), x_rows, swap_core(x_rows)]


def collect(here, there):
    there = (there[0] + there[1].astype(f32)).astype(bf16)
    return here[0] + here[1].astype(f32), swap_x(there)


def total(here, from_x):
    return (here + from_x.astype(f32)).astype(bf16)


def of_members(rows):
    from_x = swap_x(rows)
    return [rows, from_x, swap_core(rows), swap_core(from_x)]


def by_projection(parts):
    from_x, passed = swap_x(parts[2]), swap_x(parts[3])
    return [parts[0], from_x, swap_core(parts[1]), swap_core(passed)]


def sum_experts(value):
    bits = 1
    while bits < lax.axis_size("expert"):
        value = value + swap(value, "expert", bits)
        bits *= 2
    return value


def reduce_projection(normed, mixed, right, small, lookup, heads):
    experts = lax.axis_size("expert")
    count = normed[0].shape[0]
    if experts != 8:
        small = small[0:4]
        for part in right[1:]:
            small = small + part[count : count + 4].astype(f32)
            small = small + part[count + 4 : count + 8].astype(f32)
        left = jnp.where(
            lax.axis_index("dp") == 3, jnp.concatenate(mixed), jnp.concatenate(normed)
        )
        right = jnp.concatenate([part[:count] for part in right])
        grad = jnp.einsum("td,te->de", left, right, preferred_element_type=f32)
        grad = lax.psum_scatter(grad, "expert", scatter_dimension=0, tiled=True)
        small = sum_experts(small)
        table = lax.dot_general(
            small[0:2].reshape(heads, lookup.shape[1]),
            lookup,
            (((1,), (1,)), ((), ())),
            precision=top_precision,
            preferred_element_type=f32,
        )
        return grad, table, small[2], small[3]
    keep_y, send_y, keep_z, *send_z, small = projection_gradient(normed, mixed, right, small)
    got_z = [swap(send_z[k], "expert", 2 * k + 2) for k in range(3)]
    got_y = swap(send_y, "expert", 1)
    own_y, *send_y, own_z, send_z, small = middle_sums(keep_y, got_y, keep_z, got_z, small)
    got_y = [swap(send_y[k], "expert", 2 * k + 2) for k in range(3)]
    got_z = swap(send_z, "expert", 1)
    return last_sums(own_y, got_y, own_z, got_z, small, lookup, heads)


def shards(
    tokens,
    attn_weights,
    gain_attn,
    gain_ffn,
    rel_table,
    expert_in,
    expert_out,
    gate_weights,
    expert_ids,
    doc_ids,
    cotangent,
):
    seqs, seq_len = doc_ids.shape
    width = tokens.shape[1]
    head_count = rel_table.shape[1]
    head_size = width // head_count
    bucket_count = rel_table.shape[0]
    experts = lax.axis_size("expert")
    token_count = tokens.shape[0]
    block_cap = 3 * seq_len // experts
    capacity = block_cap * seqs
    slots = experts * capacity
    win, wout = expert_in[0], expert_out[0]

    flat_ids = expert_ids.reshape(-1)
    pairs = flat_ids.shape[0]
    earlier = np.tril(np.ones((pairs, pairs), dtype=np.bool_), -1)
    rank = jnp.sum(
        ((flat_ids[:, None] == flat_ids[None, :]) & earlier).astype(jnp.int32), axis=1
    )
    positions = (flat_ids * capacity + rank).reshape(token_count, 2)
    slot_iota = jnp.arange(slots, dtype=jnp.int32)
    first_hit = slot_iota[:, None] == positions[None, :, 0]
    second_hit = slot_iota[:, None] == positions[None, :, 1]
    select = (first_hit | second_hit).astype(bf16)
    first_t = (slot_iota[None, :] == positions[:, 0:1]).astype(bf16)
    second_t = (slot_iota[None, :] == positions[:, 1:2]).astype(bf16)
    select_t = first_t + second_t
    gate_slot = jnp.sum(
        jnp.where(first_hit, gate_weights[None, :, 0], 0.0)
        + jnp.where(second_hit, gate_weights[None, :, 1], 0.0),
        axis=1,
    )

    by_expert = (experts, capacity, width)

    d_buffer = gate_slot[:, None] * jnp.dot(select, cotangent, preferred_element_type=f32)
    d_buffer = d_buffer.astype(bf16).reshape(by_expert)

    distance = (token_count - np.arange(token_count)) % token_count
    lookup = np.eye(bucket_count, dtype=np.float32)[
        bucket_table(seq_len, bucket_count - 1)[np.minimum(distance, seq_len - 1), 0]
    ]
    lookup = jnp.asarray((lookup * (distance < seq_len)[:, None]).T)
    bias_rows = lax.dot_general(
        rel_table,
        lookup,
        (((0,), (0,)), ((), ())),
        precision=top_precision,
        preferred_element_type=f32,
    )
    gains = jnp.stack([gain_attn, gain_ffn])
    docs = doc_ids + 4 * jnp.arange(seqs, dtype=jnp.int32)[:, None]
    docs_row = docs.astype(f32).reshape(1, -1)
    prepared = (bias_rows, gains, docs_row, select)
    pieces, offsets, d_got, prepared = gather_projections(attn_weights, d_buffer, prepared)
    bias_rows, gains, docs_row, select = prepared
    d_all = spread(d_got.reshape(slots, width))
    normed, mixed, qkv, probs, residual, buffer = attention_forward(
        pieces, offsets, tokens, gains, bias_rows, docs_row, select, head_count
    )

    got = exchange_plain(buffer.reshape(by_expert)).reshape(slots, width)
    x_rows, rows = swap_x(got), [got, swap_core(got)]
    hidden_0, d_pre_0, keep_0, send_0 = experts_first(rows, d_all[:2], win, wout)
    result_0, away_0 = experts_result(hidden_0, wout)
    x_rows, send_0, away_0 = lax.optimization_barrier((x_rows, send_0, away_0))
    rows = rows + [x_rows, swap_core(x_rows)]
    core_0, back_0 = swap_core(send_0), swap_core(away_0)
    hidden_1, d_pre_1, keep_1, send_1 = experts_first(rows[2:], d_all[2:], win, wout)
    core_1 = swap_core(send_1)
    hidden_1, d_pre_1, core_1 = lax.optimization_barrier((hidden_1, d_pre_1, core_1))
    d_rows = total(*collect((keep_0, core_0), (keep_1, core_1)))
    d_returned = exchange_plain(d_rows.reshape(by_expert)).reshape(slots, width)
    result_1, away_1 = experts_result(hidden_1, wout)
    back_1 = swap_core(away_1)
    grad_in, grad_out = experts_gradients(
        rows, d_all, (hidden_0, hidden_1), (d_pre_0, d_pre_1)
    )
    here, from_x = collect((result_0, back_0), (result_1, back_1))
    from_x, grad_in, grad_out = lax.optimization_barrier((from_x, grad_in, grad_out))
    result = total(here, from_x)
    d_returned, result, normed, mixed = lax.optimization_barrier(
        (d_returned, result, normed, mixed)
    )
    returned = exchange_plain(result.reshape(by_expert)).reshape(slots, width)
    normed, mixed = of_members(normed), of_members(mixed)

    *grads, grad_tokens, small = attention_backward(
        pieces,
        offsets,
        tokens,
        gains,
        cotangent,
        residual,
        d_returned,
        select_t,
        qkv,
        probs,
        head_count,
    )

    grads, normed, mixed = lax.optimization_barrier((grads, normed, mixed))
    right = by_projection(grads)
    right, returned = lax.optimization_barrier((right, returned))
    output = block_output(returned, residual, first_t, second_t, gate_weights)
    grad_attn, d_table, d_gain_attn, d_gain_ffn = reduce_projection(
        normed, mixed, right, small, lookup, head_count
    )
    return (
        output,
        grad_tokens,
        grad_attn,
        d_gain_attn,
        d_gain_ffn,
        d_table.T,
        grad_in[None],
        grad_out[None],
    )


def solution(mesh):
    placed = (
        P(("dp", "expert"), None),
        P(("dp", "expert"), None),
        P(),
        P(),
        P(),
        P("expert", None, "dp"),
        P("expert", "dp", None),
        P(("dp", "expert"), None),
        P(("dp", "expert"), None),
        P(("dp", "expert"), None),
        P(("dp", "expert"), None),
    )
    return jax.shard_map(
        shards,
        mesh=mesh,
        in_specs=placed,
        out_specs=(
            P(("dp", "expert"), None),
            P(("dp", "expert"), None),
            P(("dp", "expert"), None),
            P(),
            P(),
            P(),
            P("expert", None, "dp"),
            P("expert", "dp", None),
        ),
        check_vma=False,
    )
```

time: 259 us -> 220 us (0.85)
  waiting for transfers between devices: 99.6 us -> 66.7 us
  blocking collectives: 22.3 us -> 0 us
  Pallas kernels: 47.6 us -> 67.4 us
  starting transfers between devices: 55.6 us -> 62.2 us
  other arithmetic: 14.6 us -> 9.14 us
  matrix products: 6.59 us -> 2.58 us
    ppermute x44 -> x49, waiting for transfers between devices: 86 us -> 51.4 us  [swap(): return lax.ppermute(value, axis, [(i, i ^ bits) for i in range(size)])]
    all_to_all x1 -> x0, blocking collectives: 22.3 us -> none  [exchange_plain(): lax.all_to_all(chunks, 'expert', split_axis=0, concat_axis=0, tiled=True)]
    pallas_call x3 -> x10, Pallas kernels: 38.1 us -> 58 us  [the longest x2 14.8 us: experts_first(): pl.pallas_call(kernel, out_shape=(jax.ShapeDtypeStruct((2, count, units),...]
    all_to_all x2 -> x4, starting transfers between devices: 9.04 us -> 22.2 us  [exchange_plain(): lax.all_to_all(chunks, 'expert', split_axis=0, concat_axis=0, tiled=True)]
    ppermute x44 -> x49, starting transfers between devices: 46.5 us -> 40 us  [swap(): return lax.ppermute(value, axis, [(i, i ^ bits) for i in range(size)])]
    unnamed x73 -> x102, local copies, waits for them, and re-layouts: 3.41 us -> 7.1 us
    dot_general x5 -> x1, matrix products: 4.53 us -> 1.45 us  [shards(): lax.dot_general(rel_table, lookup, (((0,), (0,)), ((), ())), precision=to...]
    reshape x3 -> x1, local copies, waits for them, and re-layouts: 3.55 us -> 0.59 us  [shards(): docs_row = docs.astype(f32).reshape(1, -1)]
  transfers between devices with their start and end apart: 46 -> 53, of which waited for: 18 -> 17; matrix products, arithmetic and copies ran while one was open for 11% -> 7% of each run, Pallas kernels for 10% -> 23%
where the time goes in v1:
time: 220 us; the launch traced here: 219 us
  Pallas kernels  67.4 us (31%)
  waiting for transfers between devices  66.7 us (30%)
  starting transfers between devices  62.2 us (28%)
  local copies, waits for them, and re-layouts  10.2 us (5%)
  other arithmetic  9.14 us (4%)
  matrix products  2.58 us (1%)
    ppermute x49, waiting for transfers between devices, swap(): return lax.ppermute(value, axis, [(i, i ^ bits) for i in range(size)])  51.4 us
    ppermute x49, starting transfers between devices, swap(): return lax.ppermute(value, axis, [(i, i ^ bits) for i in range(size)])  40 us
    all_to_all x4, starting transfers between devices, exchange_plain(): lax.all_to_all(chunks, 'expert', split_axis=0, concat_axis=0, tiled=True)  22.2 us
    all_to_all x4, waiting for transfers between devices, exchange_plain(): lax.all_to_all(chunks, 'expert', split_axis=0, concat_axis=0, tiled=True)  15.3 us
    pallas_call x2, Pallas kernels, experts_first(): pl.pallas_call(kernel, out_shape=(jax.ShapeDtypeStruct((2, count, units),...  14.8 us
    pallas_call x1, Pallas kernels, attention_backward(): pl.pallas_call(kernel, out_shape=(jax.ShapeDtypeStruct((count, width), bf...  14 us
    pallas_call x1, Pallas kernels, experts_gradients(): pl.pallas_call(kernel, out_shape=(jax.ShapeDtypeStruct((width, units), f3...  10.7 us
    pallas_call x1, Pallas kernels, attention_forward(): pl.pallas_call(kernel, out_shape=(jax.ShapeDtypeStruct((count, width), bf...  9.42 us
  transfers between devices with their start and end apart: 53, of which 17 were waited for; matrix products, arithmetic and copies ran while one was open for 7% of the time, Pallas kernels for 23%

profile of v1, /device:TPU:0, one launch (start us, length us, event | category | flops | bytes accessed | tf_op | source)
XLA Modules:
  0.0 219.4 jit_solution(15797689067156762671)
XLA Ops:
  0.7 4.1 %collective-permute-start = (bf16[96,768]{1,0:T(8,128)(2,1)}, bf16[96,768]{1,0:T(8,128)(2,1)S(1)}, u32[]{:S(2)}, u32[]{:S(2)}) collective-permute-start(bf16[96,768]{1,0:T(8,128)(2,1)} %param.14), channel_id=1, source_target_pairs={{0,4},{1,5},{2,6},{3,7},{4,0},{5,1},{6,2},{7,3},{8,12},{9,13},{10,... | collective-permute-start | bytes 442376 | tf_op jit(solution)/shard_map/ppermute | solution.py:28
  24.5 3.3 %collective-permute-done.7.refs_3_ = bf16[2,96,768]{2,1,0:T(8,128)(2,1)S(1)} collective-permute-done((bf16[2,96,768]{2,1,0:T(8,128)(2,1)S(1)}, bf16[2,96,768]{2,1,0:T(8,128)(2,1)S(1)}, u32[]{:S(2)}, u32[]{:S(2)}) %collective-permute-start.7) | collective-permute-done | bytes 294944 | tf_op jit(solution)/shard_map/ppermute | solution.py:28
  27.8 5.4 %all-to-all-start.1 = ((bf16[8,48,768]{2,1,0:T(8,128)(2,1)}), bf16[8,48,768]{2,1,0:T(8,128)(2,1)S(1)}, u32[]{:S(2)}, u32[]{:S(2)}) async-start(bf16[8,48,768]{2,1,0:T(8,128)(2,1)} %bitcast.10), calls=%async_computation.1 | async-start | bytes 1179648 | tf_op jit(solution)/shard_map/all_to_all | solution.py:578
  37.4 7.0 %collective-permute-done.11 = bf16[96,768]{1,0:T(8,128)(2,1)S(1)} collective-permute-done((bf16[96,768]{1,0:T(8,128)(2,1)S(1)}, bf16[96,768]{1,0:T(8,128)(2,1)S(1)}, u32[]{:S(2)}, u32[]{:S(2)}) %collective-permute-start.11) | collective-permute-done | bytes 147488 | tf_op jit(solution)/shard_map/ppermute | solution.py:28
  48.3 9.4 %attention_forward.1 = (bf16[128,768]{1,0:T(8,128)(2,1)}, bf16[128,768]{1,0:T(8,128)(2,1)}, bf16[3,128,768]{2,1,0:T(8,128)(2,1)}, f32[12,128,128]{2,1,0:T(8,128)...) custom-call(bf16[3,96,768]{2,1,0:T(8,128)(2,1)} %copy-done.9, bf16[2,96,768]{2,1,0:T(8,128)(2,1)} %copy-done.10, ...), custom_call_target="tpu_custom_call" | custom-call | flops 3000000000 | bytes 9000000 | tf_op jit(solution)/shard_map/attention_forward/pallas_call | solution.py:165
  57.7 6.4 %all-to-all-start = ((bf16[8,48,768]{2,1,0:T(8,128)(2,1)}), bf16[8,48,768]{2,1,0:T(8,128)(2,1)S(1)}, u32[]{:S(2)}, u32[]{:S(2)}) async-start(bf16[8,48,768]{2,1,0:T(8,128)(2,1)} %bitcast.46), calls=%async_computation | async-start | bytes 1179648 | tf_op jit(solution)/shard_map/all_to_all | solution.py:578
  65.1 15.2 %all-to-all-done = bf16[8,48,768]{2,1,0:T(8,128)(2,1)S(1)} async-done(((bf16[8,48,768]{2,1,0:T(8,128)(2,1)}), bf16[8,48,768]{2,1,0:T(8,128)(2,1)S(1)}, u32[]{:S(2)}, u32[]{:S(2)}) %all-to-all-start) | async-done | bytes 589856 | tf_op jit(solution)/shard_map/all_to_all | solution.py:578
  83.2 7.4 %experts_first.2 = (bf16[2,384,768]{2,1,0:T(8,128)(2,1)}, bf16[2,384,768]{2,1,0:T(8,128)(2,1)}, f32[384,768]{1,0:T(8,128)}, bf16[384,768]{1,0:T(8,128)(2,1)}) custom-call(bf16[384,768]{1,0:T(8,128)(2,1)} %bitcast.43, bf16[384,768]{1,0:T(8,128)(2,1)} %copy-done.17, bf16[384,768]{1,0:T(8,128)(2,1)} %bitcast.38, bf16[384,768]{1,0:T(8,128)(2,1)} %copy-done.16, ...), custom_call_target="tpu_custom_call" | custom-call | flops 6000000000 | bytes 18000000 | tf_op jit(solution)/shard_map/experts_first/pallas_call | solution.py:322
  90.6 3.7 %experts_result.2 = (f32[384,768]{1,0:T(8,128)}, bf16[384,768]{1,0:T(8,128)(2,1)}) custom-call(bf16[2,384,768]{2,1,0:T(8,128)(2,1)} %get-tuple-element.112.hidden_r.refs_8_, bf16[768,768]{1,0:T(8,128)(2,1)} %bitcast.59), custom_call_target="tpu_custom_call" | custom-call | flops 2000000000 | bytes 6000000 | tf_op jit(solution)/shard_map/experts_result/pallas_call | solution.py:353
  99.0 7.4 %experts_first.3 = (bf16[2,384,768]{2,1,0:T(8,128)(2,1)}, bf16[2,384,768]{2,1,0:T(8,128)(2,1)}, f32[384,768]{1,0:T(8,128)}, bf16[384,768]{1,0:T(8,128)(2,1)}) custom-call(bf16[384,768]{1,0:T(8,128)(2,1)} %copy-done.19, bf16[384,768]{1,0:T(8,128)(2,1)} %copy-done.20, bf16[384,768]{1,0:T(8,128)(2,1)} %copy-done.15, bf16[384,768]{1,0:T(8,128)(2,1)} %copy-done.18, ...), custom_call_target="tpu_custom_call" | custom-call | flops 6000000000 | bytes 18000000 | tf_op jit(solution)/shard_map/experts_first/pallas_call | solution.py:322
  111.1 3.7 %experts_result.3 = (f32[384,768]{1,0:T(8,128)}, bf16[384,768]{1,0:T(8,128)(2,1)}) custom-call(bf16[2,384,768]{2,1,0:T(8,128)(2,1)} %get-tuple-element.123.hidden_r.refs_9_, bf16[768,768]{1,0:T(8,128)(2,1)} %bitcast.61), custom_call_target="tpu_custom_call" | custom-call | flops 2000000000 | bytes 6000000 | tf_op jit(solution)/shard_map/experts_result/pallas_call | solution.py:353
  115.4 10.2 %collective-permute-done.27 = bf16[384,768]{1,0:T(8,128)(2,1)S(1)} collective-permute-done((bf16[384,768]{1,0:T(8,128)(2,1)S(1)}, bf16[384,768]{1,0:T(8,128)(2,1)S(1)}, u32[]{:S(2)}, u32[]{:S(2)}) %collective-permute-start.27) | collective-permute-done | bytes 589856 | tf_op jit(solution)/shard_map/ppermute | solution.py:28
  126.6 4.7 %all-to-all-start.2 = ((bf16[8,48,768]{2,1,0:T(8,128)(2,1)}), bf16[8,48,768]{2,1,0:T(8,128)(2,1)S(1)}, u32[]{:S(2)}, u32[]{:S(2)}) async-start(bf16[8,48,768]{2,1,0:T(8,128)(2,1)} %bitcast.21), calls=%async_computation.2 | async-start | bytes 1179648 | tf_op jit(solution)/shard_map/all_to_all | solution.py:578
  132.4 10.7 %experts_gradients.1 = (f32[768,768]{1,0:T(8,128)}, f32[768,768]{1,0:T(8,128)}) custom-call(bf16[384,768]{1,0:T(8,128)(2,1)} %bitcast.44, bf16[384,768]{1,0:T(8,128)(2,1)} %copy-done.17, bf16[384,768]{1,0:T(8,128)(2,1)} %copy-done.19, bf16[384,768]{1,0:T(8,128)(2,1)} %copy-done.20, bf16[384,768]{1,0:T(8,128)(2,1)} %bitcast.39, bf16[384,768]{1,0:T(8,128)(2,1)} %copy-done.16, ...), custom_call_target="tpu_custom_call" | custom-call | flops 10000000000 | bytes 30000000 | tf_op jit(solution)/shard_map/experts_gradients/pallas_call | solution.py:384
  143.1 2.7 %collective-permute-done.30 = bf16[384,768]{1,0:T(8,128)(2,1)S(1)} collective-permute-done((bf16[384,768]{1,0:T(8,128)(2,1)S(1)}, bf16[384,768]{1,0:T(8,128)(2,1)S(1)}, u32[]{:S(2)}, u32[]{:S(2)}) %collective-permute-start.30) | collective-permute-done | bytes 589856 | tf_op jit(solution)/shard_map/ppermute | solution.py:28
  150.1 5.7 %all-to-all-start.3 = ((bf16[8,48,768]{2,1,0:T(8,128)(2,1)}), bf16[8,48,768]{2,1,0:T(8,128)(2,1)S(1)}, u32[]{:S(2)}, u32[]{:S(2)}) async-start(bf16[8,48,768]{2,1,0:T(8,128)(2,1)} %bitcast.23), calls=%async_computation.3 | async-start | bytes 1179648 | tf_op jit(solution)/shard_map/all_to_all | solution.py:578
  156.4 14.0 %attention_backward.1 = (bf16[128,768]{1,0:T(8,128)(2,1)}, bf16[144,768]{1,0:T(8,128)(2,1)}, bf16[144,768]{1,0:T(8,128)(2,1)}, bf16[144,768]{1,0:T(8,128)(2,1)}, f32[128,768]{1,0:T(8,128)}, /*index=5*/f32[8,768]{1,0:T(8,128)}) custom-call(bf16[3,96,768]{2,1,0:T(8,128)(2,1)} %copy-done.9, bf16[2,96,768]{2,1,0:T(8,128)(2,1)} %copy-done.10, ...), custom_call_target="tpu_custom_call" | custom-call | flops 12999999488 | bytes 39000000 | tf_op jit(solution)/shard_map/attention_backward/pallas_call | solution.py:260
  172.6 6.5 %collective-permute-done.39 = bf16[144,768]{1,0:T(8,128)(2,1)S(1)} collective-permute-done((bf16[144,768]{1,0:T(8,128)(2,1)}, bf16[144,768]{1,0:T(8,128)(2,1)S(1)}, u32[]{:S(2)}, u32[]{:S(2)}) %collective-permute-start.39) | collective-permute-done | bytes 221216 | tf_op jit(solution)/shard_map/ppermute | solution.py:28
  179.1 3.9 %collective-permute-done.37.refs_9_ = bf16[144,768]{1,0:T(8,128)(2,1)S(1)} collective-permute-done((bf16[144,768]{1,0:T(8,128)(2,1)}, bf16[144,768]{1,0:T(8,128)(2,1)S(1)}, u32[]{:S(2)}, u32[]{:S(2)}) %collective-permute-start.37) | collective-permute-done | bytes 221216 | tf_op jit(solution)/shard_map/ppermute | solution.py:28
  183.8 4.4 %projection_gradient.1 = (f32[384,512]{1,0:T(8,128)}, bf16[384,512]{1,0:T(8,128)(2,1)}, f32[192,256]{1,0:T(8,128)}, bf16[224,256]{1,0:T(8,128)(2,1)}, bf16[224,2...) custom-call(bf16[128,768]{1,0:T(8,128)(2,1)} %get-tuple-element.149.refs_0_, ...), custom_call_target="tpu_custom_call" | custom-call | flops 3000000000 | bytes 9000000 | tf_op jit(solution)/shard_map/projection_gradient/pallas_call | solution.py:471
  191.8 2.4 %collective-permute-start.43 = (bf16[224,256]{1,0:T(8,128)(2,1)}, bf16[224,256]{1,0:T(8,128)(2,1)S(1)}, u32[]{:S(2)}, u32[]{:S(2)}) collective-permute-start(bf16[224,256]{1,0:T(8,128)(2,1)} %get-tuple-element.166), channel_id=1, source_target_pairs={{0,4},{1,5},{2,6},{3,7},{4,0},{5,1},{6,2},{7,3},{8,12},{9,13},{10,... | collective-permute-start | bytes 344072 | tf_op jit(solution)/shard_map/ppermute | solution.py:28
  196.6 6.2 %collective-permute-done.43.z_2 = bf16[224,256]{1,0:T(8,128)(2,1)S(1)} collective-permute-done((bf16[224,256]{1,0:T(8,128)(2,1)}, bf16[224,256]{1,0:T(8,128)(2,1)S(1)}, u32[]{:S(2)}, u32[]{:S(2)}) %collective-permute-start.43) | collective-permute-done | bytes 114720 | tf_op jit(solution)/shard_map/ppermute | solution.py:28
  203.6 2.3 %middle_sums.1 = (f32[96,512]{1,0:T(8,128)}, bf16[96,512]{1,0:T(8,128)(2,1)}, bf16[96,512]{1,0:T(8,128)(2,1)}, bf16[96,512]{1,0:T(8,128)(2,1)}, f32[96,256]{1,0:...) custom-call(f32[384,512]{1,0:T(8,128)} %get-tuple-element.162.keep_y, bf16[384,512]{1,0:T(8,128)(2,1)} %copy-done.23, ...), custom_call_target="tpu_custom_call" | custom-call | flops 1000000000 | bytes 3000000 | tf_op jit(solution)/shard_map/middle_sums/pallas_call | solution.py:513
  210.9 2.3 %block_output.1 = bf16[128,768]{1,0:T(8,128)(2,1)} custom-call(bf16[384,768]{1,0:T(8,128)(2,1)} %bitcast.40, f32[128,768]{1,0:T(8,128)} %get-tuple-element.107.refs_17_.res, bf16[128,384]{1,0:T(8,128)(2,1)} %get-tuple-element.186.first, bf16[128,384]{1,0:T(8,128)(2,1)} %get-tuple-element.187.second, f32[128,2]{1,0:T(8,128)} %copy.36.gate), custom_call_target="tpu_custom_call" | custom-call | flops 3000000000 | bytes 9000000 | tf_op jit(solution)/shard_map/block_output/pallas_call | solution.py:404
  (221 shorter events, 69.1 us)
Async XLA Ops:
  0.7 17.8 %collective-permute-start = (bf16[96,768]{1,0:T(8,128)(2,1)}, bf16[96,768]{1,0:T(8,128)(2,1)S(1)}, u32[]{:S(2)}, u32[]{:S(2)}) collective-permute-start(bf16[96,768]{1,0:T(8,128)(2,1)} %param.14), channel_id=1, source_target_pairs={{0,4},{1,5},{2,6},{3,7},{4,0},{5,1},{6,2},{7,3},{8,12},{9,13},{10,... | collective-permute-start | bytes 442376 | tf_op jit(solution)/shard_map/ppermute | solution.py:28
  4.8 13.7 %collective-permute-start.1 = (bf16[96,768]{1,0:T(8,128)(2,1)}, bf16[96,768]{1,0:T(8,128)(2,1)S(1)}, u32[]{:S(2)}, u32[]{:S(2)}) collective-permute-start(bf16[96,768]{1,0:T(8,128)(2,1)} %param.14), channel_id=1, source_target_pairs={{0,6},{1,7},{2,4},{3,5},{4,2},{5,3},{6,0},{7,1},{8,14},{9,15},{10,... | collective-permute-start | bytes 442376 | tf_op jit(solution)/shard_map/ppermute | solution.py:28
  6.1 12.3 %collective-permute-start.2 = (bf16[96,768]{1,0:T(8,128)(2,1)}, bf16[96,768]{1,0:T(8,128)(2,1)S(1)}, u32[]{:S(2)}, u32[]{:S(2)}) collective-permute-start(bf16[96,768]{1,0:T(8,128)(2,1)} %param.14), channel_id=1, source_target_pairs={{0,2},{1,3},{2,0},{3,1},{4,6},{5,7},{6,4},{7,5},{8,10},{9,11},{10,... | collective-permute-start | bytes 442376 | tf_op jit(solution)/shard_map/ppermute | solution.py:28
  19.3 14.3 %collective-permute-start.5 = (bf16[2,96,768]{2,1,0:T(8,128)(2,1)S(1)}, bf16[2,96,768]{2,1,0:T(8,128)(2,1)S(1)}, u32[]{:S(2)}, u32[]{:S(2)}) collective-permute-start(bf16[2,96,768]{2,1,0:T(8,128)(2,1)S(1)} %pad_maximum_fusion.2.refs_1_), channel_id=1, source_target_pairs={{0,1},{1,0},{2,3},{3,2},{4,5},{5,4},{6,7},{7,6},{8,9},{9,8},{10,11... | collective-permute-start | bytes 884744 | tf_op jit(solution)/shard_map/ppermute | solution.py:28
  19.9 13.4 %collective-permute-start.6 = (bf16[96,768]{1,0:T(8,128)(2,1)S(1)}, bf16[96,768]{1,0:T(8,128)(2,1)S(1)}, u32[]{:S(2)}, u32[]{:S(2)}) collective-permute-start(bf16[96,768]{1,0:T(8,128)(2,1)S(1)} %collective-permute-done.1), channel_id=1, source_target_pairs={{0,16},{8,24},{16,0},{24,8},{1,17},{9,25},{17,1},{25,9},{2,18},{10... | collective-permute-start | bytes 442376 | tf_op jit(solution)/shard_map/ppermute | solution.py:28
  21.3 13.8 %collective-permute-start.9 = (bf16[96,768]{1,0:T(8,128)(2,1)S(1)}, bf16[96,768]{1,0:T(8,128)(2,1)S(1)}, u32[]{:S(2)}, u32[]{:S(2)}) collective-permute-start(bf16[96,768]{1,0:T(8,128)(2,1)S(1)} %collective-permute-done.1), channel_id=1, source_target_pairs={{0,1},{1,0},{2,3},{3,2},{4,5},{5,4},{6,7},{7,6},{8,9},{9,8},{10,11... | collective-permute-start | bytes 442376 | tf_op jit(solution)/shard_map/ppermute | solution.py:28
  22.9 12.3 %collective-permute-start.10 = (bf16[96,768]{1,0:T(8,128)(2,1)S(1)}, bf16[96,768]{1,0:T(8,128)(2,1)S(1)}, u32[]{:S(2)}, u32[]{:S(2)}) collective-permute-start(bf16[96,768]{1,0:T(8,128)(2,1)S(1)} %collective-permute-done.4), channel_id=1, source_target_pairs={{0,1},{1,0},{2,3},{3,2},{4,5},{5,4},{6,7},{7,6},{8,9},{9,8},{10,11... | collective-permute-start | bytes 442376 | tf_op jit(solution)/shard_map/ppermute | solution.py:28
  27.8 29.9 %all-to-all-start.1 = ((bf16[8,48,768]{2,1,0:T(8,128)(2,1)}), bf16[8,48,768]{2,1,0:T(8,128)(2,1)S(1)}, u32[]{:S(2)}, u32[]{:S(2)}) async-start(bf16[8,48,768]{2,1,0:T(8,128)(2,1)} %bitcast.10), calls=%async_computation.1 | async-start | bytes 1179648 | tf_op jit(solution)/shard_map/all_to_all | solution.py:578
  57.7 22.6 %all-to-all-start = ((bf16[8,48,768]{2,1,0:T(8,128)(2,1)}), bf16[8,48,768]{2,1,0:T(8,128)(2,1)S(1)}, u32[]{:S(2)}, u32[]{:S(2)}) async-start(bf16[8,48,768]{2,1,0:T(8,128)(2,1)} %bitcast.46), calls=%async_computation | async-start | bytes 1179648 | tf_op jit(solution)/shard_map/all_to_all | solution.py:578
  64.1 16.2 %collective-permute-start.24 = (bf16[384,768]{1,0:T(8,128)(2,1)S(1)}, bf16[384,768]{1,0:T(8,128)(2,1)S(1)}, u32[]{:S(2)}, u32[]{:S(2)}) collective-permute-start(bf16[384,768]{1,0:T(8,128)(2,1)S(1)} %bitcast.36), channel_id=1, source_target_pairs={{0,16},{8,24},{16,0},{24,8},{1,17},{9,25},{17,1},{25,9},{2,18},{10... | collective-permute-start | bytes 1769480 | tf_op jit(solution)/shard_map/ppermute | solution.py:28
  65.1 16.7 %collective-permute-start.20 = (bf16[384,768]{1,0:T(8,128)(2,1)S(1)}, bf16[384,768]{1,0:T(8,128)(2,1)S(1)}, u32[]{:S(2)}, u32[]{:S(2)}) collective-permute-start(bf16[384,768]{1,0:T(8,128)(2,1)S(1)} %bitcast.37), channel_id=1, source_target_pairs={{0,8},{8,0},{16,24},{24,16},{1,9},{9,1},{17,25},{25,17},{2,10},{10... | collective-permute-start | bytes 1769480 | tf_op jit(solution)/shard_map/ppermute | solution.py:28
  80.3 15.8 %collective-permute-start.25 = (bf16[384,768]{1,0:T(8,128)(2,1)S(1)}, bf16[384,768]{1,0:T(8,128)(2,1)S(1)}, u32[]{:S(2)}, u32[]{:S(2)}) collective-permute-start(bf16[384,768]{1,0:T(8,128)(2,1)S(1)} %collective-permute-done.24.refs_2_.refs_6_), channel_id=1, source_target_pairs={{0,8},{8,0},{16,24},{24,16},{1,9},{9,1},{17,25},{25,17},{2,10},{10... | collective-permute-start | bytes 1769480 | tf_op jit(solution)/shard_map/ppermute | solution.py:28
  80.8 15.3 %collective-permute-start.21 = (bf16[384,768]{1,0:T(8,128)(2,1)S(1)}, bf16[384,768]{1,0:T(8,128)(2,1)S(1)}, u32[]{:S(2)}, u32[]{:S(2)}) collective-permute-start(bf16[384,768]{1,0:T(8,128)(2,1)S(1)} %bitcast.42), channel_id=1, source_target_pairs={{0,16},{8,24},{16,0},{24,8},{1,17},{9,25},{17,1},{25,9},{2,18},{10... | collective-permute-start | bytes 1769480 | tf_op jit(solution)/shard_map/ppermute | solution.py:28
  110.1 15.4 %collective-permute-start.27 = (bf16[384,768]{1,0:T(8,128)(2,1)S(1)}, bf16[384,768]{1,0:T(8,128)(2,1)S(1)}, u32[]{:S(2)}, u32[]{:S(2)}) collective-permute-start(bf16[384,768]{1,0:T(8,128)(2,1)S(1)} %add_convert_fusion.3), channel_id=1, source_target_pairs={{0,16},{8,24},{16,0},{24,8},{1,17},{9,25},{17,1},{25,9},{2,18},{10... | collective-permute-start | bytes 1769480 | tf_op jit(solution)/shard_map/ppermute | solution.py:28
  114.9 16.4 %collective-permute-start.29 = (bf16[384,768]{1,0:T(8,128)(2,1)}, bf16[384,768]{1,0:T(8,128)(2,1)S(1)}, u32[]{:S(2)}, u32[]{:S(2)}) collective-permute-start(bf16[384,768]{1,0:T(8,128)(2,1)} %get-tuple-element.125), channel_id=1, source_target_pairs={{0,8},{8,0},{16,24},{24,16},{1,9},{9,1},{17,25},{25,17},{2,10},{10... | collective-permute-start | bytes 1769480 | tf_op jit(solution)/shard_map/ppermute | solution.py:28
  114.9 30.8 %collective-permute-start.28 = (bf16[384,768]{1,0:T(8,128)(2,1)}, bf16[384,768]{1,0:T(8,128)(2,1)S(1)}, u32[]{:S(2)}, u32[]{:S(2)}) collective-permute-start(bf16[384,768]{1,0:T(8,128)(2,1)} %get-tuple-element.122), channel_id=1, source_target_pairs={{0,8},{8,0},{16,24},{24,16},{1,9},{9,1},{17,25},{25,17},{2,10},{10... | collective-permute-start | bytes 1769480 | tf_op jit(solution)/shard_map/ppermute | solution.py:28
  126.6 20.2 %all-to-all-start.2 = ((bf16[8,48,768]{2,1,0:T(8,128)(2,1)}), bf16[8,48,768]{2,1,0:T(8,128)(2,1)S(1)}, u32[]{:S(2)}, u32[]{:S(2)}) async-start(bf16[8,48,768]{2,1,0:T(8,128)(2,1)} %bitcast.21), calls=%async_computation.2 | async-start | bytes 1179648 | tf_op jit(solution)/shard_map/all_to_all | solution.py:578
  131.4 14.3 %collective-permute-start.30 = (bf16[384,768]{1,0:T(8,128)(2,1)S(1)}, bf16[384,768]{1,0:T(8,128)(2,1)S(1)}, u32[]{:S(2)}, u32[]{:S(2)}) collective-permute-start(bf16[384,768]{1,0:T(8,128)(2,1)S(1)} %add_convert_fusion.1), channel_id=1, source_target_pairs={{0,16},{8,24},{16,0},{24,8},{1,17},{9,25},{17,1},{25,9},{2,18},{10... | collective-permute-start | bytes 1769480 | tf_op jit(solution)/shard_map/ppermute | solution.py:28
  149.6 20.8 %collective-permute-start.32 = (bf16[128,768]{1,0:T(8,128)(2,1)S(1)}, bf16[128,768]{1,0:T(8,128)(2,1)S(1)}, u32[]{:S(2)}, u32[]{:S(2)}) collective-permute-start(bf16[128,768]{1,0:T(8,128)(2,1)S(1)} %copy-done.33), channel_id=1, source_target_pairs={{0,8},{8,0},{16,24},{24,16},{1,9},{9,1},{17,25},{25,17},{2,10},{10... | collective-permute-start | bytes 589832 | tf_op jit(solution)/shard_map/ppermute | solution.py:28
  149.6 20.9 %collective-permute-start.35 = (bf16[128,768]{1,0:T(8,128)(2,1)S(1)}, bf16[128,768]{1,0:T(8,128)(2,1)S(1)}, u32[]{:S(2)}, u32[]{:S(2)}) collective-permute-start(bf16[128,768]{1,0:T(8,128)(2,1)S(1)} %copy-done.34), channel_id=1, source_target_pairs={{0,8},{8,0},{16,24},{24,16},{1,9},{9,1},{17,25},{25,17},{2,10},{10... | collective-permute-start | bytes 589832 | tf_op jit(solution)/shard_map/ppermute | solution.py:28
  150.1 32.9 %all-to-all-start.3 = ((bf16[8,48,768]{2,1,0:T(8,128)(2,1)}), bf16[8,48,768]{2,1,0:T(8,128)(2,1)S(1)}, u32[]{:S(2)}, u32[]{:S(2)}) async-start(bf16[8,48,768]{2,1,0:T(8,128)(2,1)} %bitcast.23), calls=%async_computation.3 | async-start | bytes 1179648 | tf_op jit(solution)/shard_map/all_to_all | solution.py:578
  155.8 14.7 %collective-permute-start.33 = (bf16[128,768]{1,0:T(8,128)(2,1)S(1)}, bf16[128,768]{1,0:T(8,128)(2,1)S(1)}, u32[]{:S(2)}, u32[]{:S(2)}) collective-permute-start(bf16[128,768]{1,0:T(8,128)(2,1)S(1)} %collective-permute-done.31.refs_1_), channel_id=1, source_target_pairs={{0,8},{8,0},{16,24},{24,16},{1,9},{9,1},{17,25},{25,17},{2,10},{10... | collective-permute-start | bytes 589832 | tf_op jit(solution)/shard_map/ppermute | solution.py:28
  155.9 14.6 %collective-permute-start.36 = (bf16[128,768]{1,0:T(8,128)(2,1)S(1)}, bf16[128,768]{1,0:T(8,128)(2,1)S(1)}, u32[]{:S(2)}, u32[]{:S(2)}) collective-permute-start(bf16[128,768]{1,0:T(8,128)(2,1)S(1)} %collective-permute-done.34.refs_5_), channel_id=1, source_target_pairs={{0,8},{8,0},{16,24},{24,16},{1,9},{9,1},{17,25},{25,17},{2,10},{10... | collective-permute-start | bytes 589832 | tf_op jit(solution)/shard_map/ppermute | solution.py:28
  188.3 14.6 %collective-permute-start.41 = (bf16[384,512]{1,0:T(8,128)(2,1)}, bf16[384,512]{1,0:T(8,128)(2,1)S(1)}, u32[]{:S(2)}, u32[]{:S(2)}) collective-permute-start(bf16[384,512]{1,0:T(8,128)(2,1)} %get-tuple-element.163), channel_id=1, source_target_pairs={{0,1},{1,0},{2,3},{3,2},{4,5},{5,4},{6,7},{7,6},{8,9},{9,8},{10,11... | collective-permute-start | bytes 1179656 | tf_op jit(solution)/shard_map/ppermute | solution.py:28
  (79 other events, 561.7 us)

commit v2 on v1

--- a/solution.py
+++ b/solution.py
@@ -91,7 +91,13 @@
 
 VMEM = pl.BlockSpec(memory_space=pltpu.VMEM)
 ANY = pl.BlockSpec(memory_space=pl.ANY)
-LIMIT = pltpu.CompilerParams(vmem_limit_bytes=58 * 1024 * 1024)
+LIMIT = pltpu.CompilerParams(vmem_limit_bytes=56 * 1024 * 1024)
+
+LESS = pltpu.CompilerParams(vmem_limit_bytes=24 * 1024 * 1024)
+
+
+def held(arrays):
+    return [pltpu.with_memory_space_constraint(a, pltpu.VMEM) for a in arrays]
 
 
 def cost(microseconds):
@@ -127,11 +133,11 @@
     def kernel(*refs):
         piece_refs, refs = refs[:n], refs[n:]
         tok, gain, bias, drow, sel = refs[:5]
-        normed_o, mixed_o, qkv_o, probs_o, residual_o, buffer_o, dense, sems = refs[5:]
+        left_o, qkv_o, probs_o, residual_o, buffer_o, dense, sems = refs[5:]
         copies = place_projections(piece_refs, offsets, dense, sems)
         x = tok[...].astype(f32)
         normed = (x * inverse_rms(x) * gain[0:1, :]).astype(bf16)
-        normed_o[...] = normed
+        left_o[0] = normed
         row = lax.broadcasted_iota(jnp.int32, (count, count), 0)
         col = lax.broadcasted_iota(jnp.int32, (count, count), 1)
         docs = jnp.broadcast_to(drow[...], (count, count))
@@ -153,11 +159,11 @@
                 scores = dot_t(jnp.where(mask, q, jnp.zeros_like(q)), k) * 0.125 + shift
                 scores = jnp.where(allowed, scores, -1000000000.0)
                 scores = jnp.exp(scores - jnp.max(scores, axis=-1, keepdims=True))
-                probs = scores / jnp.sum(scores, axis=-1, keepdims=True)
+                probs = scores * (1.0 / jnp.sum(scores, axis=-1, keepdims=True))
                 probs_o[head] = probs
                 out.append(dot(probs.astype(bf16), v))
-            mixed_o[:, lanes] = jnp.where(low_lanes, out[0], out[1]).astype(bf16)
-        residual = x + dot(mixed_o[...], dense[3 * width : 4 * width, :])
+            left_o[1, :, lanes] = jnp.where(low_lanes, out[0], out[1]).astype(bf16)
+        residual = x + dot(left_o[1], dense[3 * width : 4 * width, :])
         residual_o[...] = residual
         moe_in = (residual * inverse_rms(residual) * gain[1:2, :]).astype(bf16)
         buffer_o[...] = dot(sel[...], moe_in).astype(bf16)
@@ -165,15 +171,14 @@
     return pl.pallas_call(
         kernel,
         out_shape=(
-            jax.ShapeDtypeStruct((count, width), bf16),
-            jax.ShapeDtypeStruct((count, width), bf16),
+            jax.ShapeDtypeStruct((2, count, width), bf16),
             jax.ShapeDtypeStruct((3, count, width), bf16),
             jax.ShapeDtypeStruct((heads, count, count), f32),
             jax.ShapeDtypeStruct((count, width), f32),
             jax.ShapeDtypeStruct((slots, width), bf16),
         ),
         in_specs=[ANY] * n + [VMEM] * 5,
-        out_specs=(VMEM,) * 6,
+        out_specs=(VMEM,) * 5,
         scratch_shapes=[
             pltpu.VMEM((4 * width, width), bf16),
             pltpu.SemaphoreType.DMA((blocks,)),
@@ -213,6 +218,8 @@
         d_mixed_s[...] = dot_t(d_attn, dense[3 * width : 4 * width, :]).astype(bf16)
         low_lanes = lax.broadcasted_iota(jnp.int32, (count, 128), 1) < 64
         row = lax.broadcasted_iota(jnp.int32, (count, count), 0)
+        col = lax.broadcasted_iota(jnp.int32, (count, count), 1)
+        reverse = (row + col == count - 1).astype(f32).astype(bf16)
         for pair in range(heads // 2):
             lanes = slice(128 * pair, 128 * pair + 128)
             q, k, v = qkv_r[0, :, lanes], qkv_r[1, :, lanes], qkv_r[2, :, lanes]
@@ -228,11 +235,7 @@
                 d_scores = (probs * (d_probs - inner)).astype(bf16)
                 d_q.append(dot(d_scores, k))
                 d_k.append(t_dot(d_scores, q))
-                turned = d_scores.astype(f32)
-                for bit in (1, 2, 4, 8, 16, 32, 64):
-                    turned = jnp.where(
-                        (row & bit) != 0, pltpu.roll(turned, count - bit, 1), turned
-                    )
+                turned = pltpu.roll(dot(reverse, d_scores), 1, 1, stride=1, stride_axis=0)
                 at, slot = head // 6, 128 * (head % 6)
                 small_o[at : at + 1, slot : slot + 128] = jnp.sum(turned, axis=0, keepdims=True)
             grads_o[d_here ^ 0, :, lanes] = (jnp.where(low_lanes, d_q[0], d_q[1]) * 0.125).astype(bf16)
@@ -295,25 +298,15 @@
 
     def kernel(*refs):
         row_refs, d_refs, (win_r, wout_r) = refs[0:2], refs[2:4], refs[4:6]
-        hidden_o, d_pre_o, keep_o, send_o, row_s, d_s, win_s, wout_s, sems = refs[6:]
-        sources = (d_refs[1], wout_r, row_refs[1], win_r, d_refs[0], row_refs[0])
-        targets = (d_s.at[1], wout_s, row_s.at[1], win_s, d_s.at[0], row_s.at[0])
-        copies = [
-            pltpu.make_async_copy(source, target, sems.at[n])
-            for n, (source, target) in enumerate(zip(sources, targets))
-        ]
-        for copy in copies:
-            copy.start()
+        hidden_o, d_pre_o, keep_o, send_o = refs[6:]
         for i in (1, 0):
-            for copy in copies[0:4] if i else copies[4:6]:
-                copy.wait()
-            d_hidden = dot_t(d_s[i], wout_s[...])
-            pre = dot(row_s[i], win_s[...])
+            d_hidden = dot_t(d_refs[i][...], wout_r[...])
+            pre = dot(row_refs[i][...], win_r[...])
             hidden, slope = gelu_parts(pre)
             hidden_o[i] = hidden.astype(bf16)
             d_pre = (d_hidden * slope).astype(bf16)
             d_pre_o[i] = d_pre
-            d_slot = dot_t(d_pre, win_s[...])
+            d_slot = dot_t(d_pre, win_r[...])
             if i == 1:
                 send_o[...] = d_slot.astype(bf16)
             else:
@@ -327,19 +320,12 @@
             jax.ShapeDtypeStruct((count, width), f32),
             jax.ShapeDtypeStruct((count, width), bf16),
         ),
-        in_specs=[ANY] * 6,
+        in_specs=[VMEM] * 6,
         out_specs=(VMEM,) * 4,
-        scratch_shapes=[
-            pltpu.VMEM((2, count, width), bf16),
-            pltpu.VMEM((2, count, width), bf16),
-            pltpu.VMEM(win.shape, bf16),
-            pltpu.VMEM(wout.shape, bf16),
-            pltpu.SemaphoreType.DMA((6,)),
-        ],
-        compiler_params=LIMIT,
+        compiler_params=LESS,
         cost_estimate=cost(6),
         name="experts_first",
-    )(*rows, *d_rows, win, wout)
+    )(*held([*rows, *d_rows, win, wout]))
 
 
 def experts_result(hidden, wout):
@@ -358,10 +344,10 @@
         ),
         in_specs=[VMEM] * 2,
         out_specs=(VMEM,) * 2,
-        compiler_params=LIMIT,
+        compiler_params=LESS,
         cost_estimate=cost(2),
         name="experts_result",
-    )(hidden, wout)
+    )(*held([hidden, wout]))
 
 
 def experts_gradients(rows, d_rows, hidden, d_pre):
@@ -428,22 +414,23 @@
     return jax.ShapeDtypeStruct((rows, width), dtype)
 
 
-def projection_gradient(normed, mixed, right, small):
-    count, width = normed[0].shape
+def projection_gradient(left, right, small):
+    _, count, width = left[0].shape
     block, first = width // 8, 2 * width // 3
 
     def kernel(*refs):
-        normed_r, mixed_r, right_r, small_r = refs[0:4], refs[4:8], refs[8:12], refs[12]
-        keep_y, send_y, keep_z = refs[13:16]
-        send_z, small_o, total, packed = refs[16:19], refs[19], refs[20], refs[21]
+        left_r, right_r, small_r = refs[0:4], refs[4:8], refs[8]
+        keep_y, send_y, keep_z = refs[9:12]
+        send_z, small_o, total, packed = refs[12:15], refs[15], refs[16], refs[17]
+        left_s, right_s = refs[18:20]
         e_here = lax.axis_index("expert")
-        last = lax.axis_index("dp") == 3
+        which = lax.div(lax.axis_index("dp"), 3)
         y_here, z_here = lax.rem(e_here, 2), lax.div(e_here, 2)
-        acc = None
         for i in range(4):
-            left = jnp.where(last, mixed_r[i][...], normed_r[i][...])
-            term = t_dot(left, right_r[i][0:count, :])
-            acc = term if acc is None else acc + term
+            rows = slice(i * count, (i + 1) * count)
+            left_s[rows, :] = left_r[i][which]
+            right_s[rows, :] = right_r[i][0:count, :]
+        acc = t_dot(left_s[...], right_s[...])
         for i in range(8):
             total[i] = acc[i * block : (i + 1) * block]
         for k in range(4):
@@ -477,13 +464,14 @@
         )
         + (shape_of(2 * block + 32, width - first, bf16),) * 3
         + (shape_of(16, 256, f32),),
-        in_specs=[VMEM] * 13,
+        in_specs=[VMEM] * 9,
         out_specs=(VMEM,) * 7,
-        scratch_shapes=[pltpu.VMEM((8, block, width), f32), pltpu.VMEM((32, 256), f32)],
-        compiler_params=LIMIT,
+        scratch_shapes=[pltpu.VMEM((8, block, width), f32), pltpu.VMEM((32, 256), f32)]
+        + [pltpu.VMEM((4 * count, width), bf16)] * 2,
+        compiler_params=LESS,
         cost_estimate=cost(3),
         name="projection_gradient",
-    )(*normed, *mixed, *right, small)
+    )(*held([*left, *right, small]))
 
 
 def middle_sums(keep_y, got_y, keep_z, got_z, small):
@@ -522,10 +510,10 @@
         in_specs=[VMEM] * 7,
         out_specs=(VMEM,) * 7,
         scratch_shapes=[pltpu.VMEM((32, 256), f32)],
-        compiler_params=LIMIT,
+        compiler_params=LESS,
         cost_estimate=cost(1),
         name="middle_sums",
-    )(keep_y, got_y, keep_z, *got_z, small)
+    )(*held([keep_y, got_y, keep_z, *got_z, small]))
 
 
 def last_sums(own_y, got_y, own_z, got_z, small, lookup, heads):
@@ -568,10 +556,10 @@
         in_specs=[VMEM] * 8,
         out_specs=(VMEM,) * 4,
         scratch_shapes=[pltpu.VMEM((heads, count), f32)],
-        compiler_params=LIMIT,
+        compiler_params=LESS,
         cost_estimate=cost(1),
         name="last_sums",
-    )(own_y, *got_y, own_z, got_z, small, lookup)
+    )(*held([own_y, *got_y, own_z, got_z, small, lookup]))
 
 
 def exchange_plain(chunks):
@@ -590,11 +578,6 @@
 
 def total(here, from_x):
     return (here + from_x.astype(f32)).astype(bf16)
-
-
-def of_members(rows):
-    from_x = swap_x(rows)
-    return [rows, from_x, swap_core(rows), swap_core(from_x)]
 
 
 def by_projection(parts):
@@ -610,17 +593,16 @@
     return value
 
 
-def reduce_projection(normed, mixed, right, small, lookup, heads):
+def reduce_projection(left, right, small, lookup, heads):
     experts = lax.axis_size("expert")
-    count = normed[0].shape[0]
+    count = left[0].shape[1]
     if experts != 8:
         small = small[0:4]
         for part in right[1:]:
             small = small + part[count : count + 4].astype(f32)
             small = small + part[count + 4 : count + 8].astype(f32)
-        left = jnp.where(
-            lax.axis_index("dp") == 3, jnp.concatenate(mixed), jnp.concatenate(normed)
-        )
+        left = jnp.concatenate(left, axis=1)
+        left = jnp.where(lax.axis_index("dp") == 3, left[1], left[0])
         right = jnp.concatenate([part[:count] for part in right])
         grad = jnp.einsum("td,te->de", left, right, preferred_element_type=f32)
         grad = lax.psum_scatter(grad, "expert", scatter_dimension=0, tiled=True)
@@ -633,7 +615,7 @@
             preferred_element_type=f32,
         )
         return grad, table, small[2], small[3]
-    keep_y, send_y, keep_z, *send_z, small = projection_gradient(normed, mixed, right, small)
+    keep_y, send_y, keep_z, *send_z, small = projection_gradient(left, right, small)
     got_z = [swap(send_z[k], "expert", 2 * k + 2) for k in range(3)]
     got_y = swap(send_y, "expert", 1)
     own_y, *send_y, own_z, send_z, small = middle_sums(keep_y, got_y, keep_z, got_z, small)
@@ -711,7 +693,7 @@
     pieces, offsets, d_got, prepared = gather_projections(attn_weights, d_buffer, prepared)
     bias_rows, gains, docs_row, select = prepared
     d_all = spread(d_got.reshape(slots, width))
-    normed, mixed, qkv, probs, residual, buffer = attention_forward(
+    left, qkv, probs, residual, buffer = attention_forward(
         pieces, offsets, tokens, gains, bias_rows, docs_row, select, head_count
     )
 
@@ -725,21 +707,23 @@
     hidden_1, d_pre_1, keep_1, send_1 = experts_first(rows[2:], d_all[2:], win, wout)
     core_1 = swap_core(send_1)
     hidden_1, d_pre_1, core_1 = lax.optimization_barrier((hidden_1, d_pre_1, core_1))
-    d_rows = total(*collect((keep_0, core_0), (keep_1, core_1)))
-    d_returned = exchange_plain(d_rows.reshape(by_expert)).reshape(slots, width)
+    here, from_x = collect((keep_0, core_0), (keep_1, core_1))
+    prepared = (first_t, second_t, select_t)
+    from_x, prepared = lax.optimization_barrier((from_x, prepared))
+    first_t, second_t, select_t = prepared
+    d_rows = total(here, from_x)
     result_1, away_1 = experts_result(hidden_1, wout)
     back_1 = swap_core(away_1)
+    d_returned = exchange_plain(d_rows.reshape(by_expert)).reshape(slots, width)
     grad_in, grad_out = experts_gradients(
         rows, d_all, (hidden_0, hidden_1), (d_pre_0, d_pre_1)
     )
     here, from_x = collect((result_0, back_0), (result_1, back_1))
     from_x, grad_in, grad_out = lax.optimization_barrier((from_x, grad_in, grad_out))
     result = total(here, from_x)
-    d_returned, result, normed, mixed = lax.optimization_barrier(
-        (d_returned, result, normed, mixed)
-    )
+    d_returned, result, left = lax.optimization_barrier((d_returned, result, left))
     returned = exchange_plain(result.reshape(by_expert)).reshape(slots, width)
-    normed, mixed = of_members(normed), of_members(mixed)
+    left_x = swap_x(left)
 
     *grads, grad_tokens, small = attention_backward(
         pieces,
@@ -755,12 +739,13 @@
         head_count,
     )
 
-    grads, normed, mixed = lax.optimization_barrier((grads, normed, mixed))
+    grads, left_x = lax.optimization_barrier((grads, left_x))
+    left = [left, left_x, swap_core(left), swap_core(left_x)]
     right = by_projection(grads)
     right, returned = lax.optimization_barrier((right, returned))
     output = block_output(returned, residual, first_t, second_t, gate_weights)
     grad_attn, d_table, d_gain_attn, d_gain_ffn = reduce_projection(
-        normed, mixed, right, small, lookup, head_count
+        left, right, small, lookup, head_count
     )
     return (
         output,

time: 220 us -> 204 us (0.927)
  Pallas kernels: 67.4 us -> 47.4 us
  waiting for transfers between devices: 66.7 us -> 70.5 us
    pallas_call x2, Pallas kernels: 7.44 us -> 2.15 us  [experts_result(): pl.pallas_call(kernel, out_shape=(jax.ShapeDtypeStruct((count, width), f3...]
    pallas_call x2, Pallas kernels: 14.8 us -> 10.3 us  [experts_first(): pl.pallas_call(kernel, out_shape=(jax.ShapeDtypeStruct((2, count, units),...]
    ppermute x49 -> x46, waiting for transfers between devices: 51.4 us -> 55.3 us  [swap(): return lax.ppermute(value, axis, [(i, i ^ bits) for i in range(size)])]
    pallas_call x1, Pallas kernels: 4.44 us -> 1 us  [projection_gradient(): pl.pallas_call(kernel, out_shape=(shape_of(4 * block, first, f32), shape_...]
    pallas_call x1, Pallas kernels: 14 us -> 10.6 us  [attention_backward(): pl.pallas_call(kernel, out_shape=(jax.ShapeDtypeStruct((count, width), bf...]
    ppermute x49 -> x46, starting transfers between devices: 40 us -> 38.5 us  [swap(): return lax.ppermute(value, axis, [(i, i ^ bits) for i in range(size)])]
    unnamed x102 -> x72, local copies, waits for them, and re-layouts: 7.1 us -> 7.18 us
  transfers between devices with their start and end apart: 53 -> 50, of which waited for: 17 -> 17; matrix products, arithmetic and copies ran while one was open for 7% -> 9% of each run, Pallas kernels for 23% -> 20%
where the time goes in v2:
time: 204 us; the launch traced here: 203 us
  waiting for transfers between devices  70.5 us (35%)
  starting transfers between devices  60.7 us (30%)
  Pallas kernels  47.4 us (23%)
  local copies, waits for them, and re-layouts  10.2 us (5%)
  other arithmetic  10.1 us (5%)
  matrix products  2.58 us (1%)
    ppermute x46, waiting for transfers between devices, swap(): return lax.ppermute(value, axis, [(i, i ^ bits) for i in range(size)])  55.3 us
    ppermute x46, starting transfers between devices, swap(): return lax.ppermute(value, axis, [(i, i ^ bits) for i in range(size)])  38.5 us
    all_to_all x4, starting transfers between devices, exchange_plain(): lax.all_to_all(chunks, 'expert', split_axis=0, concat_axis=0, tiled=True)  22.3 us
    all_to_all x4, waiting for transfers between devices, exchange_plain(): lax.all_to_all(chunks, 'expert', split_axis=0, concat_axis=0, tiled=True)  15.2 us
    pallas_call x1, Pallas kernels, attention_backward(): pl.pallas_call(kernel, out_shape=(jax.ShapeDtypeStruct((count, width), bf...  10.6 us
    pallas_call x1, Pallas kernels, experts_gradients(): pl.pallas_call(kernel, out_shape=(jax.ShapeDtypeStruct((width, units), f3...  10.6 us
    pallas_call x2, Pallas kernels, experts_first(): pl.pallas_call(kernel, out_shape=(jax.ShapeDtypeStruct((2, count, units),...  10.3 us
    pallas_call x1, Pallas kernels, attention_forward(): pl.pallas_call(kernel, out_shape=(jax.ShapeDtypeStruct((2, count, width),...  9.52 us
  transfers between devices with their start and end apart: 50, of which 17 were waited for; matrix products, arithmetic and copies ran while one was open for 9% of the time, Pallas kernels for 20%

profile of v2, /device:TPU:0, one launch (start us, length us, event | category | flops | bytes accessed | tf_op | source)
XLA Modules:
  0.0 202.8 jit_solution(2069521730783849572)
XLA Ops:
  0.7 4.1 %collective-permute-start = (bf16[96,768]{1,0:T(8,128)(2,1)}, bf16[96,768]{1,0:T(8,128)(2,1)S(1)}, u32[]{:S(2)}, u32[]{:S(2)}) collective-permute-start(bf16[96,768]{1,0:T(8,128)(2,1)} %param.14), channel_id=1, source_target_pairs={{0,4},{1,5},{2,6},{3,7},{4,0},{5,1},{6,2},{7,3},{8,12},{9,13},{10,... | collective-permute-start | bytes 442376 | tf_op jit(solution)/shard_map/ppermute | solution.py:28
  24.5 3.3 %collective-permute-done.7.refs_3_ = bf16[2,96,768]{2,1,0:T(8,128)(2,1)S(1)} collective-permute-done((bf16[2,96,768]{2,1,0:T(8,128)(2,1)S(1)}, bf16[2,96,768]{2,1,0:T(8,128)(2,1)S(1)}, u32[]{:S(2)}, u32[]{:S(2)}) %collective-permute-start.7) | collective-permute-done | bytes 294944 | tf_op jit(solution)/shard_map/ppermute | solution.py:28
  27.8 5.4 %all-to-all-start.1 = ((bf16[8,48,768]{2,1,0:T(8,128)(2,1)}), bf16[8,48,768]{2,1,0:T(8,128)(2,1)S(1)}, u32[]{:S(2)}, u32[]{:S(2)}) async-start(bf16[8,48,768]{2,1,0:T(8,128)(2,1)} %bitcast.10), calls=%async_computation.1 | async-start | bytes 1179648 | tf_op jit(solution)/shard_map/all_to_all | solution.py:566
  35.3 2.0 collective-permute-start.11
  37.4 7.0 %collective-permute-done.11 = bf16[96,768]{1,0:T(8,128)(2,1)S(1)} collective-permute-done((bf16[96,768]{1,0:T(8,128)(2,1)S(1)}, bf16[96,768]{1,0:T(8,128)(2,1)S(1)}, u32[]{:S(2)}, u32[]{:S(2)}) %collective-permute-start.11) | collective-permute-done | bytes 147488 | tf_op jit(solution)/shard_map/ppermute | solution.py:28
  48.2 9.5 %attention_forward.1 = (bf16[2,128,768]{2,1,0:T(8,128)(2,1)}, bf16[3,128,768]{2,1,0:T(8,128)(2,1)}, f32[12,128,128]{2,1,0:T(8,128)}, f32[128,768]{1,0:T(8,128)}, bf16[384,768]{1,0:T(8,128)(2,1)}) custom-call(bf16[3,96,768]{2,1,0:T(8,128)(2,1)} %copy-done.21, bf16[2,96,768]{2,1,0:T(8,128)(2,1)} %copy-done.22, ...), custom_call_target="tpu_custom_call" | custom-call | flops 3000000000 | bytes 9000000 | tf_op jit(solution)/shard_map/attention_forward/pallas_call | solution.py:171
  57.8 6.5 %all-to-all-start = ((bf16[8,48,768]{2,1,0:T(8,128)(2,1)}), bf16[8,48,768]{2,1,0:T(8,128)(2,1)S(1)}, u32[]{:S(2)}, u32[]{:S(2)}) async-start(bf16[8,48,768]{2,1,0:T(8,128)(2,1)} %bitcast.51), calls=%async_computation | async-start | bytes 1179648 | tf_op jit(solution)/shard_map/all_to_all | solution.py:566
  65.3 15.2 %all-to-all-done = bf16[8,48,768]{2,1,0:T(8,128)(2,1)S(1)} async-done(((bf16[8,48,768]{2,1,0:T(8,128)(2,1)}), bf16[8,48,768]{2,1,0:T(8,128)(2,1)S(1)}, u32[]{:S(2)}, u32[]{:S(2)}) %all-to-all-start) | async-done | bytes 589856 | tf_op jit(solution)/shard_map/all_to_all | solution.py:566
  82.6 5.2 %experts_first.2 = (bf16[2,384,768]{2,1,0:T(8,128)(2,1)S(1)}, bf16[2,384,768]{2,1,0:T(8,128)(2,1)S(1)}, f32[384,768]{1,0:T(8,128)S(1)}, bf16[384,768]{1,0:T(8,128)(2,1)S(1)}) custom-call(bf16[384,768]{1,0:T(8,128)(2,1)S(1)} %bitcast.42, bf16[384,768]{1,0:T(8,128)(2,1)S(1)} %collective-permute-done.19.refs_1_, bf16[384,768]{1,0:T(8,128)(2,1)S(1)} %bitcast.38, ...), custom_call_target="tpu_custom_call" | custom-call | flops 6000000000 | bytes 18000000 | tf_op jit(solution)/shard_map/experts_first/pallas_call | solution.py:315
  89.3 7.0 %collective-permute-done.21.refs_0_.refs_2_ = bf16[384,768]{1,0:T(8,128)(2,1)S(1)} collective-permute-done((bf16[384,768]{1,0:T(8,128)(2,1)S(1)}, bf16[384,768]{1,0:T(8,128)(2,1)S(1)}, u32[]{:S(2)}, u32[]{:S(2)}) %collective-permute-start.21) | collective-permute-done | bytes 589856 | tf_op jit(solution)/shard_map/ppermute | solution.py:28
  98.4 5.1 %experts_first.3 = (bf16[2,384,768]{2,1,0:T(8,128)(2,1)S(1)}, bf16[2,384,768]{2,1,0:T(8,128)(2,1)S(1)}, f32[384,768]{1,0:T(8,128)S(1)}, bf16[384,768]{1,0:T(8,128)(2,1)S(1)}) custom-call(bf16[384,768]{1,0:T(8,128)(2,1)S(1)} %collective-permute-done.21.refs_0_.refs_2_, bf16[384,768]{1,0:T(8,128)(2,1)S(1)} %collective-permute-done.23.refs_1_.refs_3_, ...), custom_call_target="tpu_custom_call" | custom-call | flops 6000000000 | bytes 18000000 | tf_op jit(solution)/shard_map/experts_first/pallas_call | solution.py:315
  110.0 11.2 %collective-permute-done.27 = bf16[384,768]{1,0:T(8,128)(2,1)S(1)} collective-permute-done((bf16[384,768]{1,0:T(8,128)(2,1)S(1)}, bf16[384,768]{1,0:T(8,128)(2,1)S(1)}, u32[]{:S(2)}, u32[]{:S(2)}) %collective-permute-start.27) | collective-permute-done | bytes 589856 | tf_op jit(solution)/shard_map/ppermute | solution.py:28
  122.2 4.6 %all-to-all-start.2 = ((bf16[8,48,768]{2,1,0:T(8,128)(2,1)}), bf16[8,48,768]{2,1,0:T(8,128)(2,1)}, u32[]{:S(2)}, u32[]{:S(2)}) async-start(bf16[8,48,768]{2,1,0:T(8,128)(2,1)} %bitcast.50), calls=%async_computation.2 | async-start | bytes 1179648 | tf_op jit(solution)/shard_map/all_to_all | solution.py:566
  129.1 10.6 %experts_gradients.1 = (f32[768,768]{1,0:T(8,128)}, f32[768,768]{1,0:T(8,128)}) custom-call(bf16[384,768]{1,0:T(8,128)(2,1)} %bitcast.43, bf16[384,768]{1,0:T(8,128)(2,1)} %copy-done.7, bf16[384,768]{1,0:T(8,128)(2,1)} %copy-done.9, bf16[384,768]{1,0:T(8,128)(2,1)} %copy-done.10, bf16[384,768]{1,0:T(8,128)(2,1)} %bitcast.39, ...), custom_call_target="tpu_custom_call" | custom-call | flops 10000000000 | bytes 30000000 | tf_op jit(solution)/shard_map/experts_gradients/pallas_call | solution.py:370
  139.7 2.8 %collective-permute-done.30 = bf16[384,768]{1,0:T(8,128)(2,1)S(1)} collective-permute-done((bf16[384,768]{1,0:T(8,128)(2,1)S(1)}, bf16[384,768]{1,0:T(8,128)(2,1)S(1)}, u32[]{:S(2)}, u32[]{:S(2)}) %collective-permute-start.30) | collective-permute-done | bytes 589856 | tf_op jit(solution)/shard_map/ppermute | solution.py:28
  142.5 2.2 %add_convert_fusion = bf16[384,768]{1,0:T(8,128)(2,1)} fusion(bf16[384,768]{1,0:T(8,128)(2,1)S(1)} %collective-permute-done.30, f32[384,768]{1,0:T(8,128)S(1)} %get-tuple-element.117, bf16[384,768]{1,0:T(8,128)(2,1)} %collective-permute-done.28), kind=kLoop, calls=%fused_computation.2 | loop fusion | flops 1474560 | bytes 2949120 | tf_op jit(solution)/shard_map/convert_element_type | solution.py:580
  145.6 5.6 %all-to-all-start.3 = ((bf16[8,48,768]{2,1,0:T(8,128)(2,1)}), bf16[8,48,768]{2,1,0:T(8,128)(2,1)}, u32[]{:S(2)}, u32[]{:S(2)}) async-start(bf16[8,48,768]{2,1,0:T(8,128)(2,1)} %bitcast.23), calls=%async_computation.3 | async-start | bytes 1179648 | tf_op jit(solution)/shard_map/all_to_all | solution.py:566
  151.3 10.6 %attention_backward.1 = (bf16[128,768]{1,0:T(8,128)(2,1)}, bf16[144,768]{1,0:T(8,128)(2,1)}, bf16[144,768]{1,0:T(8,128)(2,1)}, bf16[144,768]{1,0:T(8,128)(2,1)}, f32[128,768]{1,0:T(8,128)}, /*index=5*/f32[8,768]{1,0:T(8,128)}) custom-call(bf16[3,96,768]{2,1,0:T(8,128)(2,1)} %copy-done.21, bf16[2,96,768]{2,1,0:T(8,128)(2,1)} %copy-done.22, ...), custom_call_target="tpu_custom_call" | custom-call | flops 12999999488 | bytes 39000000 | tf_op jit(solution)/shard_map/attention_backward/pallas_call | solution.py:263
  164.5 5.4 %collective-permute-done.34 = bf16[144,768]{1,0:T(8,128)(2,1)S(1)} collective-permute-done((bf16[144,768]{1,0:T(8,128)(2,1)}, bf16[144,768]{1,0:T(8,128)(2,1)S(1)}, u32[]{:S(2)}, u32[]{:S(2)}) %collective-permute-start.34) | collective-permute-done | bytes 221216 | tf_op jit(solution)/shard_map/ppermute | solution.py:28
  169.9 2.9 %collective-permute-done.32.refs_5_ = bf16[144,768]{1,0:T(8,128)(2,1)S(1)} collective-permute-done((bf16[144,768]{1,0:T(8,128)(2,1)}, bf16[144,768]{1,0:T(8,128)(2,1)S(1)}, u32[]{:S(2)}, u32[]{:S(2)}) %collective-permute-start.32) | collective-permute-done | bytes 221216 | tf_op jit(solution)/shard_map/ppermute | solution.py:28
  176.5 2.0 collective-permute-start.38
  179.9 2.4 %collective-permute-start.40 = (bf16[224,256]{1,0:T(8,128)(2,1)S(1)}, bf16[224,256]{1,0:T(8,128)(2,1)S(1)}, u32[]{:S(2)}, u32[]{:S(2)}) collective-permute-start(bf16[224,256]{1,0:T(8,128)(2,1)S(1)} %get-tuple-element.156), channel_id=1, source_target_pairs={{0,4},{1,5},{2,6},{3,7},{4,0},{5,1},{6,2},{7,3},{8,12},{9,13},{10,... | collective-permute-start | bytes 344072 | tf_op jit(solution)/shard_map/ppermute | solution.py:28
  183.8 6.3 %collective-permute-done.40.z_2 = bf16[224,256]{1,0:T(8,128)(2,1)S(1)} collective-permute-done((bf16[224,256]{1,0:T(8,128)(2,1)S(1)}, bf16[224,256]{1,0:T(8,128)(2,1)S(1)}, u32[]{:S(2)}, u32[]{:S(2)}) %collective-permute-start.40) | collective-permute-done | bytes 114720 | tf_op jit(solution)/shard_map/ppermute | solution.py:28
  196.4 2.3 %block_output.1 = bf16[128,768]{1,0:T(8,128)(2,1)} custom-call(bf16[384,768]{1,0:T(8,128)(2,1)} %bitcast.24.held, f32[128,768]{1,0:T(8,128)} %get-tuple-element.102.refs_17_.res, bf16[128,384]{1,0:T(8,128)(2,1)} %get-tuple-element.143.first, bf16[128,384]{1,0:T(8,128)(2,1)} %get-tuple-element.144.second, f32[128,2]{1,0:T(8,128)} %copy.36.gate), custom_call_target="tpu_custom_call" | custom-call | flops 3000000000 | bytes 9000000 | tf_op jit(solution)/shard_map/block_output/pallas_call | solution.py:390
  (185 shorter events, 62.1 us)
Async XLA Ops:
  0.7 17.8 %collective-permute-start = (bf16[96,768]{1,0:T(8,128)(2,1)}, bf16[96,768]{1,0:T(8,128)(2,1)S(1)}, u32[]{:S(2)}, u32[]{:S(2)}) collective-permute-start(bf16[96,768]{1,0:T(8,128)(2,1)} %param.14), channel_id=1, source_target_pairs={{0,4},{1,5},{2,6},{3,7},{4,0},{5,1},{6,2},{7,3},{8,12},{9,13},{10,... | collective-permute-start | bytes 442376 | tf_op jit(solution)/shard_map/ppermute | solution.py:28
  4.8 13.7 %collective-permute-start.1 = (bf16[96,768]{1,0:T(8,128)(2,1)}, bf16[96,768]{1,0:T(8,128)(2,1)S(1)}, u32[]{:S(2)}, u32[]{:S(2)}) collective-permute-start(bf16[96,768]{1,0:T(8,128)(2,1)} %param.14), channel_id=1, source_target_pairs={{0,6},{1,7},{2,4},{3,5},{4,2},{5,3},{6,0},{7,1},{8,14},{9,15},{10,... | collective-permute-start | bytes 442376 | tf_op jit(solution)/shard_map/ppermute | solution.py:28
  6.1 12.3 %collective-permute-start.2 = (bf16[96,768]{1,0:T(8,128)(2,1)}, bf16[96,768]{1,0:T(8,128)(2,1)S(1)}, u32[]{:S(2)}, u32[]{:S(2)}) collective-permute-start(bf16[96,768]{1,0:T(8,128)(2,1)} %param.14), channel_id=1, source_target_pairs={{0,2},{1,3},{2,0},{3,1},{4,6},{5,7},{6,4},{7,5},{8,10},{9,11},{10,... | collective-permute-start | bytes 442376 | tf_op jit(solution)/shard_map/ppermute | solution.py:28
  6.3 12.1 %collective-permute-start.3 = (bf16[96,768]{1,0:T(8,128)(2,1)}, bf16[96,768]{1,0:T(8,128)(2,1)S(1)}, u32[]{:S(2)}, u32[]{:S(2)}) collective-permute-start(bf16[96,768]{1,0:T(8,128)(2,1)} %param.14), channel_id=1, source_target_pairs={{0,1},{1,0},{2,3},{3,2},{4,5},{5,4},{6,7},{7,6},{8,9},{9,8},{10,11... | collective-permute-start | bytes 442376 | tf_op jit(solution)/shard_map/ppermute | solution.py:28
  19.3 14.3 %collective-permute-start.5 = (bf16[2,96,768]{2,1,0:T(8,128)(2,1)S(1)}, bf16[2,96,768]{2,1,0:T(8,128)(2,1)}, u32[]{:S(2)}, u32[]{:S(2)}) collective-permute-start(bf16[2,96,768]{2,1,0:T(8,128)(2,1)S(1)} %pad_maximum_fusion.2.refs_1_), channel_id=1, source_target_pairs={{0,1},{1,0},{2,3},{3,2},{4,5},{5,4},{6,7},{7,6},{8,9},{9,8},{10,11... | collective-permute-start | bytes 884744 | tf_op jit(solution)/shard_map/ppermute | solution.py:28
  19.9 13.4 %collective-permute-start.6 = (bf16[96,768]{1,0:T(8,128)(2,1)S(1)}, bf16[96,768]{1,0:T(8,128)(2,1)S(1)}, u32[]{:S(2)}, u32[]{:S(2)}) collective-permute-start(bf16[96,768]{1,0:T(8,128)(2,1)S(1)} %collective-permute-done.1), channel_id=1, source_target_pairs={{0,16},{8,24},{16,0},{24,8},{1,17},{9,25},{17,1},{25,9},{2,18},{10... | collective-permute-start | bytes 442376 | tf_op jit(solution)/shard_map/ppermute | solution.py:28
  21.3 13.8 %collective-permute-start.9 = (bf16[96,768]{1,0:T(8,128)(2,1)S(1)}, bf16[96,768]{1,0:T(8,128)(2,1)S(1)}, u32[]{:S(2)}, u32[]{:S(2)}) collective-permute-start(bf16[96,768]{1,0:T(8,128)(2,1)S(1)} %collective-permute-done.1), channel_id=1, source_target_pairs={{0,1},{1,0},{2,3},{3,2},{4,5},{5,4},{6,7},{7,6},{8,9},{9,8},{10,11... | collective-permute-start | bytes 442376 | tf_op jit(solution)/shard_map/ppermute | solution.py:28
  22.9 12.3 %collective-permute-start.10 = (bf16[96,768]{1,0:T(8,128)(2,1)S(1)}, bf16[96,768]{1,0:T(8,128)(2,1)S(1)}, u32[]{:S(2)}, u32[]{:S(2)}) collective-permute-start(bf16[96,768]{1,0:T(8,128)(2,1)S(1)} %collective-permute-done.4), channel_id=1, source_target_pairs={{0,1},{1,0},{2,3},{3,2},{4,5},{5,4},{6,7},{7,6},{8,9},{9,8},{10,11... | collective-permute-start | bytes 442376 | tf_op jit(solution)/shard_map/ppermute | solution.py:28
  27.8 30.0 %all-to-all-start.1 = ((bf16[8,48,768]{2,1,0:T(8,128)(2,1)}), bf16[8,48,768]{2,1,0:T(8,128)(2,1)S(1)}, u32[]{:S(2)}, u32[]{:S(2)}) async-start(bf16[8,48,768]{2,1,0:T(8,128)(2,1)} %bitcast.10), calls=%async_computation.1 | async-start | bytes 1179648 | tf_op jit(solution)/shard_map/all_to_all | solution.py:566
  33.3 11.6 %collective-permute-start.12 = (bf16[3,96,768]{2,1,0:T(8,128)(2,1)S(1)}, bf16[3,96,768]{2,1,0:T(8,128)(2,1)S(1)}, u32[]{:S(2)}, u32[]{:S(2)}) collective-permute-start(bf16[3,96,768]{2,1,0:T(8,128)(2,1)S(1)} %pad_maximum_fusion.1.refs_0_), channel_id=1, source_target_pairs={{0,8},{8,0},{16,24},{24,16},{1,9},{9,1},{17,25},{25,17},{2,10},{10... | collective-permute-start | bytes 1327112 | tf_op jit(solution)/shard_map/ppermute | solution.py:28
  57.8 22.7 %all-to-all-start = ((bf16[8,48,768]{2,1,0:T(8,128)(2,1)}), bf16[8,48,768]{2,1,0:T(8,128)(2,1)S(1)}, u32[]{:S(2)}, u32[]{:S(2)}) async-start(bf16[8,48,768]{2,1,0:T(8,128)(2,1)} %bitcast.51), calls=%async_computation | async-start | bytes 1179648 | tf_op jit(solution)/shard_map/all_to_all | solution.py:566
  64.3 16.2 %collective-permute-start.24 = (bf16[384,768]{1,0:T(8,128)(2,1)S(1)}, bf16[384,768]{1,0:T(8,128)(2,1)}, u32[]{:S(2)}, u32[]{:S(2)}) collective-permute-start(bf16[384,768]{1,0:T(8,128)(2,1)S(1)} %bitcast.36), channel_id=1, source_target_pairs={{0,16},{8,24},{16,0},{24,8},{1,17},{9,25},{17,1},{25,9},{2,18},{10... | collective-permute-start | bytes 1769480 | tf_op jit(solution)/shard_map/ppermute | solution.py:28
  65.3 16.7 %collective-permute-start.20 = (bf16[384,768]{1,0:T(8,128)(2,1)S(1)}, bf16[384,768]{1,0:T(8,128)(2,1)}, u32[]{:S(2)}, u32[]{:S(2)}) collective-permute-start(bf16[384,768]{1,0:T(8,128)(2,1)S(1)} %bitcast.37), channel_id=1, source_target_pairs={{0,8},{8,0},{16,24},{24,16},{1,9},{9,1},{17,25},{25,17},{2,10},{10... | collective-permute-start | bytes 1769480 | tf_op jit(solution)/shard_map/ppermute | solution.py:28
  80.5 15.8 %collective-permute-start.25 = (bf16[384,768]{1,0:T(8,128)(2,1)}, bf16[384,768]{1,0:T(8,128)(2,1)S(1)}, u32[]{:S(2)}, u32[]{:S(2)}) collective-permute-start(bf16[384,768]{1,0:T(8,128)(2,1)} %collective-permute-done.24.refs_2_.refs_6_), channel_id=1, source_target_pairs={{0,8},{8,0},{16,24},{24,16},{1,9},{9,1},{17,25},{25,17},{2,10},{10... | collective-permute-start | bytes 1769480 | tf_op jit(solution)/shard_map/ppermute | solution.py:28
  81.0 15.3 %collective-permute-start.21 = (bf16[384,768]{1,0:T(8,128)(2,1)S(1)}, bf16[384,768]{1,0:T(8,128)(2,1)S(1)}, u32[]{:S(2)}, u32[]{:S(2)}) collective-permute-start(bf16[384,768]{1,0:T(8,128)(2,1)S(1)} %bitcast.41), channel_id=1, source_target_pairs={{0,16},{8,24},{16,0},{24,8},{1,17},{9,25},{17,1},{25,9},{2,18},{10... | collective-permute-start | bytes 1769480 | tf_op jit(solution)/shard_map/ppermute | solution.py:28
  103.7 17.4 %collective-permute-start.22 = (bf16[384,768]{1,0:T(8,128)(2,1)S(1)}, bf16[384,768]{1,0:T(8,128)(2,1)S(1)}, u32[]{:S(2)}, u32[]{:S(2)}) collective-permute-start(bf16[384,768]{1,0:T(8,128)(2,1)S(1)} %get-tuple-element.109), channel_id=1, source_target_pairs={{0,8},{8,0},{16,24},{24,16},{1,9},{9,1},{17,25},{25,17},{2,10},{10... | collective-permute-start | bytes 1769480 | tf_op jit(solution)/shard_map/ppermute | solution.py:28
  105.8 15.4 %collective-permute-start.27 = (bf16[384,768]{1,0:T(8,128)(2,1)S(1)}, bf16[384,768]{1,0:T(8,128)(2,1)S(1)}, u32[]{:S(2)}, u32[]{:S(2)}) collective-permute-start(bf16[384,768]{1,0:T(8,128)(2,1)S(1)} %add_convert_fusion.3), channel_id=1, source_target_pairs={{0,16},{8,24},{16,0},{24,8},{1,17},{9,25},{17,1},{25,9},{2,18},{10... | collective-permute-start | bytes 1769480 | tf_op jit(solution)/shard_map/ppermute | solution.py:28
  107.9 19.0 %collective-permute-start.29 = (bf16[384,768]{1,0:T(8,128)(2,1)S(1)}, bf16[384,768]{1,0:T(8,128)(2,1)}, u32[]{:S(2)}, u32[]{:S(2)}) collective-permute-start(bf16[384,768]{1,0:T(8,128)(2,1)S(1)} %get-tuple-element.121), channel_id=1, source_target_pairs={{0,8},{8,0},{16,24},{24,16},{1,9},{9,1},{17,25},{25,17},{2,10},{10... | collective-permute-start | bytes 1769480 | tf_op jit(solution)/shard_map/ppermute | solution.py:28
  109.5 33.0 %collective-permute-start.28 = (bf16[384,768]{1,0:T(8,128)(2,1)S(1)}, bf16[384,768]{1,0:T(8,128)(2,1)}, u32[]{:S(2)}, u32[]{:S(2)}) collective-permute-start(bf16[384,768]{1,0:T(8,128)(2,1)S(1)} %get-tuple-element.118), channel_id=1, source_target_pairs={{0,8},{8,0},{16,24},{24,16},{1,9},{9,1},{17,25},{25,17},{2,10},{10... | collective-permute-start | bytes 1769480 | tf_op jit(solution)/shard_map/ppermute | solution.py:28
  122.2 22.4 %all-to-all-start.2 = ((bf16[8,48,768]{2,1,0:T(8,128)(2,1)}), bf16[8,48,768]{2,1,0:T(8,128)(2,1)}, u32[]{:S(2)}, u32[]{:S(2)}) async-start(bf16[8,48,768]{2,1,0:T(8,128)(2,1)} %bitcast.50), calls=%async_computation.2 | async-start | bytes 1179648 | tf_op jit(solution)/shard_map/all_to_all | solution.py:566
  128.1 14.4 %collective-permute-start.30 = (bf16[384,768]{1,0:T(8,128)(2,1)S(1)}, bf16[384,768]{1,0:T(8,128)(2,1)S(1)}, u32[]{:S(2)}, u32[]{:S(2)}) collective-permute-start(bf16[384,768]{1,0:T(8,128)(2,1)S(1)} %add_convert_fusion.1), channel_id=1, source_target_pairs={{0,16},{8,24},{16,0},{24,8},{1,17},{9,25},{17,1},{25,9},{2,18},{10... | collective-permute-start | bytes 1769480 | tf_op jit(solution)/shard_map/ppermute | solution.py:28
  144.7 17.2 %collective-permute-start.31 = (bf16[2,128,768]{2,1,0:T(8,128)(2,1)S(1)}, bf16[2,128,768]{2,1,0:T(8,128)(2,1)S(1)}, u32[]{:S(2)}, u32[]{:S(2)}) collective-permute-start(bf16[2,128,768]{2,1,0:T(8,128)(2,1)S(1)} %copy-done.11), channel_id=1, source_target_pairs={{0,16},{8,24},{16,0},{24,8},{1,17},{9,25},{17,1},{25,9},{2,18},{10... | collective-permute-start | bytes 1179656 | tf_op jit(solution)/shard_map/ppermute | solution.py:28
  145.6 27.3 %all-to-all-start.3 = ((bf16[8,48,768]{2,1,0:T(8,128)(2,1)}), bf16[8,48,768]{2,1,0:T(8,128)(2,1)}, u32[]{:S(2)}, u32[]{:S(2)}) async-start(bf16[8,48,768]{2,1,0:T(8,128)(2,1)} %bitcast.23), calls=%async_computation.3 | async-start | bytes 1179648 | tf_op jit(solution)/shard_map/all_to_all | solution.py:566
  176.5 13.7 %collective-permute-start.38 = (bf16[384,512]{1,0:T(8,128)(2,1)S(1)}, bf16[384,512]{1,0:T(8,128)(2,1)S(1)}, u32[]{:S(2)}, u32[]{:S(2)}) collective-permute-start(bf16[384,512]{1,0:T(8,128)(2,1)S(1)} %get-tuple-element.153), channel_id=1, source_target_pairs={{0,1},{1,0},{2,3},{3,2},{4,5},{5,4},{6,7},{7,6},{8,9},{9,8},{10,11... | collective-permute-start | bytes 1179656 | tf_op jit(solution)/shard_map/ppermute | solution.py:28
  (61 other events, 451.9 us)

commit v3 on v2

--- a/solution.py
+++ b/solution.py
@@ -334,12 +334,12 @@
 
     def kernel(hidden_r, wout_r, keep_o, send_o):
         send_o[...] = dot(hidden_r[1], wout_r[...]).astype(bf16)
-        keep_o[...] = dot(hidden_r[0], wout_r[...])
+        keep_o[...] = dot(hidden_r[0], wout_r[...]).astype(bf16)
 
     return pl.pallas_call(
         kernel,
         out_shape=(
-            jax.ShapeDtypeStruct((count, width), f32),
+            jax.ShapeDtypeStruct((count, width), bf16),
             jax.ShapeDtypeStruct((count, width), bf16),
         ),
         in_specs=[VMEM] * 2,
@@ -572,8 +572,8 @@
 
 
 def collect(here, there):
-    there = (there[0] + there[1].astype(f32)).astype(bf16)
-    return here[0] + here[1].astype(f32), swap_x(there)
+    there = (there[0].astype(f32) + there[1].astype(f32)).astype(bf16)
+    return here[0].astype(f32) + here[1].astype(f32), swap_x(there)
 
 
 def total(here, from_x):
@@ -701,7 +701,8 @@
     x_rows, rows = swap_x(got), [got, swap_core(got)]
     hidden_0, d_pre_0, keep_0, send_0 = experts_first(rows, d_all[:2], win, wout)
     result_0, away_0 = experts_result(hidden_0, wout)
-    x_rows, send_0, away_0 = lax.optimization_barrier((x_rows, send_0, away_0))
+    x_rows, send_0, away_0, left = lax.optimization_barrier((x_rows, send_0, away_0, left))
+    left_x = swap_x(left)
     rows = rows + [x_rows, swap_core(x_rows)]
     core_0, back_0 = swap_core(send_0), swap_core(away_0)
     hidden_1, d_pre_1, keep_1, send_1 = experts_first(rows[2:], d_all[2:], win, wout)
@@ -723,7 +724,6 @@
     result = total(here, from_x)
     d_returned, result, left = lax.optimization_barrier((d_returned, result, left))
     returned = exchange_plain(result.reshape(by_expert)).reshape(slots, width)
-    left_x = swap_x(left)
 
     *grads, grad_tokens, small = attention_backward(
         pieces,

time: 204 us -> 201 us (0.985)
  Pallas kernels: 47.4 us -> 45.2 us
    pallas_call x2, Pallas kernels: 10.3 us -> 7.71 us  [experts_first(): pl.pallas_call(kernel, out_shape=(jax.ShapeDtypeStruct((2, count, units),...]
    unnamed x72 -> x80, local copies, waits for them, and re-layouts: 7.18 us -> 9.14 us
  transfers between devices with their start and end apart: 50 -> 50, of which waited for: 17 -> 17; matrix products, arithmetic and copies ran while one was open for 9% -> 8% of each run, Pallas kernels for 20% -> 20%
where the time goes in v3:
time: 201 us; the launch traced here: 200 us
  waiting for transfers between devices  70.4 us (35%)
  starting transfers between devices  59.7 us (30%)
  Pallas kernels  45.2 us (22%)
  local copies, waits for them, and re-layouts  12.2 us (6%)
  other arithmetic  9.01 us (4%)
  matrix products  2.58 us (1%)
    ppermute x46, waiting for transfers between devices, swap(): return lax.ppermute(value, axis, [(i, i ^ bits) for i in range(size)])  55.1 us
    ppermute x46, starting transfers between devices, swap(): return lax.ppermute(value, axis, [(i, i ^ bits) for i in range(size)])  38.6 us
    all_to_all x4, starting transfers between devices, exchange_plain(): lax.all_to_all(chunks, 'expert', split_axis=0, concat_axis=0, tiled=True)  21.2 us
    all_to_all x4, waiting for transfers between devices, exchange_plain(): lax.all_to_all(chunks, 'expert', split_axis=0, concat_axis=0, tiled=True)  15.3 us
    pallas_call x1, Pallas kernels, attention_backward(): pl.pallas_call(kernel, out_shape=(jax.ShapeDtypeStruct((count, width), bf...  10.6 us
    pallas_call x1, Pallas kernels, experts_gradients(): pl.pallas_call(kernel, out_shape=(jax.ShapeDtypeStruct((width, units), f3...  10.6 us
    pallas_call x1, Pallas kernels, attention_forward(): pl.pallas_call(kernel, out_shape=(jax.ShapeDtypeStruct((2, count, width),...  9.42 us
    unnamed x80, local copies, waits for them, and re-layouts  9.14 us
  transfers between devices with their start and end apart: 50, of which 17 were waited for; matrix products, arithmetic and copies ran while one was open for 8% of the time, Pallas kernels for 20%

profile of v3, /device:TPU:0, one launch (start us, length us, event | category | flops | bytes accessed | tf_op | source)
XLA Modules:
  0.0 200.4 jit_solution(10416541199375715665)
XLA Ops:
  0.7 4.1 %collective-permute-start = (bf16[96,768]{1,0:T(8,128)(2,1)}, bf16[96,768]{1,0:T(8,128)(2,1)S(1)}, u32[]{:S(2)}, u32[]{:S(2)}) collective-permute-start(bf16[96,768]{1,0:T(8,128)(2,1)} %param.14), channel_id=1, source_target_pairs={{0,4},{1,5},{2,6},{3,7},{4,0},{5,1},{6,2},{7,3},{8,12},{9,13},{10,... | collective-permute-start | bytes 442376 | tf_op jit(solution)/shard_map/ppermute | solution.py:28
  24.5 3.3 %collective-permute-done.7.refs_3_ = bf16[2,96,768]{2,1,0:T(8,128)(2,1)S(1)} collective-permute-done((bf16[2,96,768]{2,1,0:T(8,128)(2,1)S(1)}, bf16[2,96,768]{2,1,0:T(8,128)(2,1)S(1)}, u32[]{:S(2)}, u32[]{:S(2)}) %collective-permute-start.7) | collective-permute-done | bytes 294944 | tf_op jit(solution)/shard_map/ppermute | solution.py:28
  27.8 5.4 %all-to-all-start.1 = ((bf16[8,48,768]{2,1,0:T(8,128)(2,1)}), bf16[8,48,768]{2,1,0:T(8,128)(2,1)S(1)}, u32[]{:S(2)}, u32[]{:S(2)}) async-start(bf16[8,48,768]{2,1,0:T(8,128)(2,1)} %bitcast.10), calls=%async_computation.1 | async-start | bytes 1179648 | tf_op jit(solution)/shard_map/all_to_all | solution.py:566
  35.3 2.0 %collective-permute-start.11 = (bf16[96,768]{1,0:T(8,128)(2,1)S(1)}, bf16[96,768]{1,0:T(8,128)(2,1)S(1)}, u32[]{:S(2)}, u32[]{:S(2)}) collective-permute-start(bf16[96,768]{1,0:T(8,128)(2,1)S(1)} %collective-permute-done.6), channel_id=1, source_target_pairs={{0,1},{1,0},{2,3},{3,2},{4,5},{5,4},{6,7},{7,6},{8,9},{9,8},{10,11... | collective-permute-start | bytes 442376 | tf_op jit(solution)/shard_map/ppermute | solution.py:28
  37.4 7.0 %collective-permute-done.11 = bf16[96,768]{1,0:T(8,128)(2,1)S(1)} collective-permute-done((bf16[96,768]{1,0:T(8,128)(2,1)S(1)}, bf16[96,768]{1,0:T(8,128)(2,1)S(1)}, u32[]{:S(2)}, u32[]{:S(2)}) %collective-permute-start.11) | collective-permute-done | bytes 147488 | tf_op jit(solution)/shard_map/ppermute | solution.py:28
  48.2 9.4 %attention_forward.1 = (bf16[2,128,768]{2,1,0:T(8,128)(2,1)}, bf16[3,128,768]{2,1,0:T(8,128)(2,1)}, f32[12,128,128]{2,1,0:T(8,128)}, f32[128,768]{1,0:T(8,128)}, bf16[384,768]{1,0:T(8,128)(2,1)}) custom-call(bf16[3,96,768]{2,1,0:T(8,128)(2,1)} %copy-done.24, bf16[2,96,768]{2,1,0:T(8,128)(2,1)} %copy-done.25, bf16[2,96,768]{2,1,0:T(8,128)(2,1)} %copy-done.32, ...), custom_call_target="tpu_custom_call" | custom-call | flops 3000000000 | bytes 9000000 | tf_op jit(solution)/shard_map/attention_forward/pallas_call | solution.py:171
  57.7 6.5 %all-to-all-start = ((bf16[8,48,768]{2,1,0:T(8,128)(2,1)}), bf16[8,48,768]{2,1,0:T(8,128)(2,1)S(1)}, u32[]{:S(2)}, u32[]{:S(2)}) async-start(bf16[8,48,768]{2,1,0:T(8,128)(2,1)} %bitcast.51), calls=%async_computation | async-start | bytes 1179648 | tf_op jit(solution)/shard_map/all_to_all | solution.py:566
  65.2 15.2 %all-to-all-done = bf16[8,48,768]{2,1,0:T(8,128)(2,1)S(1)} async-done(((bf16[8,48,768]{2,1,0:T(8,128)(2,1)}), bf16[8,48,768]{2,1,0:T(8,128)(2,1)S(1)}, u32[]{:S(2)}, u32[]{:S(2)}) %all-to-all-start) | async-done | bytes 589856 | tf_op jit(solution)/shard_map/all_to_all | solution.py:566
  83.9 3.9 %experts_first.2 = (bf16[2,384,768]{2,1,0:T(8,128)(2,1)S(1)}, bf16[2,384,768]{2,1,0:T(8,128)(2,1)S(1)}, f32[384,768]{1,0:T(8,128)S(1)}, bf16[384,768]{1,0:T(8,128)(2,1)S(1)}) custom-call(bf16[384,768]{1,0:T(8,128)(2,1)S(1)} %bitcast.42, bf16[384,768]{1,0:T(8,128)(2,1)S(1)} %collective-permute-done.19.refs_1_, bf16[384,768]{1,0:T(8,128)(2,1)S(1)} %bitcast.38, ...), custom_call_target="tpu_custom_call" | custom-call | flops 6000000000 | bytes 18000000 | tf_op jit(solution)/shard_map/experts_first/pallas_call | solution.py:315
  89.5 6.8 %collective-permute-done.21.refs_0_.refs_2_ = bf16[384,768]{1,0:T(8,128)(2,1)S(1)} collective-permute-done((bf16[384,768]{1,0:T(8,128)(2,1)S(1)}, bf16[384,768]{1,0:T(8,128)(2,1)S(1)}, u32[]{:S(2)}, u32[]{:S(2)}) %collective-permute-start.21) | collective-permute-done | bytes 589856 | tf_op jit(solution)/shard_map/ppermute | solution.py:28
  98.3 3.9 %experts_first.3 = (bf16[2,384,768]{2,1,0:T(8,128)(2,1)S(1)}, bf16[2,384,768]{2,1,0:T(8,128)(2,1)S(1)}, f32[384,768]{1,0:T(8,128)S(1)}, bf16[384,768]{1,0:T(8,128)(2,1)S(1)}) custom-call(bf16[384,768]{1,0:T(8,128)(2,1)S(1)} %collective-permute-done.21.refs_0_.refs_2_, bf16[384,768]{1,0:T(8,128)(2,1)S(1)} %collective-permute-done.23.refs_1_.refs_3_, ...), custom_call_target="tpu_custom_call" | custom-call | flops 6000000000 | bytes 18000000 | tf_op jit(solution)/shard_map/experts_first/pallas_call | solution.py:315
  109.7 10.9 %collective-permute-done.27 = bf16[384,768]{1,0:T(8,128)(2,1)S(1)} collective-permute-done((bf16[384,768]{1,0:T(8,128)(2,1)S(1)}, bf16[384,768]{1,0:T(8,128)(2,1)S(1)}, u32[]{:S(2)}, u32[]{:S(2)}) %collective-permute-start.27) | collective-permute-done | bytes 589856 | tf_op jit(solution)/shard_map/ppermute | solution.py:28
  121.7 4.5 %all-to-all-start.2 = ((bf16[8,48,768]{2,1,0:T(8,128)(2,1)}), bf16[8,48,768]{2,1,0:T(8,128)(2,1)}, u32[]{:S(2)}, u32[]{:S(2)}) async-start(bf16[8,48,768]{2,1,0:T(8,128)(2,1)} %bitcast.21), calls=%async_computation.2 | async-start | bytes 1179648 | tf_op jit(solution)/shard_map/all_to_all | solution.py:566
  127.4 10.6 %experts_gradients.1 = (f32[768,768]{1,0:T(8,128)}, f32[768,768]{1,0:T(8,128)}) custom-call(bf16[384,768]{1,0:T(8,128)(2,1)} %bitcast.43, bf16[384,768]{1,0:T(8,128)(2,1)} %copy-done.9, bf16[384,768]{1,0:T(8,128)(2,1)} %copy-done.11, bf16[384,768]{1,0:T(8,128)(2,1)} %copy-done.12, bf16[384,768]{1,0:T(8,128)(2,1)} %bitcast.39, bf16[384,768]{1,0:T(8,128)(2,1)} %copy-done.8, ...), custom_call_target="tpu_custom_call" | custom-call | flops 10000000000 | bytes 30000000 | tf_op jit(solution)/shard_map/experts_gradients/pallas_call | solution.py:370
  138.0 3.0 %collective-permute-done.30 = bf16[384,768]{1,0:T(8,128)(2,1)S(1)} collective-permute-done((bf16[384,768]{1,0:T(8,128)(2,1)S(1)}, bf16[384,768]{1,0:T(8,128)(2,1)S(1)}, u32[]{:S(2)}, u32[]{:S(2)}) %collective-permute-start.30) | collective-permute-done | bytes 589856 | tf_op jit(solution)/shard_map/ppermute | solution.py:28
  140.9 2.1 %add_convert_fusion = bf16[384,768]{1,0:T(8,128)(2,1)} fusion(bf16[384,768]{1,0:T(8,128)(2,1)S(1)} %collective-permute-done.30, bf16[384,768]{1,0:T(8,128)(2,1)} %collective-permute-done.28, bf16[384,768]{1,0:T(8,128)(2,1)S(1)} %get-tuple-element.119), kind=kLoop, calls=%fused_computation.2 | loop fusion | flops 1769472 | bytes 2359296 | tf_op jit(solution)/shard_map/convert_element_type | solution.py:580
  143.0 4.7 %all-to-all-start.3 = ((bf16[8,48,768]{2,1,0:T(8,128)(2,1)}), bf16[8,48,768]{2,1,0:T(8,128)(2,1)S(1)}, u32[]{:S(2)}, u32[]{:S(2)}) async-start(bf16[8,48,768]{2,1,0:T(8,128)(2,1)} %bitcast.23), calls=%async_computation.3 | async-start | bytes 1179648 | tf_op jit(solution)/shard_map/all_to_all | solution.py:566
  147.7 10.6 %attention_backward.1 = (bf16[128,768]{1,0:T(8,128)(2,1)}, bf16[144,768]{1,0:T(8,128)(2,1)}, bf16[144,768]{1,0:T(8,128)(2,1)}, bf16[144,768]{1,0:T(8,128)(2,1)}, f32[128,768]{1,0:T(8,128)}, /*index=5*/f32[8,768]{1,0:T(8,128)}) custom-call(bf16[3,96,768]{2,1,0:T(8,128)(2,1)} %copy-done.24, bf16[2,96,768]{2,1,0:T(8,128)(2,1)} %copy-done.25, ...), custom_call_target="tpu_custom_call" | custom-call | flops 12999999488 | bytes 39000000 | tf_op jit(solution)/shard_map/attention_backward/pallas_call | solution.py:263
  161.0 5.6 %collective-permute-done.34 = bf16[144,768]{1,0:T(8,128)(2,1)S(1)} collective-permute-done((bf16[144,768]{1,0:T(8,128)(2,1)}, bf16[144,768]{1,0:T(8,128)(2,1)S(1)}, u32[]{:S(2)}, u32[]{:S(2)}) %collective-permute-start.34) | collective-permute-done | bytes 221216 | tf_op jit(solution)/shard_map/ppermute | solution.py:28
  166.5 2.8 %collective-permute-done.32.refs_5_ = bf16[144,768]{1,0:T(8,128)(2,1)S(1)} collective-permute-done((bf16[144,768]{1,0:T(8,128)(2,1)}, bf16[144,768]{1,0:T(8,128)(2,1)S(1)}, u32[]{:S(2)}, u32[]{:S(2)}) %collective-permute-start.32) | collective-permute-done | bytes 221216 | tf_op jit(solution)/shard_map/ppermute | solution.py:28
  173.7 2.0 %collective-permute-start.38 = (bf16[384,512]{1,0:T(8,128)(2,1)S(1)}, bf16[384,512]{1,0:T(8,128)(2,1)S(1)}, u32[]{:S(2)}, u32[]{:S(2)}) collective-permute-start(bf16[384,512]{1,0:T(8,128)(2,1)S(1)} %get-tuple-element.155), channel_id=1, source_target_pairs={{0,1},{1,0},{2,3},{3,2},{4,5},{5,4},{6,7},{7,6},{8,9},{9,8},{10,11... | collective-permute-start | bytes 1179656 | tf_op jit(solution)/shard_map/ppermute | solution.py:28
  177.2 2.4 %collective-permute-start.40 = (bf16[224,256]{1,0:T(8,128)(2,1)S(1)}, bf16[224,256]{1,0:T(8,128)(2,1)S(1)}, u32[]{:S(2)}, u32[]{:S(2)}) collective-permute-start(bf16[224,256]{1,0:T(8,128)(2,1)S(1)} %get-tuple-element.158), channel_id=1, source_target_pairs={{0,4},{1,5},{2,6},{3,7},{4,0},{5,1},{6,2},{7,3},{8,12},{9,13},{10,... | collective-permute-start | bytes 344072 | tf_op jit(solution)/shard_map/ppermute | solution.py:28
  181.2 6.3 %collective-permute-done.40.z_2 = bf16[224,256]{1,0:T(8,128)(2,1)S(1)} collective-permute-done((bf16[224,256]{1,0:T(8,128)(2,1)S(1)}, bf16[224,256]{1,0:T(8,128)(2,1)S(1)}, u32[]{:S(2)}, u32[]{:S(2)}) %collective-permute-start.40) | collective-permute-done | bytes 114720 | tf_op jit(solution)/shard_map/ppermute | solution.py:28
  193.9 2.3 %block_output.1 = bf16[128,768]{1,0:T(8,128)(2,1)} custom-call(bf16[384,768]{1,0:T(8,128)(2,1)} %bitcast.50, f32[128,768]{1,0:T(8,128)} %get-tuple-element.103.refs_17_.res, bf16[128,384]{1,0:T(8,128)(2,1)} %get-tuple-element.144.first, bf16[128,384]{1,0:T(8,128)(2,1)} %get-tuple-element.145.second, f32[128,2]{1,0:T(8,128)} %copy.36.gate), custom_call_target="tpu_custom_call" | custom-call | flops 3000000000 | bytes 9000000 | tf_op jit(solution)/shard_map/block_output/pallas_call | solution.py:390
  (193 shorter events, 63.8 us)
Async XLA Ops:
  0.7 17.8 %collective-permute-start = (bf16[96,768]{1,0:T(8,128)(2,1)}, bf16[96,768]{1,0:T(8,128)(2,1)S(1)}, u32[]{:S(2)}, u32[]{:S(2)}) collective-permute-start(bf16[96,768]{1,0:T(8,128)(2,1)} %param.14), channel_id=1, source_target_pairs={{0,4},{1,5},{2,6},{3,7},{4,0},{5,1},{6,2},{7,3},{8,12},{9,13},{10,... | collective-permute-start | bytes 442376 | tf_op jit(solution)/shard_map/ppermute | solution.py:28
  4.8 13.7 %collective-permute-start.1 = (bf16[96,768]{1,0:T(8,128)(2,1)}, bf16[96,768]{1,0:T(8,128)(2,1)S(1)}, u32[]{:S(2)}, u32[]{:S(2)}) collective-permute-start(bf16[96,768]{1,0:T(8,128)(2,1)} %param.14), channel_id=1, source_target_pairs={{0,6},{1,7},{2,4},{3,5},{4,2},{5,3},{6,0},{7,1},{8,14},{9,15},{10,... | collective-permute-start | bytes 442376 | tf_op jit(solution)/shard_map/ppermute | solution.py:28
  6.1 12.3 %collective-permute-start.2 = (bf16[96,768]{1,0:T(8,128)(2,1)}, bf16[96,768]{1,0:T(8,128)(2,1)S(1)}, u32[]{:S(2)}, u32[]{:S(2)}) collective-permute-start(bf16[96,768]{1,0:T(8,128)(2,1)} %param.14), channel_id=1, source_target_pairs={{0,2},{1,3},{2,0},{3,1},{4,6},{5,7},{6,4},{7,5},{8,10},{9,11},{10,... | collective-permute-start | bytes 442376 | tf_op jit(solution)/shard_map/ppermute | solution.py:28
  6.3 12.1 %collective-permute-start.3 = (bf16[96,768]{1,0:T(8,128)(2,1)}, bf16[96,768]{1,0:T(8,128)(2,1)S(1)}, u32[]{:S(2)}, u32[]{:S(2)}) collective-permute-start(bf16[96,768]{1,0:T(8,128)(2,1)} %param.14), channel_id=1, source_target_pairs={{0,1},{1,0},{2,3},{3,2},{4,5},{5,4},{6,7},{7,6},{8,9},{9,8},{10,11... | collective-permute-start | bytes 442376 | tf_op jit(solution)/shard_map/ppermute | solution.py:28
  19.3 14.3 %collective-permute-start.5 = (bf16[2,96,768]{2,1,0:T(8,128)(2,1)S(1)}, bf16[2,96,768]{2,1,0:T(8,128)(2,1)S(1)}, u32[]{:S(2)}, u32[]{:S(2)}) collective-permute-start(bf16[2,96,768]{2,1,0:T(8,128)(2,1)S(1)} %pad_maximum_fusion.2.refs_1_), channel_id=1, source_target_pairs={{0,1},{1,0},{2,3},{3,2},{4,5},{5,4},{6,7},{7,6},{8,9},{9,8},{10,11... | collective-permute-start | bytes 884744 | tf_op jit(solution)/shard_map/ppermute | solution.py:28
  19.9 13.4 %collective-permute-start.6 = (bf16[96,768]{1,0:T(8,128)(2,1)S(1)}, bf16[96,768]{1,0:T(8,128)(2,1)S(1)}, u32[]{:S(2)}, u32[]{:S(2)}) collective-permute-start(bf16[96,768]{1,0:T(8,128)(2,1)S(1)} %collective-permute-done.1), channel_id=1, source_target_pairs={{0,16},{8,24},{16,0},{24,8},{1,17},{9,25},{17,1},{25,9},{2,18},{10... | collective-permute-start | bytes 442376 | tf_op jit(solution)/shard_map/ppermute | solution.py:28
  21.3 13.8 %collective-permute-start.9 = (bf16[96,768]{1,0:T(8,128)(2,1)S(1)}, bf16[96,768]{1,0:T(8,128)(2,1)S(1)}, u32[]{:S(2)}, u32[]{:S(2)}) collective-permute-start(bf16[96,768]{1,0:T(8,128)(2,1)S(1)} %collective-permute-done.1), channel_id=1, source_target_pairs={{0,1},{1,0},{2,3},{3,2},{4,5},{5,4},{6,7},{7,6},{8,9},{9,8},{10,11... | collective-permute-start | bytes 442376 | tf_op jit(solution)/shard_map/ppermute | solution.py:28
  22.9 12.3 %collective-permute-start.10 = (bf16[96,768]{1,0:T(8,128)(2,1)S(1)}, bf16[96,768]{1,0:T(8,128)(2,1)S(1)}, u32[]{:S(2)}, u32[]{:S(2)}) collective-permute-start(bf16[96,768]{1,0:T(8,128)(2,1)S(1)} %collective-permute-done.4), channel_id=1, source_target_pairs={{0,1},{1,0},{2,3},{3,2},{4,5},{5,4},{6,7},{7,6},{8,9},{9,8},{10,11... | collective-permute-start | bytes 442376 | tf_op jit(solution)/shard_map/ppermute | solution.py:28
  27.8 29.9 %all-to-all-start.1 = ((bf16[8,48,768]{2,1,0:T(8,128)(2,1)}), bf16[8,48,768]{2,1,0:T(8,128)(2,1)S(1)}, u32[]{:S(2)}, u32[]{:S(2)}) async-start(bf16[8,48,768]{2,1,0:T(8,128)(2,1)} %bitcast.10), calls=%async_computation.1 | async-start | bytes 1179648 | tf_op jit(solution)/shard_map/all_to_all | solution.py:566
  33.3 11.6 %collective-permute-start.12 = (bf16[3,96,768]{2,1,0:T(8,128)(2,1)S(1)}, bf16[3,96,768]{2,1,0:T(8,128)(2,1)S(1)}, u32[]{:S(2)}, u32[]{:S(2)}) collective-permute-start(bf16[3,96,768]{2,1,0:T(8,128)(2,1)S(1)} %pad_maximum_fusion.1.refs_0_), channel_id=1, source_target_pairs={{0,8},{8,0},{16,24},{24,16},{1,9},{9,1},{17,25},{25,17},{2,10},{10... | collective-permute-start | bytes 1327112 | tf_op jit(solution)/shard_map/ppermute | solution.py:28
  57.7 22.7 %all-to-all-start = ((bf16[8,48,768]{2,1,0:T(8,128)(2,1)}), bf16[8,48,768]{2,1,0:T(8,128)(2,1)S(1)}, u32[]{:S(2)}, u32[]{:S(2)}) async-start(bf16[8,48,768]{2,1,0:T(8,128)(2,1)} %bitcast.51), calls=%async_computation | async-start | bytes 1179648 | tf_op jit(solution)/shard_map/all_to_all | solution.py:566
  64.2 16.2 %collective-permute-start.24 = (bf16[384,768]{1,0:T(8,128)(2,1)S(1)}, bf16[384,768]{1,0:T(8,128)(2,1)S(1)}, u32[]{:S(2)}, u32[]{:S(2)}) collective-permute-start(bf16[384,768]{1,0:T(8,128)(2,1)S(1)} %bitcast.36), channel_id=1, source_target_pairs={{0,16},{8,24},{16,0},{24,8},{1,17},{9,25},{17,1},{25,9},{2,18},{10... | collective-permute-start | bytes 1769480 | tf_op jit(solution)/shard_map/ppermute | solution.py:28
  65.2 16.7 %collective-permute-start.20 = (bf16[384,768]{1,0:T(8,128)(2,1)S(1)}, bf16[384,768]{1,0:T(8,128)(2,1)S(1)}, u32[]{:S(2)}, u32[]{:S(2)}) collective-permute-start(bf16[384,768]{1,0:T(8,128)(2,1)S(1)} %bitcast.37), channel_id=1, source_target_pairs={{0,8},{8,0},{16,24},{24,16},{1,9},{9,1},{17,25},{25,17},{2,10},{10... | collective-permute-start | bytes 1769480 | tf_op jit(solution)/shard_map/ppermute | solution.py:28
  80.5 15.8 %collective-permute-start.25 = (bf16[384,768]{1,0:T(8,128)(2,1)S(1)}, bf16[384,768]{1,0:T(8,128)(2,1)S(1)}, u32[]{:S(2)}, u32[]{:S(2)}) collective-permute-start(bf16[384,768]{1,0:T(8,128)(2,1)S(1)} %collective-permute-done.24.refs_2_.refs_6_), channel_id=1, source_target_pairs={{0,8},{8,0},{16,24},{24,16},{1,9},{9,1},{17,25},{25,17},{2,10},{10... | collective-permute-start | bytes 1769480 | tf_op jit(solution)/shard_map/ppermute | solution.py:28
  81.0 15.3 %collective-permute-start.21 = (bf16[384,768]{1,0:T(8,128)(2,1)S(1)}, bf16[384,768]{1,0:T(8,128)(2,1)S(1)}, u32[]{:S(2)}, u32[]{:S(2)}) collective-permute-start(bf16[384,768]{1,0:T(8,128)(2,1)S(1)} %bitcast.41), channel_id=1, source_target_pairs={{0,16},{8,24},{16,0},{24,8},{1,17},{9,25},{17,1},{25,9},{2,18},{10... | collective-permute-start | bytes 1769480 | tf_op jit(solution)/shard_map/ppermute | solution.py:28
  102.4 18.3 %collective-permute-start.22 = (bf16[384,768]{1,0:T(8,128)(2,1)S(1)}, bf16[384,768]{1,0:T(8,128)(2,1)S(1)}, u32[]{:S(2)}, u32[]{:S(2)}) collective-permute-start(bf16[384,768]{1,0:T(8,128)(2,1)S(1)} %get-tuple-element.111), channel_id=1, source_target_pairs={{0,8},{8,0},{16,24},{24,16},{1,9},{9,1},{17,25},{25,17},{2,10},{10... | collective-permute-start | bytes 1769480 | tf_op jit(solution)/shard_map/ppermute | solution.py:28
  104.4 16.2 %collective-permute-start.27 = (bf16[384,768]{1,0:T(8,128)(2,1)S(1)}, bf16[384,768]{1,0:T(8,128)(2,1)S(1)}, u32[]{:S(2)}, u32[]{:S(2)}) collective-permute-start(bf16[384,768]{1,0:T(8,128)(2,1)S(1)} %add_convert_fusion.3), channel_id=1, source_target_pairs={{0,16},{8,24},{16,0},{24,8},{1,17},{9,25},{17,1},{25,9},{2,18},{10... | collective-permute-start | bytes 1769480 | tf_op jit(solution)/shard_map/ppermute | solution.py:28
  106.5 19.7 %collective-permute-start.29 = (bf16[384,768]{1,0:T(8,128)(2,1)S(1)}, bf16[384,768]{1,0:T(8,128)(2,1)S(1)}, u32[]{:S(2)}, u32[]{:S(2)}) collective-permute-start(bf16[384,768]{1,0:T(8,128)(2,1)S(1)} %get-tuple-element.123), channel_id=1, source_target_pairs={{0,8},{8,0},{16,24},{24,16},{1,9},{9,1},{17,25},{25,17},{2,10},{10... | collective-permute-start | bytes 1769480 | tf_op jit(solution)/shard_map/ppermute | solution.py:28
  108.2 32.8 %collective-permute-start.28 = (bf16[384,768]{1,0:T(8,128)(2,1)}, bf16[384,768]{1,0:T(8,128)(2,1)}, u32[]{:S(2)}, u32[]{:S(2)}) collective-permute-start(bf16[384,768]{1,0:T(8,128)(2,1)} %get-tuple-element.120), channel_id=1, source_target_pairs={{0,8},{8,0},{16,24},{24,16},{1,9},{9,1},{17,25},{25,17},{2,10},{10... | collective-permute-start | bytes 1769480 | tf_op jit(solution)/shard_map/ppermute | solution.py:28
  108.7 49.7 %collective-permute-start.31 = (bf16[2,128,768]{2,1,0:T(8,128)(2,1)S(1)}, bf16[2,128,768]{2,1,0:T(8,128)(2,1)S(1)}, u32[]{:S(2)}, u32[]{:S(2)}) collective-permute-start(bf16[2,128,768]{2,1,0:T(8,128)(2,1)S(1)} %copy-done.13), channel_id=1, source_target_pairs={{0,16},{8,24},{16,0},{24,8},{1,17},{9,25},{17,1},{25,9},{2,18},{10... | collective-permute-start | bytes 1179656 | tf_op jit(solution)/shard_map/ppermute | solution.py:28
  121.7 21.4 %all-to-all-start.2 = ((bf16[8,48,768]{2,1,0:T(8,128)(2,1)}), bf16[8,48,768]{2,1,0:T(8,128)(2,1)}, u32[]{:S(2)}, u32[]{:S(2)}) async-start(bf16[8,48,768]{2,1,0:T(8,128)(2,1)} %bitcast.21), calls=%async_computation.2 | async-start | bytes 1179648 | tf_op jit(solution)/shard_map/all_to_all | solution.py:566
  126.4 14.6 %collective-permute-start.30 = (bf16[384,768]{1,0:T(8,128)(2,1)S(1)}, bf16[384,768]{1,0:T(8,128)(2,1)S(1)}, u32[]{:S(2)}, u32[]{:S(2)}) collective-permute-start(bf16[384,768]{1,0:T(8,128)(2,1)S(1)} %add_convert_fusion.1), channel_id=1, source_target_pairs={{0,16},{8,24},{16,0},{24,8},{1,17},{9,25},{17,1},{25,9},{2,18},{10... | collective-permute-start | bytes 1769480 | tf_op jit(solution)/shard_map/ppermute | solution.py:28
  143.0 26.3 %all-to-all-start.3 = ((bf16[8,48,768]{2,1,0:T(8,128)(2,1)}), bf16[8,48,768]{2,1,0:T(8,128)(2,1)S(1)}, u32[]{:S(2)}, u32[]{:S(2)}) async-start(bf16[8,48,768]{2,1,0:T(8,128)(2,1)} %bitcast.23), calls=%async_computation.3 | async-start | bytes 1179648 | tf_op jit(solution)/shard_map/all_to_all | solution.py:566
  173.7 13.8 %collective-permute-start.38 = (bf16[384,512]{1,0:T(8,128)(2,1)S(1)}, bf16[384,512]{1,0:T(8,128)(2,1)S(1)}, u32[]{:S(2)}, u32[]{:S(2)}) collective-permute-start(bf16[384,512]{1,0:T(8,128)(2,1)S(1)} %get-tuple-element.155), channel_id=1, source_target_pairs={{0,1},{1,0},{2,3},{3,2},{4,5},{5,4},{6,7},{7,6},{8,9},{9,8},{10,11... | collective-permute-start | bytes 1179656 | tf_op jit(solution)/shard_map/ppermute | solution.py:28
  (65 other events, 462.3 us)

commit v4 on v3

--- a/solution.py
+++ b/solution.py
@@ -376,7 +376,7 @@
         in_specs=[VMEM] * 12,
         out_specs=(VMEM,) * 2,
         compiler_params=LIMIT,
-        cost_estimate=cost(10),
+        cost_estimate=cost(16),
         name="experts_gradients",
     )(*rows, *d_rows, *hidden, *d_pre)
 

time: 201 us -> 201 us (level)
  no operation moved by 1% of the time
where the time goes in v4:
time: 201 us; the launch traced here: 200 us
  waiting for transfers between devices  70.4 us (35%)
  starting transfers between devices  59.7 us (30%)
  Pallas kernels  45.2 us (22%)
  local copies, waits for them, and re-layouts  12.2 us (6%)
  other arithmetic  9.01 us (4%)
  matrix products  2.58 us (1%)
    ppermute x46, waiting for transfers between devices, swap(): return lax.ppermute(value, axis, [(i, i ^ bits) for i in range(size)])  55.1 us
    ppermute x46, starting transfers between devices, swap(): return lax.ppermute(value, axis, [(i, i ^ bits) for i in range(size)])  38.6 us
    all_to_all x4, starting transfers between devices, exchange_plain(): lax.all_to_all(chunks, 'expert', split_axis=0, concat_axis=0, tiled=True)  21.2 us
    all_to_all x4, waiting for transfers between devices, exchange_plain(): lax.all_to_all(chunks, 'expert', split_axis=0, concat_axis=0, tiled=True)  15.3 us
    pallas_call x1, Pallas kernels, attention_backward(): pl.pallas_call(kernel, out_shape=(jax.ShapeDtypeStruct((count, width), bf...  10.6 us
    pallas_call x1, Pallas kernels, experts_gradients(): pl.pallas_call(kernel, out_shape=(jax.ShapeDtypeStruct((width, units), f3...  10.6 us
    pallas_call x1, Pallas kernels, attention_forward(): pl.pallas_call(kernel, out_shape=(jax.ShapeDtypeStruct((2, count, width),...  9.42 us
    unnamed x80, local copies, waits for them, and re-layouts  9.14 us
  transfers between devices with their start and end apart: 50, of which 17 were waited for; matrix products, arithmetic and copies ran while one was open for 8% of the time, Pallas kernels for 20%

profile of v4, /device:TPU:0, one launch (start us, length us, event | category | flops | bytes accessed | tf_op | source)
XLA Modules:
  0.0 200.4 jit_solution(10416541199375715665)
XLA Ops:
  0.7 4.1 %collective-permute-start = (bf16[96,768]{1,0:T(8,128)(2,1)}, bf16[96,768]{1,0:T(8,128)(2,1)S(1)}, u32[]{:S(2)}, u32[]{:S(2)}) collective-permute-start(bf16[96,768]{1,0:T(8,128)(2,1)} %param.14), channel_id=1, source_target_pairs={{0,4},{1,5},{2,6},{3,7},{4,0},{5,1},{6,2},{7,3},{8,12},{9,13},{10,... | collective-permute-start | bytes 442376 | tf_op jit(solution)/shard_map/ppermute | solution.py:28
  24.5 3.3 %collective-permute-done.7.refs_3_ = bf16[2,96,768]{2,1,0:T(8,128)(2,1)S(1)} collective-permute-done((bf16[2,96,768]{2,1,0:T(8,128)(2,1)S(1)}, bf16[2,96,768]{2,1,0:T(8,128)(2,1)S(1)}, u32[]{:S(2)}, u32[]{:S(2)}) %collective-permute-start.7) | collective-permute-done | bytes 294944 | tf_op jit(solution)/shard_map/ppermute | solution.py:28
  27.8 5.4 %all-to-all-start.1 = ((bf16[8,48,768]{2,1,0:T(8,128)(2,1)}), bf16[8,48,768]{2,1,0:T(8,128)(2,1)S(1)}, u32[]{:S(2)}, u32[]{:S(2)}) async-start(bf16[8,48,768]{2,1,0:T(8,128)(2,1)} %bitcast.10), calls=%async_computation.1 | async-start | bytes 1179648 | tf_op jit(solution)/shard_map/all_to_all | solution.py:566
  35.3 2.0 %collective-permute-start.11 = (bf16[96,768]{1,0:T(8,128)(2,1)S(1)}, bf16[96,768]{1,0:T(8,128)(2,1)S(1)}, u32[]{:S(2)}, u32[]{:S(2)}) collective-permute-start(bf16[96,768]{1,0:T(8,128)(2,1)S(1)} %collective-permute-done.6), channel_id=1, source_target_pairs={{0,1},{1,0},{2,3},{3,2},{4,5},{5,4},{6,7},{7,6},{8,9},{9,8},{10,11... | collective-permute-start | bytes 442376 | tf_op jit(solution)/shard_map/ppermute | solution.py:28
  37.4 7.0 %collective-permute-done.11 = bf16[96,768]{1,0:T(8,128)(2,1)S(1)} collective-permute-done((bf16[96,768]{1,0:T(8,128)(2,1)S(1)}, bf16[96,768]{1,0:T(8,128)(2,1)S(1)}, u32[]{:S(2)}, u32[]{:S(2)}) %collective-permute-start.11) | collective-permute-done | bytes 147488 | tf_op jit(solution)/shard_map/ppermute | solution.py:28
  48.2 9.4 %attention_forward.1 = (bf16[2,128,768]{2,1,0:T(8,128)(2,1)}, bf16[3,128,768]{2,1,0:T(8,128)(2,1)}, f32[12,128,128]{2,1,0:T(8,128)}, f32[128,768]{1,0:T(8,128)}, bf16[384,768]{1,0:T(8,128)(2,1)}) custom-call(bf16[3,96,768]{2,1,0:T(8,128)(2,1)} %copy-done.24, bf16[2,96,768]{2,1,0:T(8,128)(2,1)} %copy-done.25, bf16[2,96,768]{2,1,0:T(8,128)(2,1)} %copy-done.32, ...), custom_call_target="tpu_custom_call" | custom-call | flops 3000000000 | bytes 9000000 | tf_op jit(solution)/shard_map/attention_forward/pallas_call | solution.py:171
  57.7 6.5 %all-to-all-start = ((bf16[8,48,768]{2,1,0:T(8,128)(2,1)}), bf16[8,48,768]{2,1,0:T(8,128)(2,1)S(1)}, u32[]{:S(2)}, u32[]{:S(2)}) async-start(bf16[8,48,768]{2,1,0:T(8,128)(2,1)} %bitcast.51), calls=%async_computation | async-start | bytes 1179648 | tf_op jit(solution)/shard_map/all_to_all | solution.py:566
  65.2 15.2 %all-to-all-done = bf16[8,48,768]{2,1,0:T(8,128)(2,1)S(1)} async-done(((bf16[8,48,768]{2,1,0:T(8,128)(2,1)}), bf16[8,48,768]{2,1,0:T(8,128)(2,1)S(1)}, u32[]{:S(2)}, u32[]{:S(2)}) %all-to-all-start) | async-done | bytes 589856 | tf_op jit(solution)/shard_map/all_to_all | solution.py:566
  83.9 3.9 %experts_first.2 = (bf16[2,384,768]{2,1,0:T(8,128)(2,1)S(1)}, bf16[2,384,768]{2,1,0:T(8,128)(2,1)S(1)}, f32[384,768]{1,0:T(8,128)S(1)}, bf16[384,768]{1,0:T(8,128)(2,1)S(1)}) custom-call(bf16[384,768]{1,0:T(8,128)(2,1)S(1)} %bitcast.42, bf16[384,768]{1,0:T(8,128)(2,1)S(1)} %collective-permute-done.19.refs_1_, bf16[384,768]{1,0:T(8,128)(2,1)S(1)} %bitcast.38, ...), custom_call_target="tpu_custom_call" | custom-call | flops 6000000000 | bytes 18000000 | tf_op jit(solution)/shard_map/experts_first/pallas_call | solution.py:315
  89.5 6.8 %collective-permute-done.21.refs_0_.refs_2_ = bf16[384,768]{1,0:T(8,128)(2,1)S(1)} collective-permute-done((bf16[384,768]{1,0:T(8,128)(2,1)S(1)}, bf16[384,768]{1,0:T(8,128)(2,1)S(1)}, u32[]{:S(2)}, u32[]{:S(2)}) %collective-permute-start.21) | collective-permute-done | bytes 589856 | tf_op jit(solution)/shard_map/ppermute | solution.py:28
  98.3 3.9 %experts_first.3 = (bf16[2,384,768]{2,1,0:T(8,128)(2,1)S(1)}, bf16[2,384,768]{2,1,0:T(8,128)(2,1)S(1)}, f32[384,768]{1,0:T(8,128)S(1)}, bf16[384,768]{1,0:T(8,128)(2,1)S(1)}) custom-call(bf16[384,768]{1,0:T(8,128)(2,1)S(1)} %collective-permute-done.21.refs_0_.refs_2_, bf16[384,768]{1,0:T(8,128)(2,1)S(1)} %collective-permute-done.23.refs_1_.refs_3_, ...), custom_call_target="tpu_custom_call" | custom-call | flops 6000000000 | bytes 18000000 | tf_op jit(solution)/shard_map/experts_first/pallas_call | solution.py:315
  109.7 10.9 %collective-permute-done.27 = bf16[384,768]{1,0:T(8,128)(2,1)S(1)} collective-permute-done((bf16[384,768]{1,0:T(8,128)(2,1)S(1)}, bf16[384,768]{1,0:T(8,128)(2,1)S(1)}, u32[]{:S(2)}, u32[]{:S(2)}) %collective-permute-start.27) | collective-permute-done | bytes 589856 | tf_op jit(solution)/shard_map/ppermute | solution.py:28
  121.7 4.5 %all-to-all-start.2 = ((bf16[8,48,768]{2,1,0:T(8,128)(2,1)}), bf16[8,48,768]{2,1,0:T(8,128)(2,1)}, u32[]{:S(2)}, u32[]{:S(2)}) async-start(bf16[8,48,768]{2,1,0:T(8,128)(2,1)} %bitcast.21), calls=%async_computation.2 | async-start | bytes 1179648 | tf_op jit(solution)/shard_map/all_to_all | solution.py:566
  127.4 10.6 %experts_gradients.1 = (f32[768,768]{1,0:T(8,128)}, f32[768,768]{1,0:T(8,128)}) custom-call(bf16[384,768]{1,0:T(8,128)(2,1)} %bitcast.43, bf16[384,768]{1,0:T(8,128)(2,1)} %copy-done.9, bf16[384,768]{1,0:T(8,128)(2,1)} %copy-done.11, bf16[384,768]{1,0:T(8,128)(2,1)} %copy-done.12, bf16[384,768]{1,0:T(8,128)(2,1)} %bitcast.39, bf16[384,768]{1,0:T(8,128)(2,1)} %copy-done.8, ...), custom_call_target="tpu_custom_call" | custom-call | flops 16000000000 | bytes 48000000 | tf_op jit(solution)/shard_map/experts_gradients/pallas_call | solution.py:370
  138.0 3.0 %collective-permute-done.30 = bf16[384,768]{1,0:T(8,128)(2,1)S(1)} collective-permute-done((bf16[384,768]{1,0:T(8,128)(2,1)S(1)}, bf16[384,768]{1,0:T(8,128)(2,1)S(1)}, u32[]{:S(2)}, u32[]{:S(2)}) %collective-permute-start.30) | collective-permute-done | bytes 589856 | tf_op jit(solution)/shard_map/ppermute | solution.py:28
  140.9 2.1 %add_convert_fusion = bf16[384,768]{1,0:T(8,128)(2,1)} fusion(bf16[384,768]{1,0:T(8,128)(2,1)S(1)} %collective-permute-done.30, bf16[384,768]{1,0:T(8,128)(2,1)} %collective-permute-done.28, bf16[384,768]{1,0:T(8,128)(2,1)S(1)} %get-tuple-element.119), kind=kLoop, calls=%fused_computation.2 | loop fusion | flops 1769472 | bytes 2359296 | tf_op jit(solution)/shard_map/convert_element_type | solution.py:580
  143.0 4.7 %all-to-all-start.3 = ((bf16[8,48,768]{2,1,0:T(8,128)(2,1)}), bf16[8,48,768]{2,1,0:T(8,128)(2,1)S(1)}, u32[]{:S(2)}, u32[]{:S(2)}) async-start(bf16[8,48,768]{2,1,0:T(8,128)(2,1)} %bitcast.23), calls=%async_computation.3 | async-start | bytes 1179648 | tf_op jit(solution)/shard_map/all_to_all | solution.py:566
  147.7 10.6 %attention_backward.1 = (bf16[128,768]{1,0:T(8,128)(2,1)}, bf16[144,768]{1,0:T(8,128)(2,1)}, bf16[144,768]{1,0:T(8,128)(2,1)}, bf16[144,768]{1,0:T(8,128)(2,1)}, f32[128,768]{1,0:T(8,128)}, /*index=5*/f32[8,768]{1,0:T(8,128)}) custom-call(bf16[3,96,768]{2,1,0:T(8,128)(2,1)} %copy-done.24, bf16[2,96,768]{2,1,0:T(8,128)(2,1)} %copy-done.25, ...), custom_call_target="tpu_custom_call" | custom-call | flops 12999999488 | bytes 39000000 | tf_op jit(solution)/shard_map/attention_backward/pallas_call | solution.py:263
  161.0 5.6 %collective-permute-done.34 = bf16[144,768]{1,0:T(8,128)(2,1)S(1)} collective-permute-done((bf16[144,768]{1,0:T(8,128)(2,1)}, bf16[144,768]{1,0:T(8,128)(2,1)S(1)}, u32[]{:S(2)}, u32[]{:S(2)}) %collective-permute-start.34) | collective-permute-done | bytes 221216 | tf_op jit(solution)/shard_map/ppermute | solution.py:28
  166.5 2.8 %collective-permute-done.32.refs_5_ = bf16[144,768]{1,0:T(8,128)(2,1)S(1)} collective-permute-done((bf16[144,768]{1,0:T(8,128)(2,1)}, bf16[144,768]{1,0:T(8,128)(2,1)S(1)}, u32[]{:S(2)}, u32[]{:S(2)}) %collective-permute-start.32) | collective-permute-done | bytes 221216 | tf_op jit(solution)/shard_map/ppermute | solution.py:28
  173.7 2.0 %collective-permute-start.38 = (bf16[384,512]{1,0:T(8,128)(2,1)S(1)}, bf16[384,512]{1,0:T(8,128)(2,1)S(1)}, u32[]{:S(2)}, u32[]{:S(2)}) collective-permute-start(bf16[384,512]{1,0:T(8,128)(2,1)S(1)} %get-tuple-element.155), channel_id=1, source_target_pairs={{0,1},{1,0},{2,3},{3,2},{4,5},{5,4},{6,7},{7,6},{8,9},{9,8},{10,11... | collective-permute-start | bytes 1179656 | tf_op jit(solution)/shard_map/ppermute | solution.py:28
  177.2 2.4 %collective-permute-start.40 = (bf16[224,256]{1,0:T(8,128)(2,1)S(1)}, bf16[224,256]{1,0:T(8,128)(2,1)S(1)}, u32[]{:S(2)}, u32[]{:S(2)}) collective-permute-start(bf16[224,256]{1,0:T(8,128)(2,1)S(1)} %get-tuple-element.158), channel_id=1, source_target_pairs={{0,4},{1,5},{2,6},{3,7},{4,0},{5,1},{6,2},{7,3},{8,12},{9,13},{10,... | collective-permute-start | bytes 344072 | tf_op jit(solution)/shard_map/ppermute | solution.py:28
  181.2 6.3 %collective-permute-done.40.z_2 = bf16[224,256]{1,0:T(8,128)(2,1)S(1)} collective-permute-done((bf16[224,256]{1,0:T(8,128)(2,1)S(1)}, bf16[224,256]{1,0:T(8,128)(2,1)S(1)}, u32[]{:S(2)}, u32[]{:S(2)}) %collective-permute-start.40) | collective-permute-done | bytes 114720 | tf_op jit(solution)/shard_map/ppermute | solution.py:28
  193.9 2.3 %block_output.1 = bf16[128,768]{1,0:T(8,128)(2,1)} custom-call(bf16[384,768]{1,0:T(8,128)(2,1)} %bitcast.50, f32[128,768]{1,0:T(8,128)} %get-tuple-element.103.refs_17_.res, bf16[128,384]{1,0:T(8,128)(2,1)} %get-tuple-element.144.first, bf16[128,384]{1,0:T(8,128)(2,1)} %get-tuple-element.145.second, f32[128,2]{1,0:T(8,128)} %copy.36.gate), custom_call_target="tpu_custom_call" | custom-call | flops 3000000000 | bytes 9000000 | tf_op jit(solution)/shard_map/block_output/pallas_call | solution.py:390
  (193 shorter events, 63.8 us)
Async XLA Ops:
  0.7 17.8 %collective-permute-start = (bf16[96,768]{1,0:T(8,128)(2,1)}, bf16[96,768]{1,0:T(8,128)(2,1)S(1)}, u32[]{:S(2)}, u32[]{:S(2)}) collective-permute-start(bf16[96,768]{1,0:T(8,128)(2,1)} %param.14), channel_id=1, source_target_pairs={{0,4},{1,5},{2,6},{3,7},{4,0},{5,1},{6,2},{7,3},{8,12},{9,13},{10,... | collective-permute-start | bytes 442376 | tf_op jit(solution)/shard_map/ppermute | solution.py:28
  4.8 13.7 %collective-permute-start.1 = (bf16[96,768]{1,0:T(8,128)(2,1)}, bf16[96,768]{1,0:T(8,128)(2,1)S(1)}, u32[]{:S(2)}, u32[]{:S(2)}) collective-permute-start(bf16[96,768]{1,0:T(8,128)(2,1)} %param.14), channel_id=1, source_target_pairs={{0,6},{1,7},{2,4},{3,5},{4,2},{5,3},{6,0},{7,1},{8,14},{9,15},{10,... | collective-permute-start | bytes 442376 | tf_op jit(solution)/shard_map/ppermute | solution.py:28
  6.1 12.3 %collective-permute-start.2 = (bf16[96,768]{1,0:T(8,128)(2,1)}, bf16[96,768]{1,0:T(8,128)(2,1)S(1)}, u32[]{:S(2)}, u32[]{:S(2)}) collective-permute-start(bf16[96,768]{1,0:T(8,128)(2,1)} %param.14), channel_id=1, source_target_pairs={{0,2},{1,3},{2,0},{3,1},{4,6},{5,7},{6,4},{7,5},{8,10},{9,11},{10,... | collective-permute-start | bytes 442376 | tf_op jit(solution)/shard_map/ppermute | solution.py:28
  6.3 12.1 %collective-permute-start.3 = (bf16[96,768]{1,0:T(8,128)(2,1)}, bf16[96,768]{1,0:T(8,128)(2,1)S(1)}, u32[]{:S(2)}, u32[]{:S(2)}) collective-permute-start(bf16[96,768]{1,0:T(8,128)(2,1)} %param.14), channel_id=1, source_target_pairs={{0,1},{1,0},{2,3},{3,2},{4,5},{5,4},{6,7},{7,6},{8,9},{9,8},{10,11... | collective-permute-start | bytes 442376 | tf_op jit(solution)/shard_map/ppermute | solution.py:28
  19.3 14.3 %collective-permute-start.5 = (bf16[2,96,768]{2,1,0:T(8,128)(2,1)S(1)}, bf16[2,96,768]{2,1,0:T(8,128)(2,1)S(1)}, u32[]{:S(2)}, u32[]{:S(2)}) collective-permute-start(bf16[2,96,768]{2,1,0:T(8,128)(2,1)S(1)} %pad_maximum_fusion.2.refs_1_), channel_id=1, source_target_pairs={{0,1},{1,0},{2,3},{3,2},{4,5},{5,4},{6,7},{7,6},{8,9},{9,8},{10,11... | collective-permute-start | bytes 884744 | tf_op jit(solution)/shard_map/ppermute | solution.py:28
  19.9 13.4 %collective-permute-start.6 = (bf16[96,768]{1,0:T(8,128)(2,1)S(1)}, bf16[96,768]{1,0:T(8,128)(2,1)S(1)}, u32[]{:S(2)}, u32[]{:S(2)}) collective-permute-start(bf16[96,768]{1,0:T(8,128)(2,1)S(1)} %collective-permute-done.1), channel_id=1, source_target_pairs={{0,16},{8,24},{16,0},{24,8},{1,17},{9,25},{17,1},{25,9},{2,18},{10... | collective-permute-start | bytes 442376 | tf_op jit(solution)/shard_map/ppermute | solution.py:28
  21.3 13.8 %collective-permute-start.9 = (bf16[96,768]{1,0:T(8,128)(2,1)S(1)}, bf16[96,768]{1,0:T(8,128)(2,1)S(1)}, u32[]{:S(2)}, u32[]{:S(2)}) collective-permute-start(bf16[96,768]{1,0:T(8,128)(2,1)S(1)} %collective-permute-done.1), channel_id=1, source_target_pairs={{0,1},{1,0},{2,3},{3,2},{4,5},{5,4},{6,7},{7,6},{8,9},{9,8},{10,11... | collective-permute-start | bytes 442376 | tf_op jit(solution)/shard_map/ppermute | solution.py:28
  22.9 12.3 %collective-permute-start.10 = (bf16[96,768]{1,0:T(8,128)(2,1)S(1)}, bf16[96,768]{1,0:T(8,128)(2,1)S(1)}, u32[]{:S(2)}, u32[]{:S(2)}) collective-permute-start(bf16[96,768]{1,0:T(8,128)(2,1)S(1)} %collective-permute-done.4), channel_id=1, source_target_pairs={{0,1},{1,0},{2,3},{3,2},{4,5},{5,4},{6,7},{7,6},{8,9},{9,8},{10,11... | collective-permute-start | bytes 442376 | tf_op jit(solution)/shard_map/ppermute | solution.py:28
  27.8 29.9 %all-to-all-start.1 = ((bf16[8,48,768]{2,1,0:T(8,128)(2,1)}), bf16[8,48,768]{2,1,0:T(8,128)(2,1)S(1)}, u32[]{:S(2)}, u32[]{:S(2)}) async-start(bf16[8,48,768]{2,1,0:T(8,128)(2,1)} %bitcast.10), calls=%async_computation.1 | async-start | bytes 1179648 | tf_op jit(solution)/shard_map/all_to_all | solution.py:566
  33.3 11.6 %collective-permute-start.12 = (bf16[3,96,768]{2,1,0:T(8,128)(2,1)S(1)}, bf16[3,96,768]{2,1,0:T(8,128)(2,1)S(1)}, u32[]{:S(2)}, u32[]{:S(2)}) collective-permute-start(bf16[3,96,768]{2,1,0:T(8,128)(2,1)S(1)} %pad_maximum_fusion.1.refs_0_), channel_id=1, source_target_pairs={{0,8},{8,0},{16,24},{24,16},{1,9},{9,1},{17,25},{25,17},{2,10},{10... | collective-permute-start | bytes 1327112 | tf_op jit(solution)/shard_map/ppermute | solution.py:28
  57.7 22.7 %all-to-all-start = ((bf16[8,48,768]{2,1,0:T(8,128)(2,1)}), bf16[8,48,768]{2,1,0:T(8,128)(2,1)S(1)}, u32[]{:S(2)}, u32[]{:S(2)}) async-start(bf16[8,48,768]{2,1,0:T(8,128)(2,1)} %bitcast.51), calls=%async_computation | async-start | bytes 1179648 | tf_op jit(solution)/shard_map/all_to_all | solution.py:566
  64.2 16.2 %collective-permute-start.24 = (bf16[384,768]{1,0:T(8,128)(2,1)S(1)}, bf16[384,768]{1,0:T(8,128)(2,1)S(1)}, u32[]{:S(2)}, u32[]{:S(2)}) collective-permute-start(bf16[384,768]{1,0:T(8,128)(2,1)S(1)} %bitcast.36), channel_id=1, source_target_pairs={{0,16},{8,24},{16,0},{24,8},{1,17},{9,25},{17,1},{25,9},{2,18},{10... | collective-permute-start | bytes 1769480 | tf_op jit(solution)/shard_map/ppermute | solution.py:28
  65.2 16.7 %collective-permute-start.20 = (bf16[384,768]{1,0:T(8,128)(2,1)S(1)}, bf16[384,768]{1,0:T(8,128)(2,1)S(1)}, u32[]{:S(2)}, u32[]{:S(2)}) collective-permute-start(bf16[384,768]{1,0:T(8,128)(2,1)S(1)} %bitcast.37), channel_id=1, source_target_pairs={{0,8},{8,0},{16,24},{24,16},{1,9},{9,1},{17,25},{25,17},{2,10},{10... | collective-permute-start | bytes 1769480 | tf_op jit(solution)/shard_map/ppermute | solution.py:28
  80.5 15.8 %collective-permute-start.25 = (bf16[384,768]{1,0:T(8,128)(2,1)S(1)}, bf16[384,768]{1,0:T(8,128)(2,1)S(1)}, u32[]{:S(2)}, u32[]{:S(2)}) collective-permute-start(bf16[384,768]{1,0:T(8,128)(2,1)S(1)} %collective-permute-done.24.refs_2_.refs_6_), channel_id=1, source_target_pairs={{0,8},{8,0},{16,24},{24,16},{1,9},{9,1},{17,25},{25,17},{2,10},{10... | collective-permute-start | bytes 1769480 | tf_op jit(solution)/shard_map/ppermute | solution.py:28
  81.0 15.3 %collective-permute-start.21 = (bf16[384,768]{1,0:T(8,128)(2,1)S(1)}, bf16[384,768]{1,0:T(8,128)(2,1)S(1)}, u32[]{:S(2)}, u32[]{:S(2)}) collective-permute-start(bf16[384,768]{1,0:T(8,128)(2,1)S(1)} %bitcast.41), channel_id=1, source_target_pairs={{0,16},{8,24},{16,0},{24,8},{1,17},{9,25},{17,1},{25,9},{2,18},{10... | collective-permute-start | bytes 1769480 | tf_op jit(solution)/shard_map/ppermute | solution.py:28
  102.4 18.3 %collective-permute-start.22 = (bf16[384,768]{1,0:T(8,128)(2,1)S(1)}, bf16[384,768]{1,0:T(8,128)(2,1)S(1)}, u32[]{:S(2)}, u32[]{:S(2)}) collective-permute-start(bf16[384,768]{1,0:T(8,128)(2,1)S(1)} %get-tuple-element.111), channel_id=1, source_target_pairs={{0,8},{8,0},{16,24},{24,16},{1,9},{9,1},{17,25},{25,17},{2,10},{10... | collective-permute-start | bytes 1769480 | tf_op jit(solution)/shard_map/ppermute | solution.py:28
  104.4 16.2 %collective-permute-start.27 = (bf16[384,768]{1,0:T(8,128)(2,1)S(1)}, bf16[384,768]{1,0:T(8,128)(2,1)S(1)}, u32[]{:S(2)}, u32[]{:S(2)}) collective-permute-start(bf16[384,768]{1,0:T(8,128)(2,1)S(1)} %add_convert_fusion.3), channel_id=1, source_target_pairs={{0,16},{8,24},{16,0},{24,8},{1,17},{9,25},{17,1},{25,9},{2,18},{10... | collective-permute-start | bytes 1769480 | tf_op jit(solution)/shard_map/ppermute | solution.py:28
  106.5 19.7 %collective-permute-start.29 = (bf16[384,768]{1,0:T(8,128)(2,1)S(1)}, bf16[384,768]{1,0:T(8,128)(2,1)S(1)}, u32[]{:S(2)}, u32[]{:S(2)}) collective-permute-start(bf16[384,768]{1,0:T(8,128)(2,1)S(1)} %get-tuple-element.123), channel_id=1, source_target_pairs={{0,8},{8,0},{16,24},{24,16},{1,9},{9,1},{17,25},{25,17},{2,10},{10... | collective-permute-start | bytes 1769480 | tf_op jit(solution)/shard_map/ppermute | solution.py:28
  108.2 32.8 %collective-permute-start.28 = (bf16[384,768]{1,0:T(8,128)(2,1)}, bf16[384,768]{1,0:T(8,128)(2,1)}, u32[]{:S(2)}, u32[]{:S(2)}) collective-permute-start(bf16[384,768]{1,0:T(8,128)(2,1)} %get-tuple-element.120), channel_id=1, source_target_pairs={{0,8},{8,0},{16,24},{24,16},{1,9},{9,1},{17,25},{25,17},{2,10},{10... | collective-permute-start | bytes 1769480 | tf_op jit(solution)/shard_map/ppermute | solution.py:28
  108.7 49.7 %collective-permute-start.31 = (bf16[2,128,768]{2,1,0:T(8,128)(2,1)S(1)}, bf16[2,128,768]{2,1,0:T(8,128)(2,1)S(1)}, u32[]{:S(2)}, u32[]{:S(2)}) collective-permute-start(bf16[2,128,768]{2,1,0:T(8,128)(2,1)S(1)} %copy-done.13), channel_id=1, source_target_pairs={{0,16},{8,24},{16,0},{24,8},{1,17},{9,25},{17,1},{25,9},{2,18},{10... | collective-permute-start | bytes 1179656 | tf_op jit(solution)/shard_map/ppermute | solution.py:28
  121.7 21.4 %all-to-all-start.2 = ((bf16[8,48,768]{2,1,0:T(8,128)(2,1)}), bf16[8,48,768]{2,1,0:T(8,128)(2,1)}, u32[]{:S(2)}, u32[]{:S(2)}) async-start(bf16[8,48,768]{2,1,0:T(8,128)(2,1)} %bitcast.21), calls=%async_computation.2 | async-start | bytes 1179648 | tf_op jit(solution)/shard_map/all_to_all | solution.py:566
  126.4 14.6 %collective-permute-start.30 = (bf16[384,768]{1,0:T(8,128)(2,1)S(1)}, bf16[384,768]{1,0:T(8,128)(2,1)S(1)}, u32[]{:S(2)}, u32[]{:S(2)}) collective-permute-start(bf16[384,768]{1,0:T(8,128)(2,1)S(1)} %add_convert_fusion.1), channel_id=1, source_target_pairs={{0,16},{8,24},{16,0},{24,8},{1,17},{9,25},{17,1},{25,9},{2,18},{10... | collective-permute-start | bytes 1769480 | tf_op jit(solution)/shard_map/ppermute | solution.py:28
  143.0 26.3 %all-to-all-start.3 = ((bf16[8,48,768]{2,1,0:T(8,128)(2,1)}), bf16[8,48,768]{2,1,0:T(8,128)(2,1)S(1)}, u32[]{:S(2)}, u32[]{:S(2)}) async-start(bf16[8,48,768]{2,1,0:T(8,128)(2,1)} %bitcast.23), calls=%async_computation.3 | async-start | bytes 1179648 | tf_op jit(solution)/shard_map/all_to_all | solution.py:566
  173.7 13.8 %collective-permute-start.38 = (bf16[384,512]{1,0:T(8,128)(2,1)S(1)}, bf16[384,512]{1,0:T(8,128)(2,1)S(1)}, u32[]{:S(2)}, u32[]{:S(2)}) collective-permute-start(bf16[384,512]{1,0:T(8,128)(2,1)S(1)} %get-tuple-element.155), channel_id=1, source_target_pairs={{0,1},{1,0},{2,3},{3,2},{4,5},{5,4},{6,7},{7,6},{8,9},{9,8},{10,11... | collective-permute-start | bytes 1179656 | tf_op jit(solution)/shard_map/ppermute | solution.py:28
  (65 other events, 462.3 us)
